TPU v7x, 32 devices: a whole 2x2x4 slice. The times are simulated.
32 devices in a mesh: groups: 2 (over x), tm: 16 (over z, y, core).
Axes of the slice: x: 2, y: 2, z: 4, core: 2. Of those that a mesh axis runs over, the one named last changes fastest.
Arguments:
- generator: float32 [256, 256], replicated, may hold values from -0.09375 to 0.09375
- derivs: float32 [4096, 256], P(('groups', 'tm')), parts along dimension 0, may hold values from 0 to 1, as said below
- forcing: bfloat16 [4096, 256, 64], P(('groups', 'tm')), parts along dimension 0, may hold values from -6 to 6
- inputs: bfloat16 [4096, 256, 64], P(('groups', 'tm')), parts along dimension 0, may hold values from -6 to 6
- terminal: float32 [512, 64], P('groups'), parts along dimension 0, may hold values from -6 to 6
Outputs:
- adjoint: bfloat16 [4096, 256, 64], P(('groups', 'tm')), parts along dimension 0
- weight_grad: float32 [512, 256], P('groups'), parts along dimension 0
There are 2 independent parts, one for each index of `groups`. A program takes and returns all parts, laid end to end along the dimension named above; an argument that names none is the same for every part. Nothing has to cross between parts.
Inputs may be any that keep to these rules, and one draw needn't show every extreme that they name: `derivs`: every entry is positive and at most 1.
All inputs are finite; a program needn't handle non-finite values.
Results may differ from a plain program's by a relative error of at most 0.0029.
Values sent between devices are 32-bit elements; how exact they have to be, the bound alone decides.
No kernel may reach another device: no remote copies, remote signals or barrier semaphores. Data moves between devices by JAX's collectives and lax.ppermute only.
A program may use at most 128 MiB of HBM per device.

v0:
```python
import math

import jax
import jax.numpy as jnp
from jax import lax
from jax.experimental import pallas as pl
from jax.experimental.pallas import tpu as pltpu
from jax.sharding import PartitionSpec as P

F32 = jnp.float32
BF16 = jnp.bfloat16
VMEM_LIMIT = 56 * 1024 * 1024
CHUNKS = 4
SEG = 8


def mm(a, b):
    return jnp.dot(a, b, preferred_element_type=F32)


def full_mm(a, b):
    return jnp.dot(a, b, precision=lax.Precision.HIGHEST, preferred_element_type=F32)


def split(x):
    high = x.astype(BF16)
    low = (x - high.astype(F32)).astype(BF16)
    return high, low


def mm3(a, b_high, b_low):
    a_high, a_low = split(a)
    return mm(a_high, b_high) + mm(a_low, b_high) + mm(a_high, b_low)


def rotation(gen):
    n = gen.shape[0]
    skew = gen - gen.T
    ident = (
        lax.broadcasted_iota(jnp.int32, (n, n), 0) == lax.broadcasted_iota(jnp.int32, (n, n), 1)
    ).astype(F32)
    c = [1.0 / math.factorial(k) for k in range(13)]
    s2 = full_mm(skew, skew)
    s3 = full_mm(s2, skew)
    s4 = full_mm(s2, s2)
    top = c[8] * ident + c[9] * skew + c[10] * s2 + c[11] * s3 + c[12] * s4
    mid = c[4] * ident + c[5] * skew + c[6] * s2 + c[7] * s3
    bottom = ident + skew + c[2] * s2 + c[3] * s3
    return bottom + full_mm(s4, mid + full_mm(s4, top)), ident


def compose_into(later, high, low, vec, width):
    out = mm3(later, high, low)
    return jnp.concatenate([out[:width], out[width:] + vec], axis=0)


def build_kernel(gen_ref, d_ref, f_ref, map_ref, raw_ref, suffix_ref, rot_ref, state):
    steps, width = d_ref.shape
    per = steps // CHUNKS
    marks = per // SEG
    rot, ident = rotation(gen_ref[...])
    rot_high, rot_low = split(rot)
    rot_ref[0] = rot_high
    rot_ref[1] = rot_low
    for g in range(CHUNKS):
        state[g, :width] = ident
        state[g, width:] = jnp.zeros_like(state[g, width:])

    def step(s, _):
        for g in range(CHUNKS):
            t = g * per + per - 1 - s
            out = mm3(state[g] * d_ref[pl.ds(t, 1), :], rot_ref[0], rot_ref[1])
            state[g, :width] = out[:width]
            state[g, width:] = out[width:] + f_ref[t].astype(F32)
        return 0

    for k in range(marks):
        lax.fori_loop(k * SEG, (k + 1) * SEG, step, 0)
        for g in range(CHUNKS):
            raw_ref[g * marks + marks - 1 - k] = state[g]

    acc = state[CHUNKS - 1]
    for g in range(CHUNKS - 2, -1, -1):
        suffix_ref[g] = acc
        high, low = split(state[g, :width])
        acc = compose_into(acc, high, low, state[g, width:], width)
    map_ref[...] = acc


def marks_kernel(raw_ref, suffix_ref, in_ref, zh_ref, zl_ref, zu_ref, flip_ref):
    count, rows, width = raw_ref.shape
    cols = rows - width
    marks = count // CHUNKS
    for j in range(count):
        g = j // marks
        if g == CHUNKS - 1:
            full = raw_ref[j]
        else:
            high, low = split(raw_ref[j, :width])
            full = compose_into(suffix_ref[g], high, low, raw_ref[j, width:], width)
        high, low = split(full[:width])
        zh_ref[j] = high
        zl_ref[j] = low
        zu_ref[j] = full[width:]
    steps = in_ref.shape[0]
    segs = steps // SEG

    def flip(s, _):
        block = jnp.concatenate([in_ref[m * SEG + s] for m in range(segs)], axis=0)
        flip_ref[s] = block.T
        return 0

    lax.fori_loop(0, SEG, flip, 0)


def compose_kernel(first_ref, second_ref, out_ref):
    width = first_ref.shape[1]
    high, low = split(second_ref[:width])
    rows = first_ref.shape[0]
    out = mm3(first_ref[...], high, low)
    if rows > width:
        out_ref[:width] = out[:width]
        out_ref[width:] = out[width:] + second_ref[width:]
    else:
        out_ref[...] = out + second_ref[width:]


def sweep_kernel(v_ref, zh_ref, zl_ref, zu_ref, rot_ref, d_ref, f_ref, flip_ref, adj_ref, grad_ref, cur):
    count, width = zh_ref.shape[0], zh_ref.shape[1]
    cols = v_ref.shape[0]
    v = v_ref[...]
    v_high, v_low = split(v)
    lows = []
    for j in range(count):
        z = mm(v_high, zh_ref[j]) + mm(v_low, zh_ref[j]) + mm(v_high, zl_ref[j]) + zu_ref[j]
        if j > 0:
            cur[(j - 1) * cols : j * cols] = z
        low = z.astype(BF16)
        adj_ref[j * SEG] = low
        lows.append(low)
    cur[(count - 1) * cols :] = v
    grad = mm(flip_ref[0], jnp.concatenate(lows, axis=0))
    for s in range(SEG - 1):
        at = SEG - 1 - s
        scaled = jnp.concatenate(
            [cur[m * cols : (m + 1) * cols] * d_ref[m * SEG + at : m * SEG + at + 1, :] for m in range(count)],
            axis=0,
        )
        out = mm3(scaled, rot_ref[0], rot_ref[1])
        force = jnp.concatenate([f_ref[m * SEG + at] for m in range(count)], axis=0)
        out = out + force.astype(F32)
        cur[...] = out
        low = out.astype(BF16)
        for m in range(count):
            adj_ref[m * SEG + at] = low[m * cols : (m + 1) * cols]
        grad = grad + mm(flip_ref[at], low)
    grad_ref[...] = grad.T


def vmem(n):
    return [pl.BlockSpec(memory_space=pltpu.VMEM)] * n


def params():
    return pltpu.CompilerParams(vmem_limit_bytes=VMEM_LIMIT)


def shape(dims, kind=F32):
    return jax.ShapeDtypeStruct(dims, kind)


def build(gen, derivs, force):
    steps, width = derivs.shape
    cols = force.shape[1]
    rows = width + cols
    return pl.pallas_call(
        build_kernel,
        out_shape=(
            shape((rows, width)),
            shape((steps // SEG, rows, width)),
            shape((CHUNKS - 1, rows, width)),
            shape((2, width, width), BF16),
        ),
        in_specs=vmem(3),
        out_specs=tuple(vmem(4)),
        scratch_shapes=[pltpu.VMEM((CHUNKS, rows, width), F32)],
        compiler_params=params(),
        name="build",
    )(gen, derivs, force)


def mark_maps(raw, suffix, ins):
    count, rows, width = raw.shape
    steps, cols, feats = ins.shape
    return pl.pallas_call(
        marks_kernel,
        out_shape=(
            shape((count, width, width), BF16),
            shape((count, width, width), BF16),
            shape((count, rows - width, width)),
            shape((SEG, feats, steps // SEG * cols), BF16),
        ),
        in_specs=vmem(3),
        out_specs=tuple(vmem(4)),
        compiler_params=params(),
        cost_estimate=pl.CostEstimate(flops=6 * count * rows * width * width, bytes_accessed=20_000_000, transcendentals=0),
        name="marks",
    )(raw, suffix, ins)


def compose(first, second):
    rows, width = first.shape
    return pl.pallas_call(
        compose_kernel,
        out_shape=shape((rows, width)),
        in_specs=vmem(2),
        out_specs=vmem(1)[0],
        compiler_params=params(),
        name="compose",
    )(first, second)


def sweep(v, zh, zl, zu, rot, derivs, force, flipped):
    steps, cols, width = force.shape
    feats = flipped.shape[1]
    return pl.pallas_call(
        sweep_kernel,
        out_shape=(shape((steps, cols, width), BF16), shape((width, feats))),
        in_specs=vmem(8),
        out_specs=tuple(vmem(2)),
        scratch_shapes=[pltpu.VMEM((steps // SEG * cols, width), F32)],
        compiler_params=params(),
        name="sweep",
    )(v, zh, zl, zu, rot, derivs, force, flipped)


def swap(x, bit):
    n = lax.axis_size("tm")
    return lax.ppermute(x, "tm", [(i, i ^ bit) for i in range(n)])


def incoming(own, terminal):
    n = lax.axis_size("tm")
    place = lax.axis_index("tm")
    rows, width = own.shape
    ident = jnp.concatenate(
        [jnp.eye(width, dtype=F32), jnp.zeros((rows - width, width), F32)], axis=0
    )
    total, later = own, ident
    bit = 1
    while bit < n // 2:
        other = swap(total, bit)
        early = (place & bit) == 0
        later = jnp.where(early, compose(other, later), later)
        total = compose(jnp.where(early, other, total), jnp.where(early, total, other))
        bit *= 2
    if n > 1:
        top = swap(compose(terminal, total), bit)
        terminal = jnp.where((place & bit) == 0, top, terminal)
    return compose(terminal, later)


def all_sum(x):
    n = lax.axis_size("tm")
    place = lax.axis_index("tm")
    halves = []
    bit = 1
    while bit < n and len(halves) < 2:
        half = x.shape[0] // 2
        upper = (place & bit) != 0
        keep = jnp.where(upper, x[half:], x[:half])
        give = jnp.where(upper, x[:half], x[half:])
        x = keep + swap(give, bit)
        halves.append((bit, upper))
        bit *= 2
    while bit < n:
        x = x + swap(x, bit)
        bit *= 2
    for at, upper in reversed(halves):
        other = swap(x, at)
        x = jnp.where(upper, jnp.concatenate([other, x], 0), jnp.concatenate([x, other], 0))
    return x


def body(generator, derivs, forcing, inputs, terminal):
    force = jnp.transpose(forcing, (0, 2, 1))
    ins = jnp.transpose(inputs, (0, 2, 1))
    own, raw, suffix, rot = build(generator, derivs, force)
    zh, zl, zu, flipped = mark_maps(raw, suffix, ins)
    v = incoming(own, terminal.T)
    adj, grad = sweep(v, zh, zl, zu, rot, derivs, force, flipped)
    return jnp.transpose(adj, (0, 2, 1)), all_sum(grad)


def solution(mesh):
    in_specs = (
        P(),
        P(("groups", "tm"), None),
        P(("groups", "tm"), None, None),
        P(("groups", "tm"), None, None),
        P("groups", None),
    )
    out_specs = (P(("groups", "tm"), None, None), P("groups", None))
    return jax.shard_map(body, mesh=mesh, in_specs=in_specs, out_specs=out_specs, check_vma=False)
```

profile of v0, /device:TPU:0, one launch (start us, length us, event | category | flops | bytes accessed | tf_op | source)
XLA Modules:
  0.0 119.5 jit_solution(8244171344923366688)
XLA Ops:
  0.6 30.2 %build.1 = (f32[320,256]{1,0:T(8,128)}, f32[16,320,256]{2,1,0:T(8,128)}, f32[3,320,256]{2,1,0:T(8,128)}, bf16[2,256,256]{2,1,0:T(8,128)(2,1)}) custom-call(f32[256,256]{1,0:T(8,128)} %gen_ref.1, f32[128,256]{1,0:T(8,128)} %d_ref.3, bf16[128,64,256]{2,1,0:T(8,128)(2,1)} %bitcast.5), custom_call_target="tpu_custom_call" | custom-call | tf_op jit(solution)/shard_map/build/pallas_call | solution.py:176
  31.3 1.5 %collective-permute-done.first_ref = f32[320,256]{1,0:T(8,128)S(1)} collective-permute-done((f32[320,256]{1,0:T(8,128)}, f32[320,256]{1,0:T(8,128)S(1)}, u32[]{:S(2)}, u32[]{:S(2)}) %collective-permute-start) | collective-permute-done | bytes 327712 | tf_op jit(solution)/shard_map/ppermute | solution.py:239
  32.8 2.0 %broadcast_select_fusion.1 = (f32[320,256]{1,0:T(8,128)}, f32[320,256]{1,0:T(8,128)}) fusion(f32[320,256]{1,0:T(8,128)} %get-tuple-element.12, f32[320,256]{1,0:T(8,128)S(1)} %collective-permute-done.first_ref, pred[]{:T(512)S(6)} %eq.18), kind=kLoop, calls=%fused_computation.4 | loop fusion | flops 163840 | bytes 1310721 | tf_op jit(solution)/shard_map/jit(_where)/select_n | solution.py:255
  34.7 2.1 %compose.8 = f32[320,256]{1,0:T(8,128)} custom-call(f32[320,256]{1,0:T(8,128)} %get-tuple-element.27.first_ref, f32[320,256]{1,0:T(8,128)} %get-tuple-element.26.second_ref), custom_call_target="tpu_custom_call" | custom-call | tf_op jit(solution)/shard_map/compose/pallas_call | solution.py:213
  36.9 2.9 %collective-permute-start.1 = (f32[320,256]{1,0:T(8,128)}, f32[320,256]{1,0:T(8,128)S(1)}, u32[]{:S(2)}, u32[]{:S(2)}) collective-permute-start(f32[320,256]{1,0:T(8,128)} %compose.8), channel_id=1, source_target_pairs={{0,2},{1,3},{2,0},{3,1},{4,6},{5,7},{6,4},{7,5},{8,10},{9,11},{10,... | collective-permute-start | bytes 983048 | tf_op jit(solution)/shard_map/ppermute | solution.py:239
  40.6 11.0 %marks.1 = (bf16[16,256,256]{2,1,0:T(8,128)(2,1)}, bf16[16,256,256]{2,1,0:T(8,128)(2,1)}, f32[16,64,256]{2,1,0:T(8,128)}, bf16[8,256,1024]{2,1,0:T(8,128)(2,1)}) custom-call(f32[16,320,256]{2,1,0:T(8,128)} %get-tuple-element.13.raw_ref, f32[3,320,256]{2,1,0:T(8,128)} %get-tuple-element.14.suffix_ref, bf16[128,64,256]{2,1,0:T(8,128)(2,1)} %bitcast.7), custom_call_target="tpu_custom_call" | custom-call | flops 2013265920 | bytes 20000000 | tf_op jit(solution)/shard_map/marks/pallas_call | solution.py:195
  51.6 2.1 %compose.12 = f32[320,256]{1,0:T(8,128)} custom-call(f32[320,256]{1,0:T(8,128)} %copy-done, f32[320,256]{1,0:T(8,128)} %pad_convert_fusion.second_ref), custom_call_target="tpu_custom_call" | custom-call | tf_op jit(solution)/shard_map/compose/pallas_call | solution.py:213
  53.7 1.0 broadcast_select_fusion.4
  54.6 2.1 %compose.9 = f32[320,256]{1,0:T(8,128)} custom-call(f32[320,256]{1,0:T(8,128)} %get-tuple-element.25.first_ref, f32[320,256]{1,0:T(8,128)} %get-tuple-element.24.second_ref), custom_call_target="tpu_custom_call" | custom-call | tf_op jit(solution)/shard_map/compose/pallas_call | solution.py:213
  56.8 1.6 %collective-permute-start.2 = (f32[320,256]{1,0:T(8,128)}, f32[320,256]{1,0:T(8,128)S(1)}, u32[]{:S(2)}, u32[]{:S(2)}) collective-permute-start(f32[320,256]{1,0:T(8,128)} %compose.9), channel_id=1, source_target_pairs={{0,4},{1,5},{2,6},{3,7},{4,0},{5,1},{6,2},{7,3},{8,12},{9,13},{10,... | collective-permute-start | bytes 983048 | tf_op jit(solution)/shard_map/ppermute | solution.py:239
  58.4 1.7 %broadcast_select_fusion.second_ref = f32[320,256]{1,0:T(8,128)} fusion(f32[320,256]{1,0:T(8,128)} %compose.12, pred[]{:T(512)S(6)} %eq.18, pred[256,256]{1,0:T(8,128)(4,1)S(1)} %iota_compare_fusion), kind=kLoop, calls=%fused_computation.3 | loop fusion | flops 163840 | bytes 720897 | tf_op jit(solution)/shard_map/jit(_where)/select_n | solution.py:254
  60.1 2.1 %compose.13 = f32[320,256]{1,0:T(8,128)} custom-call(f32[320,256]{1,0:T(8,128)} %copy-done.1, f32[320,256]{1,0:T(8,128)} %broadcast_select_fusion.second_ref), custom_call_target="tpu_custom_call" | custom-call | tf_op jit(solution)/shard_map/compose/pallas_call | solution.py:213
  62.2 1.8 %broadcast_select_fusion.3.second_ref = f32[320,256]{1,0:T(8,128)} fusion(f32[320,256]{1,0:T(8,128)} %compose.13, f32[320,256]{1,0:T(8,128)} %broadcast_select_fusion.second_ref, pred[]{:T(512)S(6)} %eq.17), kind=kLoop, calls=%fused_computation.6 | loop fusion | flops 81920 | bytes 983041 | tf_op jit(solution)/shard_map/jit(_where)/select_n | solution.py:254
  64.0 2.5 %collective-permute-done.2.first_ref = f32[320,256]{1,0:T(8,128)S(1)} collective-permute-done((f32[320,256]{1,0:T(8,128)}, f32[320,256]{1,0:T(8,128)S(1)}, u32[]{:S(2)}, u32[]{:S(2)}) %collective-permute-start.2) | collective-permute-done | bytes 327712 | tf_op jit(solution)/shard_map/ppermute | solution.py:239
  66.5 2.0 %broadcast_select_fusion.7 = (f32[320,256]{1,0:T(8,128)}, f32[320,256]{1,0:T(8,128)}) fusion(f32[320,256]{1,0:T(8,128)} %compose.9, f32[320,256]{1,0:T(8,128)S(1)} %collective-permute-done.2.first_ref, pred[]{:T(512)S(6)} %eq.16), kind=kLoop, calls=%fused_computation.10 | loop fusion | flops 163840 | bytes 1310721 | tf_op jit(solution)/shard_map/jit(_where)/select_n | solution.py:255
  68.5 2.1 %compose.10.second_ref = f32[320,256]{1,0:T(8,128)} custom-call(f32[320,256]{1,0:T(8,128)} %get-tuple-element.23.first_ref, f32[320,256]{1,0:T(8,128)} %get-tuple-element.22.second_ref), custom_call_target="tpu_custom_call" | custom-call | tf_op jit(solution)/shard_map/compose/pallas_call | solution.py:213
  70.6 1.8 %compose.11 = f32[64,256]{1,0:T(8,128)} custom-call(f32[64,256]{1,0:T(8,128)} %bitcast.8, f32[320,256]{1,0:T(8,128)} %compose.10.second_ref), custom_call_target="tpu_custom_call" | custom-call | tf_op jit(solution)/shard_map/compose/pallas_call | solution.py:213
  72.4 2.6 %collective-permute-start.3 = (f32[64,256]{1,0:T(8,128)}, f32[64,256]{1,0:T(8,128)S(1)}, u32[]{:S(2)}, u32[]{:S(2)}) collective-permute-start(f32[64,256]{1,0:T(8,128)} %compose.11), channel_id=1, source_target_pairs={{0,8},{1,9},{2,10},{3,11},{4,12},{5,13},{6,14},{7,15},{8,0},{9,1},... | collective-permute-start | bytes 196616 | tf_op jit(solution)/shard_map/ppermute | solution.py:239
  75.0 2.1 %compose.14 = f32[320,256]{1,0:T(8,128)} custom-call(f32[320,256]{1,0:T(8,128)} %copy-done.3, f32[320,256]{1,0:T(8,128)} %broadcast_select_fusion.3.second_ref), custom_call_target="tpu_custom_call" | custom-call | tf_op jit(solution)/shard_map/compose/pallas_call | solution.py:213
  77.1 1.7 %broadcast_select_fusion.6.second_ref = f32[320,256]{1,0:T(8,128)} fusion(f32[320,256]{1,0:T(8,128)} %compose.14, f32[320,256]{1,0:T(8,128)} %broadcast_select_fusion.3.second_ref, pred[]{:T(512)S(6)} %eq.16), kind=kLoop, calls=%fused_computation.9 | loop fusion | flops 81920 | bytes 983041 | tf_op jit(solution)/shard_map/jit(_where)/select_n | solution.py:254
  79.4 1.8 %compose.15.v_ref = f32[64,256]{1,0:T(8,128)} custom-call(f32[64,256]{1,0:T(8,128)} %broadcast_select_fusion.9.first_ref, f32[320,256]{1,0:T(8,128)} %broadcast_select_fusion.6.second_ref), custom_call_target="tpu_custom_call" | custom-call | tf_op jit(solution)/shard_map/compose/pallas_call | solution.py:213
  81.3 14.4 %sweep.1 = (bf16[128,64,256]{2,1,0:T(8,128)(2,1)}, f32[256,256]{1,0:T(8,128)}) custom-call(f32[64,256]{1,0:T(8,128)} %compose.15.v_ref, bf16[16,256,256]{2,1,0:T(8,128)(2,1)} %get-tuple-element.15.zh_ref, bf16[16,256,256]{2,1,0:T(8,128)(2,1)} %get-tuple-element.16.zl_ref, f32[16,64,256]{2,1,0:T(8,128)} %get-tuple-element.17.zu_ref, ...), custom_call_target="tpu_custom_call" | custom-call | tf_op jit(solution)/shard_map/sweep/pallas_call | solution.py:226
  95.7 1.0 slice_select_fusion
  96.7 1.3 %collective-permute-done.4 = f32[128,256]{1,0:T(8,128)S(1)} collective-permute-done((f32[128,256]{1,0:T(8,128)S(1)}, f32[128,256]{1,0:T(8,128)S(1)}, u32[]{:S(2)}, u32[]{:S(2)}) %collective-permute-start.4) | collective-permute-done | bytes 131104 | tf_op jit(solution)/shard_map/ppermute | solution.py:239
  98.1 1.0 select_add_fusion
  99.7 3.8 %collective-permute-done.5 = f32[64,256]{1,0:T(8,128)S(1)} collective-permute-done((f32[64,256]{1,0:T(8,128)S(1)}, f32[64,256]{1,0:T(8,128)S(1)}, u32[]{:S(2)}, u32[]{:S(2)}) %collective-permute-start.5) | collective-permute-done | bytes 65568 | tf_op jit(solution)/shard_map/ppermute | solution.py:239
  103.4 1.6 %collective-permute-start.6 = (f32[64,256]{1,0:T(8,128)S(1)}, f32[64,256]{1,0:T(8,128)S(1)}, u32[]{:S(2)}, u32[]{:S(2)}) collective-permute-start(f32[64,256]{1,0:T(8,128)S(1)} %select_add_fusion.1), channel_id=1, source_target_pairs={{0,4},{1,5},{2,6},{3,7},{4,0},{5,1},{6,2},{7,3},{8,12},{9,13},{10,... | collective-permute-start | bytes 196616 | tf_op jit(solution)/shard_map/ppermute | solution.py:239
  105.1 2.7 %collective-permute-done.6 = f32[64,256]{1,0:T(8,128)S(1)} collective-permute-done((f32[64,256]{1,0:T(8,128)S(1)}, f32[64,256]{1,0:T(8,128)S(1)}, u32[]{:S(2)}, u32[]{:S(2)}) %collective-permute-start.6) | collective-permute-done | bytes 65568 | tf_op jit(solution)/shard_map/ppermute | solution.py:239
  107.8 1.7 %collective-permute-start.7 = (f32[64,256]{1,0:T(8,128)S(1)}, f32[64,256]{1,0:T(8,128)S(1)}, u32[]{:S(2)}, u32[]{:S(2)}) collective-permute-start(f32[64,256]{1,0:T(8,128)S(1)} %add.14), channel_id=1, source_target_pairs={{0,8},{1,9},{2,10},{3,11},{4,12},{5,13},{6,14},{7,15},{8,0},{9,1},... | collective-permute-start | bytes 196616 | tf_op jit(solution)/shard_map/ppermute | solution.py:239
  109.5 3.5 %collective-permute-done.7 = f32[64,256]{1,0:T(8,128)S(1)} collective-permute-done((f32[64,256]{1,0:T(8,128)S(1)}, f32[64,256]{1,0:T(8,128)S(1)}, u32[]{:S(2)}, u32[]{:S(2)}) %collective-permute-start.7) | collective-permute-done | bytes 65568 | tf_op jit(solution)/shard_map/ppermute | solution.py:239
  113.6 3.8 %collective-permute-done.8 = f32[64,256]{1,0:T(8,128)S(1)} collective-permute-done((f32[64,256]{1,0:T(8,128)S(1)}, f32[64,256]{1,0:T(8,128)S(1)}, u32[]{:S(2)}, u32[]{:S(2)}) %collective-permute-start.8) | collective-permute-done | bytes 65568 | tf_op jit(solution)/shard_map/ppermute | solution.py:239
  117.4 1.3 %collective-permute-done.9 = f32[128,256]{1,0:T(8,128)S(1)} collective-permute-done((f32[128,256]{1,0:T(8,128)S(1)}, f32[128,256]{1,0:T(8,128)S(1)}, u32[]{:S(2)}, u32[]{:S(2)}) %collective-permute-start.9) | collective-permute-done | bytes 131104 | tf_op jit(solution)/shard_map/ppermute | solution.py:239
  (26 shorter events, 3.9 us)
Async XLA Ops:
  30.8 1.9 %collective-permute-start = (f32[320,256]{1,0:T(8,128)}, f32[320,256]{1,0:T(8,128)S(1)}, u32[]{:S(2)}, u32[]{:S(2)}) collective-permute-start(f32[320,256]{1,0:T(8,128)} %get-tuple-element.12), channel_id=1, source_target_pairs={{0,1},{1,0},{2,3},{3,2},{4,5},{5,4},{6,7},{7,6},{8,9},{9,8},{10,11... | collective-permute-start | bytes 983048 | tf_op jit(solution)/shard_map/ppermute | solution.py:239
  32.8 18.8 %copy-start = (f32[320,256]{1,0:T(8,128)}, f32[320,256]{1,0:T(8,128)S(1)}, u32[]{:S(2)}) copy-start(f32[320,256]{1,0:T(8,128)S(1)} %collective-permute-done.first_ref) | copy-start | bytes 983044
  36.9 16.8 %collective-permute-start.1 = (f32[320,256]{1,0:T(8,128)}, f32[320,256]{1,0:T(8,128)S(1)}, u32[]{:S(2)}, u32[]{:S(2)}) collective-permute-start(f32[320,256]{1,0:T(8,128)} %compose.8), channel_id=1, source_target_pairs={{0,2},{1,3},{2,0},{3,1},{4,6},{5,7},{6,4},{7,5},{8,10},{9,11},{10,... | collective-permute-start | bytes 983048 | tf_op jit(solution)/shard_map/ppermute | solution.py:239
  40.6 13.1 %copy-start.2 = (f32[320,256]{1,0:T(8,128)S(1)}, f32[320,256]{1,0:T(8,128)}, u32[]{:S(2)}) copy-start(f32[320,256]{1,0:T(8,128)} %compose.8) | copy-start | bytes 983044
  53.7 6.4 %copy-start.1 = (f32[320,256]{1,0:T(8,128)}, f32[320,256]{1,0:T(8,128)S(1)}, u32[]{:S(2)}) copy-start(f32[320,256]{1,0:T(8,128)S(1)} %collective-permute-done.1.first_ref) | copy-start | bytes 983044
  54.6 24.2 %copy-start.4 = (f32[256,64]{0,1:T(8,128)S(1)}, f32[256,64]{0,1:T(8,128)}, u32[]{:S(2)}) copy-start(f32[256,64]{0,1:T(8,128)} %param.9) | copy-start | bytes 196612
  56.8 9.7 %collective-permute-start.2 = (f32[320,256]{1,0:T(8,128)}, f32[320,256]{1,0:T(8,128)S(1)}, u32[]{:S(2)}, u32[]{:S(2)}) collective-permute-start(f32[320,256]{1,0:T(8,128)} %compose.9), channel_id=1, source_target_pairs={{0,4},{1,5},{2,6},{3,7},{4,0},{5,1},{6,2},{7,3},{8,12},{9,13},{10,... | collective-permute-start | bytes 983048 | tf_op jit(solution)/shard_map/ppermute | solution.py:239
  66.5 8.5 %copy-start.3 = (f32[320,256]{1,0:T(8,128)}, f32[320,256]{1,0:T(8,128)S(1)}, u32[]{:S(2)}) copy-start(f32[320,256]{1,0:T(8,128)S(1)} %collective-permute-done.2.first_ref) | copy-start | bytes 983044
  72.4 6.4 %collective-permute-start.3 = (f32[64,256]{1,0:T(8,128)}, f32[64,256]{1,0:T(8,128)S(1)}, u32[]{:S(2)}, u32[]{:S(2)}) collective-permute-start(f32[64,256]{1,0:T(8,128)} %compose.11), channel_id=1, source_target_pairs={{0,8},{1,9},{2,10},{3,11},{4,12},{5,13},{6,14},{7,15},{8,0},{9,1},... | collective-permute-start | bytes 196616 | tf_op jit(solution)/shard_map/ppermute | solution.py:239
  96.7 1.4 %collective-permute-start.4 = (f32[128,256]{1,0:T(8,128)S(1)}, f32[128,256]{1,0:T(8,128)S(1)}, u32[]{:S(2)}, u32[]{:S(2)}) collective-permute-start(f32[128,256]{1,0:T(8,128)S(1)} %slice_select_fusion), channel_id=1, source_target_pairs={{0,1},{1,0},{2,3},{3,2},{4,5},{5,4},{6,7},{7,6},{8,9},{9,8},{10,11... | collective-permute-start | bytes 393224 | tf_op jit(solution)/shard_map/ppermute | solution.py:239
  99.1 4.3 %collective-permute-start.5 = (f32[64,256]{1,0:T(8,128)S(1)}, f32[64,256]{1,0:T(8,128)S(1)}, u32[]{:S(2)}, u32[]{:S(2)}) collective-permute-start(f32[64,256]{1,0:T(8,128)S(1)} %slice_select_fusion.1), channel_id=1, source_target_pairs={{0,2},{1,3},{2,0},{3,1},{4,6},{5,7},{6,4},{7,5},{8,10},{9,11},{10,... | collective-permute-start | bytes 196616 | tf_op jit(solution)/shard_map/ppermute | solution.py:239
  103.4 4.3 %collective-permute-start.6 = (f32[64,256]{1,0:T(8,128)S(1)}, f32[64,256]{1,0:T(8,128)S(1)}, u32[]{:S(2)}, u32[]{:S(2)}) collective-permute-start(f32[64,256]{1,0:T(8,128)S(1)} %select_add_fusion.1), channel_id=1, source_target_pairs={{0,4},{1,5},{2,6},{3,7},{4,0},{5,1},{6,2},{7,3},{8,12},{9,13},{10,... | collective-permute-start | bytes 196616 | tf_op jit(solution)/shard_map/ppermute | solution.py:239
  107.8 5.2 %collective-permute-start.7 = (f32[64,256]{1,0:T(8,128)S(1)}, f32[64,256]{1,0:T(8,128)S(1)}, u32[]{:S(2)}, u32[]{:S(2)}) collective-permute-start(f32[64,256]{1,0:T(8,128)S(1)} %add.14), channel_id=1, source_target_pairs={{0,8},{1,9},{2,10},{3,11},{4,12},{5,13},{6,14},{7,15},{8,0},{9,1},... | collective-permute-start | bytes 196616 | tf_op jit(solution)/shard_map/ppermute | solution.py:239
  113.0 4.3 %collective-permute-start.8 = (f32[64,256]{1,0:T(8,128)S(1)}, f32[64,256]{1,0:T(8,128)S(1)}, u32[]{:S(2)}, u32[]{:S(2)}) collective-permute-start(f32[64,256]{1,0:T(8,128)S(1)} %add.15), channel_id=1, source_target_pairs={{0,2},{1,3},{2,0},{3,1},{4,6},{5,7},{6,4},{7,5},{8,10},{9,11},{10,... | collective-permute-start | bytes 196616 | tf_op jit(solution)/shard_map/ppermute | solution.py:239
  117.4 1.4 %collective-permute-start.9 = (f32[128,256]{1,0:T(8,128)S(1)}, f32[128,256]{1,0:T(8,128)S(1)}, u32[]{:S(2)}, u32[]{:S(2)}) collective-permute-start(f32[128,256]{1,0:T(8,128)S(1)} %maximum_select_fusion.1), channel_id=1, source_target_pairs={{0,1},{1,0},{2,3},{3,2},{4,5},{5,4},{6,7},{7,6},{8,9},{9,8},{10,11... | collective-permute-start | bytes 393224 | tf_op jit(solution)/shard_map/ppermute | solution.py:239
where the time goes:
time: 120 us
  Pallas kernels  71.9 us (60%)
  waiting for transfers between devices  20.3 us (17%)
  other arithmetic  14.3 us (12%)
  starting transfers between devices  12.2 us (10%)
    pallas_call x1, Pallas kernels, build(): pl.pallas_call(build_kernel, out_shape=(shape((rows, width)), shape((step...  30.2 us
    ppermute x10, waiting for transfers between devices, swap(): return lax.ppermute(x, 'tm', [(i, i ^ bit) for i in range(n)])  20.3 us
    pallas_call x8, Pallas kernels, compose(): pl.pallas_call(compose_kernel, out_shape=shape((rows, width)), in_specs=v...  16.3 us
    pallas_call x1, Pallas kernels, sweep(): pl.pallas_call(sweep_kernel, out_shape=(shape((steps, cols, width), BF16)...  14.4 us
    ppermute x10, starting transfers between devices, swap(): return lax.ppermute(x, 'tm', [(i, i ^ bit) for i in range(n)])  12.2 us
    pallas_call x1, Pallas kernels, mark_maps(): pl.pallas_call(marks_kernel, out_shape=(shape((count, width, width), BF16...  11 us
    select_n x3, other arithmetic, incoming(): later = jnp.where(early, compose(other, later), later)  5.23 us
    select_n x3, other arithmetic, incoming(): jnp.where(early, total, other)  4.92 us
  transfers between devices with their start and end apart: 10, of which 8 were waited for; matrix products, arithmetic and copies ran while one was open for 5% of the time, Pallas kernels for 15%

commit v1 on v0

v1 whole, which is shorter than its diff:
```python
import functools
import math

import jax
import jax.numpy as jnp
from jax import lax
from jax.experimental import pallas as pl
from jax.experimental.pallas import tpu as pltpu
from jax.sharding import PartitionSpec as P

F32 = jnp.float32
BF16 = jnp.bfloat16
VMEM_LIMIT = 24 * 1024 * 1024
CHUNKS = 4
SEG = 8


def mm(a, b):
    return jnp.dot(a, b, preferred_element_type=F32)


def full_mm(a, b):
    return jnp.dot(a, b, precision=lax.Precision.HIGHEST, preferred_element_type=F32)


def split(x):
    high = x.astype(BF16)
    low = (x - high.astype(F32)).astype(BF16)
    return high, low


def mm3(a, b_high, b_low):
    a_high, a_low = split(a)
    return mm(a_high, b_high) + mm(a_low, b_high) + mm(a_high, b_low)


def rotation(gen):
    n = gen.shape[0]
    skew = gen - gen.T
    ident = (
        lax.broadcasted_iota(jnp.int32, (n, n), 0) == lax.broadcasted_iota(jnp.int32, (n, n), 1)
    ).astype(F32)
    c = [1.0 / math.factorial(k) for k in range(13)]
    s2 = full_mm(skew, skew)
    s3 = full_mm(s2, skew)
    s4 = full_mm(s2, s2)
    top = c[8] * ident + c[9] * skew + c[10] * s2 + c[11] * s3 + c[12] * s4
    mid = c[4] * ident + c[5] * skew + c[6] * s2 + c[7] * s3
    bottom = ident + skew + c[2] * s2 + c[3] * s3
    return bottom + full_mm(s4, mid + full_mm(s4, top)), ident


def compose(rows_in, through, width):
    high, low = split(through[:width])
    out = mm3(rows_in, high, low)
    return jnp.concatenate([out[:width], out[width:] + through[width:]], axis=0)


def apply(vec, through, width):
    high, low = split(through[:width])
    return mm3(vec, high, low) + through[width:]


def build_kernel(gen_ref, d_ref, f_hbm, map_ref, raw_ref, suffix_ref, rot_ref, f_ref, sem):
    steps, width = d_ref.shape
    per = steps // CHUNKS
    marks = per // SEG
    fetch = pltpu.make_async_copy(f_hbm, f_ref, sem)
    fetch.start()
    rot, ident = rotation(gen_ref[...])
    rot_high, rot_low = split(rot)
    rot_ref[0] = rot_high
    rot_ref[1] = rot_low
    fetch.wait()

    def run(k, states):
        for s in range(SEG):
            out = []
            for g in range(CHUNKS):
                t = g * per + per - 1 - k * SEG - s
                moved = mm3(states[g] * d_ref[pl.ds(t, 1), :], rot_ref[0], rot_ref[1])
                out.append(
                    jnp.concatenate([moved[:width], moved[width:] + f_ref[t].astype(F32)], axis=0)
                )
            states = out
        for g in range(CHUNKS):
            raw_ref[g * marks + marks - 1 - k] = states[g]

    first = jnp.concatenate([ident, jnp.zeros((f_ref.shape[1], width), F32)], axis=0)
    run(0, [first] * CHUNKS)

    def more(k, _):
        run(k, [raw_ref[g * marks + marks - k] for g in range(CHUNKS)])
        return 0

    lax.fori_loop(1, marks, more, 0)
    acc = raw_ref[(CHUNKS - 1) * marks]
    for g in range(CHUNKS - 2, -1, -1):
        suffix_ref[g] = acc
        acc = compose(acc, raw_ref[g * marks], width)
    map_ref[...] = acc


def marks_kernel(raw_ref, suffix_ref, in_hbm, zh_ref, zl_ref, zu_ref, flip_ref, in_ref, sem):
    fetch = pltpu.make_async_copy(in_hbm, in_ref, sem)
    fetch.start()
    count, rows, width = raw_ref.shape
    marks = count // CHUNKS
    for j in range(count):
        g = j // marks
        full = raw_ref[j]
        if g < CHUNKS - 1:
            full = compose(suffix_ref[g], full, width)
        high, low = split(full[:width])
        zh_ref[j] = high
        zl_ref[j] = low
        zu_ref[j] = full[width:]
    fetch.wait()
    segs = in_ref.shape[0] // SEG
    for s in range(SEG):
        block = jnp.concatenate([in_ref[m * SEG + s] for m in range(segs)], axis=0)
        flip_ref[s] = block.T


def early(bit):
    return (lax.axis_index("tm") & bit) == 0


def merge_kernel(bit, own_ref, other_ref, out_ref):
    width = own_ref.shape[1]
    first = early(bit)

    @pl.when(first)
    def _():
        out_ref[...] = compose(other_ref[...], own_ref[...], width)

    @pl.when(jnp.logical_not(first))
    def _():
        out_ref[...] = compose(own_ref[...], other_ref[...], width)


def top_kernel(bit, vec_ref, own_ref, other_ref, out_ref):
    width = own_ref.shape[1]
    first = early(bit)

    @pl.when(first)
    def _():
        out_ref[...] = apply(apply(vec_ref[...], other_ref[...], width), own_ref[...], width)

    @pl.when(jnp.logical_not(first))
    def _():
        out_ref[...] = apply(apply(vec_ref[...], own_ref[...], width), other_ref[...], width)


def later_kernel(bit, other_ref, later_ref, out_ref):
    width = other_ref.shape[1]
    first = early(bit)

    @pl.when(first)
    def _():
        out_ref[...] = compose(other_ref[...], later_ref[...], width)

    @pl.when(jnp.logical_not(first))
    def _():
        out_ref[...] = later_ref[...]


def first_later_kernel(bit, other_ref, out_ref):
    rows, width = other_ref.shape
    first = early(bit)

    @pl.when(first)
    def _():
        out_ref[...] = other_ref[...]

    @pl.when(jnp.logical_not(first))
    def _():
        out_ref[...] = (
            lax.broadcasted_iota(jnp.int32, (rows, width), 0) == lax.broadcasted_iota(jnp.int32, (rows, width), 1)
        ).astype(F32)


def sweep_kernel(
    bit, end_ref, got_ref, later_ref, zh_ref, zl_ref, zu_ref, rot_ref, d_ref, f_ref, flip_ref,
    adj_hbm, keep_ref, give_ref, cur, low_ref, sems,
):
    count, width = zh_ref.shape[0], zh_ref.shape[1]
    cols = end_ref.shape[0]
    v = jnp.where(early(bit), got_ref[...], end_ref[...])
    v = apply(v, later_ref[...], width)
    v_high, v_low = split(v)

    def send(at):
        return pltpu.make_async_copy(low_ref.at[at], adj_hbm.at[:, at], sems.at[at])

    for j in range(count):
        z = mm(v_high, zh_ref[j]) + mm(v_low, zh_ref[j]) + mm(v_high, zl_ref[j]) + zu_ref[j]
        if j > 0:
            cur[j - 1] = z
        low_ref[0, j] = z.astype(BF16)
    cur[count - 1] = v
    send(0).start()
    grad = mm(flip_ref[0], low_ref[0].reshape(count * cols, width))
    pack = 4
    for s in range(SEG - 1):
        at = SEG - 1 - s
        for p in range(0, count, pack):
            scaled = jnp.concatenate(
                [cur[m] * d_ref[m * SEG + at : m * SEG + at + 1, :] for m in range(p, p + pack)], axis=0
            )
            out = mm3(scaled, rot_ref[0], rot_ref[1])
            for m in range(p, p + pack):
                value = out[(m - p) * cols : (m - p + 1) * cols] + f_ref[m * SEG + at].astype(F32)
                cur[m] = value
                low_ref[at, m] = value.astype(BF16)
        send(at).start()
        grad = grad + mm(flip_ref[at], low_ref[at].reshape(count * cols, width))
    grad = grad.T
    half = width // 2
    first = early(1)
    keep_ref[...] = jnp.where(first, grad[:half], grad[half:])
    give_ref[...] = jnp.where(first, grad[half:], grad[:half])
    for at in range(SEG):
        send(at).wait()


def halve_kernel(bit, keep_ref, got_ref, mine_ref, give_ref):
    total = keep_ref[...] + got_ref[...]
    half = total.shape[0] // 2
    first = early(bit)
    mine_ref[...] = jnp.where(first, total[:half], total[half:])
    give_ref[...] = jnp.where(first, total[half:], total[:half])


def join_kernel(own_ref, far_ref, core_ref, both_ref, out_ref):
    rows = own_ref.shape[0]
    place = lax.axis_index("tm")
    low, high = place & 1, (place // 2) & 1
    for ref, a, b in (
        (own_ref, low, high),
        (far_ref, low, 1 - high),
        (core_ref, 1 - low, high),
        (both_ref, 1 - low, 1 - high),
    ):
        out_ref[pl.ds(pl.multiple_of((2 * a + b) * rows, rows), rows), :] = ref[...]


VM = pltpu.VMEM


def near(x):
    return pltpu.with_memory_space_constraint(x, VM)


def call(kernel, name, out, *args, where=None, scratch=(), flops=0, data=0):
    where = where or {}
    ins = [pl.BlockSpec(memory_space=pl.ANY if i in where else VM) for i in range(len(args))]
    args = [a if i in where else near(a) for i, a in enumerate(args)]
    outs = tuple(
        pl.BlockSpec(memory_space=pl.ANY if isinstance(o, jax.ShapeDtypeStruct) and len(o.shape) > 2 else VM)
        for o in out
    )
    return pl.pallas_call(
        kernel,
        out_shape=tuple(out),
        in_specs=ins,
        out_specs=outs,
        scratch_shapes=list(scratch),
        compiler_params=pltpu.CompilerParams(vmem_limit_bytes=VMEM_LIMIT),
        cost_estimate=pl.CostEstimate(flops=flops, bytes_accessed=data, transcendentals=0),
        name=name,
    )(*args)


def build(gen, derivs, force):
    steps, width = derivs.shape
    cols = force.shape[1]
    rows = width + cols
    return call(
        build_kernel,
        "build",
        (
            VM((rows, width), F32),
            VM((steps // SEG, rows, width), F32),
            VM((CHUNKS - 1, rows, width), F32),
            VM((2, width, width), BF16),
            VM(force.shape, BF16),
        ),
        gen,
        derivs,
        force,
        where={2},
        scratch=[pltpu.SemaphoreType.DMA],
        flops=6 * steps * rows * width * width,
    )


def mark_maps(raw, suffix, ins):
    count, rows, width = raw.shape
    steps, cols, feats = ins.shape
    return call(
        marks_kernel,
        "marks",
        (
            VM((count, width, width), BF16),
            VM((count, width, width), BF16),
            VM((count, rows - width, width), F32),
            VM((SEG, feats, steps // SEG * cols), BF16),
        ),
        raw,
        suffix,
        ins,
        where={2},
        scratch=[VM(ins.shape, BF16), pltpu.SemaphoreType.DMA],
        flops=6 * count * rows * width * width,
        data=15_000_000,
    )


def sweep(bit, end, got, later, zh, zl, zu, rot, derivs, force, flipped):
    steps, cols, width = force.shape
    feats = flipped.shape[1]
    segs = steps // SEG
    adj, keep, give = call(
        functools.partial(sweep_kernel, bit),
        "sweep",
        (
            shape((segs, SEG, cols, width), BF16),
            VM((width // 2, feats), F32),
            VM((width // 2, feats), F32),
        ),
        end, got, later, zh, zl, zu, rot, derivs, force, flipped,
        scratch=[
            VM((segs, cols, width), F32),
            VM((SEG, segs, cols, width), BF16),
            pltpu.SemaphoreType.DMA((SEG,)),
        ],
        flops=8 * steps * cols * width * width,
    )
    return adj.reshape(steps, cols, width), keep, give


def shape(dims, kind=F32):
    return jax.ShapeDtypeStruct(dims, kind)


def swap(x, bit):
    n = lax.axis_size("tm")
    return lax.ppermute(x, "tm", [(i, i ^ bit) for i in range(n)])


def incoming(own, terminal):
    n = lax.axis_size("tm")
    rows, width = own.shape
    flops = 6 * rows * width * width
    bits = [1 << k for k in range(n.bit_length() - 1)]
    total, later, top = own, None, None
    vec = VM(terminal.shape, F32)
    whole = VM(own.shape, F32)
    for bit in bits[:-1]:
        other = swap(total, bit)
        if later is None:
            (later,) = call(functools.partial(first_later_kernel, bit), "later", (whole,), other)
        else:
            (later,) = call(functools.partial(later_kernel, bit), "later", (whole,), other, later, flops=flops)
        if bit < bits[-2]:
            (total,) = call(functools.partial(merge_kernel, bit), "merge", (whole,), total, other, flops=flops)
        else:
            (top,) = call(functools.partial(top_kernel, bit), "top", (vec,), terminal, total, other, flops=flops // 5)
    return bits[-1], swap(top, bits[-1]), later


def all_sum(keep, give):
    n = lax.axis_size("tm")
    quarter = VM((keep.shape[0] // 2, keep.shape[1]), F32)
    mine, give = call(functools.partial(halve_kernel, 2), "halve", (quarter, quarter), keep, swap(give, 1))
    x = mine + swap(give, 2)
    bit = 4
    while bit < n:
        x = x + swap(x, bit)
        bit *= 2
    far = swap(x, 2)
    core = swap(x, 1)
    both = swap(far, 1)
    (out,) = call(join_kernel, "join", (shape((4 * x.shape[0], x.shape[1])),), x, far, core, both)
    return out


def body(generator, derivs, forcing, inputs, terminal):
    force = jnp.transpose(forcing, (0, 2, 1))
    ins = jnp.transpose(inputs, (0, 2, 1))
    end = terminal.T
    own, raw, suffix, rot, force = build(generator, derivs, force)
    zh, zl, zu, flipped = mark_maps(raw, suffix, ins)
    bit, got, later = incoming(own, end)
    adj, keep, give = sweep(bit, end, got, later, zh, zl, zu, rot, derivs, force, flipped)
    return jnp.transpose(adj, (0, 2, 1)), all_sum(keep, give)


def solution(mesh):
    in_specs = (
        P(),
        P(("groups", "tm"), None),
        P(("groups", "tm"), None, None),
        P(("groups", "tm"), None, None),
        P("groups", None),
    )
    out_specs = (P(("groups", "tm"), None, None), P("groups", None))
    return jax.shard_map(body, mesh=mesh, in_specs=in_specs, out_specs=out_specs, check_vma=False)
```

time: 120 us -> 84.2 us (0.70)
  Pallas kernels: 71.9 us -> 33.7 us
  other arithmetic: 14.3 us -> 0.03 us
  waiting for transfers between devices: 20.3 us -> 32.4 us
  local copies, waits for them, and re-layouts: 0.02 us -> 4.05 us
    pallas_call x11, Pallas kernels: 71.9 us -> 33.7 us  [call(): pl.pallas_call(kernel, out_shape=tuple(out), in_specs=ins, out_specs=outs...]
    select_n x11 -> x0, other arithmetic: 12.5 us -> none  [the longest x3 5.23 us: incoming(): later = jnp.where(early, compose(other, later), later)]
    ppermute x10 -> x11, waiting for transfers between devices: 20.3 us -> 32.4 us  [swap(): return lax.ppermute(x, 'tm', [(i, i ^ bit) for i in range(n)])]
    unnamed x10 -> x12, local copies, waits for them, and re-layouts: 0.02 us -> 4.05 us
    ppermute x10 -> x11, starting transfers between devices: 12.2 us -> 13.1 us  [swap(): return lax.ppermute(x, 'tm', [(i, i ^ bit) for i in range(n)])]
  transfers between devices with their start and end apart: 10 -> 11, of which waited for: 8 -> 9; matrix products, arithmetic and copies ran while one was open for 5% -> 0% of each run, Pallas kernels for 15% -> 5%
where the time goes in v1:
time: 84.2 us; the launch traced here: 84 us
  Pallas kernels  33.7 us (40%)
  waiting for transfers between devices  32.4 us (38%)
  starting transfers between devices  13.1 us (16%)
  local copies, waits for them, and re-layouts  4.05 us (5%)
    pallas_call x11, Pallas kernels, call(): pl.pallas_call(kernel, out_shape=tuple(out), in_specs=ins, out_specs=outs...  33.7 us
    ppermute x11, waiting for transfers between devices, swap(): return lax.ppermute(x, 'tm', [(i, i ^ bit) for i in range(n)])  32.4 us
    ppermute x11, starting transfers between devices, swap(): return lax.ppermute(x, 'tm', [(i, i ^ bit) for i in range(n)])  13.1 us
    unnamed x12, local copies, waits for them, and re-layouts  4.05 us
  transfers between devices with their start and end apart: 11, of which 9 were waited for; matrix products, arithmetic and copies ran while one was open for 0% of the time, Pallas kernels for 5%

profile of v1, /device:TPU:0, one launch (start us, length us, event | category | flops | bytes accessed | tf_op | source)
XLA Modules:
  0.0 84.0 jit_solution(5708752017043698974)
XLA Ops:
  0.6 2.2 %copy-done.2 = bf16[128,256,64]{1,2,0:T(8,128)(2,1)S(1)} copy-done((bf16[128,256,64]{1,2,0:T(8,128)(2,1)S(1)}, bf16[128,256,64]{1,2,0:T(8,128)(2,1)}, u32[]{:S(2)}) %copy-start.2) | copy-done | bytes 4194328
  2.8 0.9 %copy-done.3 = f32[256,256]{1,0:T(8,128)S(1)} copy-done((f32[256,256]{1,0:T(8,128)S(1)}, f32[256,256]{1,0:T(8,128)}, u32[]{:S(2)}) %copy-start.3) | copy-done | bytes 262168
  3.8 0.9 %copy-done.4 = f32[128,256]{1,0:T(8,128)S(1)} copy-done((f32[128,256]{1,0:T(8,128)S(1)}, f32[128,256]{1,0:T(8,128)}, u32[]{:S(2)}) %copy-start.4) | copy-done | bytes 131096
  4.7 21.1 %build.1 = (f32[320,256]{1,0:T(8,128)S(1)}, f32[16,320,256]{2,1,0:T(8,128)S(1)}, f32[3,320,256]{2,1,0:T(8,128)S(1)}, bf16[2,256,256]{2,1,0:T(8,128)(2,1)S(1)}, bf16[128,64,256]{2,1,0:T(8,128)(2,1)S(1)}) custom-call(f32[256,256]{1,0:T(8,128)S(1)} %copy-done.3, f32[128,256]{1,0:T(8,128)S(1)} %copy-done.4, bf16[128,64,256]{2,1,0:T(8,128)(2,1)S(1)} %bitcast.9), custom_call_target="tpu_custom_call" | custom-call | flops 16106127360 | tf_op jit(solution)/shard_map/build/pallas_call | solution.py:263
  25.8 0.5 collective-permute-start
  26.3 1.3 %collective-permute-done.other_ref = f32[320,256]{1,0:T(8,128)S(1)} collective-permute-done((f32[320,256]{1,0:T(8,128)S(1)}, f32[320,256]{1,0:T(8,128)S(1)}, u32[]{:S(2)}, u32[]{:S(2)}) %collective-permute-start) | collective-permute-done | bytes 327712 | tf_op jit(solution)/shard_map/ppermute | solution.py:349
  27.6 0.3 merge.2.own_ref
  27.9 3.0 %collective-permute-start.1 = (f32[320,256]{1,0:T(8,128)S(1)}, f32[320,256]{1,0:T(8,128)S(1)}, u32[]{:S(2)}, u32[]{:S(2)}) collective-permute-start(f32[320,256]{1,0:T(8,128)S(1)} %merge.2.own_ref), channel_id=1, source_target_pairs={{0,2},{1,3},{2,0},{3,1},{4,6},{5,7},{6,4},{7,5},{8,10},{9,11},{10,... | collective-permute-start | bytes 983048 | tf_op jit(solution)/shard_map/ppermute | solution.py:349
  30.8 8.0 %collective-permute-done.1.other_ref = f32[320,256]{1,0:T(8,128)S(1)} collective-permute-done((f32[320,256]{1,0:T(8,128)S(1)}, f32[320,256]{1,0:T(8,128)S(1)}, u32[]{:S(2)}, u32[]{:S(2)}) %collective-permute-start.1) | collective-permute-done | bytes 327712 | tf_op jit(solution)/shard_map/ppermute | solution.py:349
  38.9 0.3 merge.3.own_ref
  39.2 1.9 %collective-permute-start.2 = (f32[320,256]{1,0:T(8,128)S(1)}, f32[320,256]{1,0:T(8,128)S(1)}, u32[]{:S(2)}, u32[]{:S(2)}) collective-permute-start(f32[320,256]{1,0:T(8,128)S(1)} %merge.3.own_ref), channel_id=1, source_target_pairs={{0,4},{1,5},{2,6},{3,7},{4,0},{5,1},{6,2},{7,3},{8,12},{9,13},{10,... | collective-permute-start | bytes 983048 | tf_op jit(solution)/shard_map/ppermute | solution.py:349
  41.0 7.4 %collective-permute-done.2.other_ref = f32[320,256]{1,0:T(8,128)S(1)} collective-permute-done((f32[320,256]{1,0:T(8,128)S(1)}, f32[320,256]{1,0:T(8,128)S(1)}, u32[]{:S(2)}, u32[]{:S(2)}) %collective-permute-start.2) | collective-permute-done | bytes 327712 | tf_op jit(solution)/shard_map/ppermute | solution.py:349
  48.5 0.6 top.1
  49.1 2.6 %collective-permute-start.3 = (f32[64,256]{1,0:T(8,128)S(1)}, f32[64,256]{1,0:T(8,128)S(1)}, u32[]{:S(2)}, u32[]{:S(2)}) collective-permute-start(f32[64,256]{1,0:T(8,128)S(1)} %top.1), channel_id=1, source_target_pairs={{0,8},{1,9},{2,10},{3,11},{4,12},{5,13},{6,14},{7,15},{8,0},{9,1},... | collective-permute-start | bytes 196616 | tf_op jit(solution)/shard_map/ppermute | solution.py:349
  51.7 3.4 %marks.1 = (bf16[16,256,256]{2,1,0:T(8,128)(2,1)S(1)}, bf16[16,256,256]{2,1,0:T(8,128)(2,1)S(1)}, f32[16,64,256]{2,1,0:T(8,128)S(1)}, bf16[8,256,1024]{2,1,0:T(8,128)(2,1)S(1)}) custom-call(f32[16,320,256]{2,1,0:T(8,128)S(1)} %get-tuple-element.17.raw_ref, f32[3,320,256]{2,1,0:T(8,128)S(1)} %get-tuple-element.18.suffix_ref, bf16[128,64,256]{2,1,0:T(8,128)(2,1)S(1)} %bitcast.6), custom_call_target="tpu_custom_call" | custom-call | flops 2013265920 | bytes 15000000 | tf_op jit(solution)/shard_map/marks/pallas_call | solution.py:263
  55.2 0.3 later.4.later_ref
  55.5 0.3 later.5.later_ref
  55.8 0.0 collective-permute-done.3.got_ref
  55.8 6.5 %sweep.1 = (bf16[16,8,64,256]{3,2,1,0:T(8,128)(2,1)}, f32[128,256]{1,0:T(8,128)S(1)}, f32[128,256]{1,0:T(8,128)S(1)}) custom-call(f32[64,256]{1,0:T(8,128)S(1)} %bitcast.8, f32[64,256]{1,0:T(8,128)S(1)} %collective-permute-done.3.got_ref, f32[320,256]{1,0:T(8,128)S(1)} %later.5.later_ref, bf16[16,256,256]{2,1,0:T(8,128)(2,1)S(1)} %get-tuple-element.19.zh_ref, ...), custom_call_target="tpu_custom_call" | custom-call | flops 4294967296 | tf_op jit(solution)/shard_map/sweep/pallas_call | solution.py:263
  62.3 0.1 collective-permute-start.4
  62.4 1.3 %collective-permute-done.4.got_ref = f32[128,256]{1,0:T(8,128)S(1)} collective-permute-done((f32[128,256]{1,0:T(8,128)S(1)}, f32[128,256]{1,0:T(8,128)S(1)}, u32[]{:S(2)}, u32[]{:S(2)}) %collective-permute-start.4) | collective-permute-done | bytes 131104 | tf_op jit(solution)/shard_map/ppermute | solution.py:349
  63.8 1.3 %collective-permute-start.5 = (f32[64,256]{1,0:T(8,128)S(1)}, f32[64,256]{1,0:T(8,128)S(1)}, u32[]{:S(2)}, u32[]{:S(2)}) collective-permute-start(f32[64,256]{1,0:T(8,128)S(1)} %get-tuple-element.29), channel_id=1, source_target_pairs={{0,2},{1,3},{2,0},{3,1},{4,6},{5,7},{6,4},{7,5},{8,10},{9,11},{10,... | collective-permute-start | bytes 196616 | tf_op jit(solution)/shard_map/ppermute | solution.py:349
  65.1 3.0 %collective-permute-done.5 = f32[64,256]{1,0:T(8,128)S(1)} collective-permute-done((f32[64,256]{1,0:T(8,128)S(1)}, f32[64,256]{1,0:T(8,128)S(1)}, u32[]{:S(2)}, u32[]{:S(2)}) %collective-permute-start.5) | collective-permute-done | bytes 65568 | tf_op jit(solution)/shard_map/ppermute | solution.py:349
  68.1 1.4 %collective-permute-start.6 = (f32[64,256]{1,0:T(8,128)S(1)}, f32[64,256]{1,0:T(8,128)S(1)}, u32[]{:S(2)}, u32[]{:S(2)}) collective-permute-start(f32[64,256]{1,0:T(8,128)S(1)} %add.9), channel_id=1, source_target_pairs={{0,4},{1,5},{2,6},{3,7},{4,0},{5,1},{6,2},{7,3},{8,12},{9,13},{10,... | collective-permute-start | bytes 196616 | tf_op jit(solution)/shard_map/ppermute | solution.py:349
  69.5 3.0 %collective-permute-done.6 = f32[64,256]{1,0:T(8,128)S(1)} collective-permute-done((f32[64,256]{1,0:T(8,128)S(1)}, f32[64,256]{1,0:T(8,128)S(1)}, u32[]{:S(2)}, u32[]{:S(2)}) %collective-permute-start.6) | collective-permute-done | bytes 65568 | tf_op jit(solution)/shard_map/ppermute | solution.py:349
  72.5 1.2 %collective-permute-start.7 = (f32[64,256]{1,0:T(8,128)S(1)}, f32[64,256]{1,0:T(8,128)S(1)}, u32[]{:S(2)}, u32[]{:S(2)}) collective-permute-start(f32[64,256]{1,0:T(8,128)S(1)} %add.10), channel_id=1, source_target_pairs={{0,8},{1,9},{2,10},{3,11},{4,12},{5,13},{6,14},{7,15},{8,0},{9,1},... | collective-permute-start | bytes 196616 | tf_op jit(solution)/shard_map/ppermute | solution.py:349
  73.7 4.0 %collective-permute-done.7 = f32[64,256]{1,0:T(8,128)S(1)} collective-permute-done((f32[64,256]{1,0:T(8,128)S(1)}, f32[64,256]{1,0:T(8,128)S(1)}, u32[]{:S(2)}, u32[]{:S(2)}) %collective-permute-start.7) | collective-permute-done | bytes 65568 | tf_op jit(solution)/shard_map/ppermute | solution.py:349
  77.7 1.3 %collective-permute-start.8 = (f32[64,256]{1,0:T(8,128)S(1)}, f32[64,256]{1,0:T(8,128)S(1)}, u32[]{:S(2)}, u32[]{:S(2)}) collective-permute-start(f32[64,256]{1,0:T(8,128)S(1)} %add.11.own_ref), channel_id=1, source_target_pairs={{0,2},{1,3},{2,0},{3,1},{4,6},{5,7},{6,4},{7,5},{8,10},{9,11},{10,... | collective-permute-start | bytes 196616 | tf_op jit(solution)/shard_map/ppermute | solution.py:349
  79.0 3.0 %collective-permute-done.8.far_ref = f32[64,256]{1,0:T(8,128)S(1)} collective-permute-done((f32[64,256]{1,0:T(8,128)S(1)}, f32[64,256]{1,0:T(8,128)S(1)}, u32[]{:S(2)}, u32[]{:S(2)}) %collective-permute-start.8) | collective-permute-done | bytes 65568 | tf_op jit(solution)/shard_map/ppermute | solution.py:349
  82.0 0.0 collective-permute-start.10
  82.0 1.2 %collective-permute-done.10.both_ref = f32[64,256]{1,0:T(8,128)S(1)} collective-permute-done((f32[64,256]{1,0:T(8,128)S(1)}, f32[64,256]{1,0:T(8,128)S(1)}, u32[]{:S(2)}, u32[]{:S(2)}) %collective-permute-start.10) | collective-permute-done | bytes 65568 | tf_op jit(solution)/shard_map/ppermute | solution.py:349
  83.3 0.7 join.1
  (16 shorter events, 0.1 us)
Async XLA Ops:
  0.6 2.2 %copy-start.2 = (bf16[128,256,64]{1,2,0:T(8,128)(2,1)S(1)}, bf16[128,256,64]{1,2,0:T(8,128)(2,1)}, u32[]{:S(2)}) copy-start(bf16[128,256,64]{1,2,0:T(8,128)(2,1)} %param.7) | copy-start | bytes 12582916
  2.8 0.9 %copy-start.3 = (f32[256,256]{1,0:T(8,128)S(1)}, f32[256,256]{1,0:T(8,128)}, u32[]{:S(2)}) copy-start(f32[256,256]{1,0:T(8,128)} %gen_ref.1) | copy-start | bytes 786436
  3.8 0.9 %copy-start.4 = (f32[128,256]{1,0:T(8,128)S(1)}, f32[128,256]{1,0:T(8,128)}, u32[]{:S(2)}) copy-start(f32[128,256]{1,0:T(8,128)} %d_ref.3) | copy-start | bytes 393220
  4.7 43.8 %copy-start.1 = (f32[256,64]{0,1:T(8,128)S(1)}, f32[256,64]{0,1:T(8,128)}, u32[]{:S(2)}) copy-start(f32[256,64]{0,1:T(8,128)} %param.9) | copy-start | bytes 196612
  4.7 47.0 %copy-start = (bf16[128,256,64]{1,2,0:T(8,128)(2,1)S(1)}, bf16[128,256,64]{1,2,0:T(8,128)(2,1)}, u32[]{:S(2)}) copy-start(bf16[128,256,64]{1,2,0:T(8,128)(2,1)} %param.8) | copy-start | bytes 12582916
  25.8 1.8 %collective-permute-start = (f32[320,256]{1,0:T(8,128)S(1)}, f32[320,256]{1,0:T(8,128)S(1)}, u32[]{:S(2)}, u32[]{:S(2)}) collective-permute-start(f32[320,256]{1,0:T(8,128)S(1)} %get-tuple-element.16.own_ref), channel_id=1, source_target_pairs={{0,1},{1,0},{2,3},{3,2},{4,5},{5,4},{6,7},{7,6},{8,9},{9,8},{10,11... | collective-permute-start | bytes 983048 | tf_op jit(solution)/shard_map/ppermute | solution.py:349
  27.9 11.0 %collective-permute-start.1 = (f32[320,256]{1,0:T(8,128)S(1)}, f32[320,256]{1,0:T(8,128)S(1)}, u32[]{:S(2)}, u32[]{:S(2)}) collective-permute-start(f32[320,256]{1,0:T(8,128)S(1)} %merge.2.own_ref), channel_id=1, source_target_pairs={{0,2},{1,3},{2,0},{3,1},{4,6},{5,7},{6,4},{7,5},{8,10},{9,11},{10,... | collective-permute-start | bytes 983048 | tf_op jit(solution)/shard_map/ppermute | solution.py:349
  39.2 9.3 %collective-permute-start.2 = (f32[320,256]{1,0:T(8,128)S(1)}, f32[320,256]{1,0:T(8,128)S(1)}, u32[]{:S(2)}, u32[]{:S(2)}) collective-permute-start(f32[320,256]{1,0:T(8,128)S(1)} %merge.3.own_ref), channel_id=1, source_target_pairs={{0,4},{1,5},{2,6},{3,7},{4,0},{5,1},{6,2},{7,3},{8,12},{9,13},{10,... | collective-permute-start | bytes 983048 | tf_op jit(solution)/shard_map/ppermute | solution.py:349
  49.1 6.7 %collective-permute-start.3 = (f32[64,256]{1,0:T(8,128)S(1)}, f32[64,256]{1,0:T(8,128)S(1)}, u32[]{:S(2)}, u32[]{:S(2)}) collective-permute-start(f32[64,256]{1,0:T(8,128)S(1)} %top.1), channel_id=1, source_target_pairs={{0,8},{1,9},{2,10},{3,11},{4,12},{5,13},{6,14},{7,15},{8,0},{9,1},... | collective-permute-start | bytes 196616 | tf_op jit(solution)/shard_map/ppermute | solution.py:349
  51.7 4.2 %copy-start.5 = (f32[128,256]{1,0:T(8,128)S(1)}, f32[128,256]{1,0:T(8,128)}, u32[]{:S(2)}) copy-start(f32[128,256]{1,0:T(8,128)} %d_ref.3) | copy-start | bytes 393220
  62.3 1.4 %collective-permute-start.4 = (f32[128,256]{1,0:T(8,128)S(1)}, f32[128,256]{1,0:T(8,128)S(1)}, u32[]{:S(2)}, u32[]{:S(2)}) collective-permute-start(f32[128,256]{1,0:T(8,128)S(1)} %get-tuple-element.27), channel_id=1, source_target_pairs={{0,1},{1,0},{2,3},{3,2},{4,5},{5,4},{6,7},{7,6},{8,9},{9,8},{10,11... | collective-permute-start | bytes 393224 | tf_op jit(solution)/shard_map/ppermute | solution.py:349
  63.8 4.3 %collective-permute-start.5 = (f32[64,256]{1,0:T(8,128)S(1)}, f32[64,256]{1,0:T(8,128)S(1)}, u32[]{:S(2)}, u32[]{:S(2)}) collective-permute-start(f32[64,256]{1,0:T(8,128)S(1)} %get-tuple-element.29), channel_id=1, source_target_pairs={{0,2},{1,3},{2,0},{3,1},{4,6},{5,7},{6,4},{7,5},{8,10},{9,11},{10,... | collective-permute-start | bytes 196616 | tf_op jit(solution)/shard_map/ppermute | solution.py:349
  68.1 4.3 %collective-permute-start.6 = (f32[64,256]{1,0:T(8,128)S(1)}, f32[64,256]{1,0:T(8,128)S(1)}, u32[]{:S(2)}, u32[]{:S(2)}) collective-permute-start(f32[64,256]{1,0:T(8,128)S(1)} %add.9), channel_id=1, source_target_pairs={{0,4},{1,5},{2,6},{3,7},{4,0},{5,1},{6,2},{7,3},{8,12},{9,13},{10,... | collective-permute-start | bytes 196616 | tf_op jit(solution)/shard_map/ppermute | solution.py:349
  72.5 5.2 %collective-permute-start.7 = (f32[64,256]{1,0:T(8,128)S(1)}, f32[64,256]{1,0:T(8,128)S(1)}, u32[]{:S(2)}, u32[]{:S(2)}) collective-permute-start(f32[64,256]{1,0:T(8,128)S(1)} %add.10), channel_id=1, source_target_pairs={{0,8},{1,9},{2,10},{3,11},{4,12},{5,13},{6,14},{7,15},{8,0},{9,1},... | collective-permute-start | bytes 196616 | tf_op jit(solution)/shard_map/ppermute | solution.py:349
  77.7 4.3 %collective-permute-start.8 = (f32[64,256]{1,0:T(8,128)S(1)}, f32[64,256]{1,0:T(8,128)S(1)}, u32[]{:S(2)}, u32[]{:S(2)}) collective-permute-start(f32[64,256]{1,0:T(8,128)S(1)} %add.11.own_ref), channel_id=1, source_target_pairs={{0,2},{1,3},{2,0},{3,1},{4,6},{5,7},{6,4},{7,5},{8,10},{9,11},{10,... | collective-permute-start | bytes 196616 | tf_op jit(solution)/shard_map/ppermute | solution.py:349
  79.0 3.0 %collective-permute-start.9 = (f32[64,256]{1,0:T(8,128)S(1)}, f32[64,256]{1,0:T(8,128)S(1)}, u32[]{:S(2)}, u32[]{:S(2)}) collective-permute-start(f32[64,256]{1,0:T(8,128)S(1)} %add.11.own_ref), channel_id=1, source_target_pairs={{0,1},{1,0},{2,3},{3,2},{4,5},{5,4},{6,7},{7,6},{8,9},{9,8},{10,11... | collective-permute-start | bytes 196616 | tf_op jit(solution)/shard_map/ppermute | solution.py:349
  82.0 1.3 %collective-permute-start.10 = (f32[64,256]{1,0:T(8,128)S(1)}, f32[64,256]{1,0:T(8,128)S(1)}, u32[]{:S(2)}, u32[]{:S(2)}) collective-permute-start(f32[64,256]{1,0:T(8,128)S(1)} %collective-permute-done.8.far_ref), channel_id=1, source_target_pairs={{0,1},{1,0},{2,3},{3,2},{4,5},{5,4},{6,7},{7,6},{8,9},{9,8},{10,11... | collective-permute-start | bytes 196616 | tf_op jit(solution)/shard_map/ppermute | solution.py:349

commit v2 on v1

--- a/solution.py
+++ b/solution.py
@@ -17,10 +17,6 @@
 
 def mm(a, b):
     return jnp.dot(a, b, preferred_element_type=F32)
-
-
-def full_mm(a, b):
-    return jnp.dot(a, b, precision=lax.Precision.HIGHEST, preferred_element_type=F32)
 
 
 def split(x):
@@ -41,13 +37,15 @@
         lax.broadcasted_iota(jnp.int32, (n, n), 0) == lax.broadcasted_iota(jnp.int32, (n, n), 1)
     ).astype(F32)
     c = [1.0 / math.factorial(k) for k in range(13)]
-    s2 = full_mm(skew, skew)
-    s3 = full_mm(s2, skew)
-    s4 = full_mm(s2, s2)
+    halves = split(skew)
+    s2 = mm3(skew, *halves)
+    s3 = mm3(s2, *halves)
+    s4 = mm3(s2, *split(s2))
     top = c[8] * ident + c[9] * skew + c[10] * s2 + c[11] * s3 + c[12] * s4
     mid = c[4] * ident + c[5] * skew + c[6] * s2 + c[7] * s3
     bottom = ident + skew + c[2] * s2 + c[3] * s3
-    return bottom + full_mm(s4, mid + full_mm(s4, top)), ident
+    inner = mid + mm3(s4, *split(top))
+    return bottom + mm3(s4, *split(inner))
 
 
 def compose(rows_in, through, width):
@@ -61,20 +59,26 @@
     return mm3(vec, high, low) + through[width:]
 
 
-def build_kernel(gen_ref, d_ref, f_hbm, map_ref, raw_ref, suffix_ref, rot_ref, f_ref, sem):
+def build_kernel(gen_hbm, d_hbm, f_hbm, map_ref, raw_ref, suffix_ref, rot_ref, d_ref, f_ref, gen_ref, sems):
     steps, width = d_ref.shape
     per = steps // CHUNKS
     marks = per // SEG
-    fetch = pltpu.make_async_copy(f_hbm, f_ref, sem)
-    fetch.start()
-    rot, ident = rotation(gen_ref[...])
+    fetches = [
+        pltpu.make_async_copy(far, here, sems.at[i])
+        for i, (far, here) in enumerate(((gen_hbm, gen_ref), (d_hbm, d_ref), (f_hbm, f_ref)))
+    ]
+    for fetch in fetches:
+        fetch.start()
+    fetches[0].wait()
+    rot = rotation(gen_ref[...])
     rot_high, rot_low = split(rot)
     rot_ref[0] = rot_high
     rot_ref[1] = rot_low
-    fetch.wait()
-
-    def run(k, states):
-        for s in range(SEG):
+    fetches[1].wait()
+    fetches[2].wait()
+
+    def run(k, states, done):
+        for s in range(done, SEG):
             out = []
             for g in range(CHUNKS):
                 t = g * per + per - 1 - k * SEG - s
@@ -86,11 +90,15 @@
         for g in range(CHUNKS):
             raw_ref[g * marks + marks - 1 - k] = states[g]
 
-    first = jnp.concatenate([ident, jnp.zeros((f_ref.shape[1], width), F32)], axis=0)
-    run(0, [first] * CHUNKS)
+    first = []
+    for g in range(CHUNKS):
+        end = (g + 1) * per
+        column = d_ref[end - 8 : end, :].T[:, 7:8]
+        first.append(jnp.concatenate([rot * column, f_ref[end - 1].astype(F32)], axis=0))
+    run(0, first, 1)
 
     def more(k, _):
-        run(k, [raw_ref[g * marks + marks - k] for g in range(CHUNKS)])
+        run(k, [raw_ref[g * marks + marks - k] for g in range(CHUNKS)], 0)
         return 0
 
     lax.fori_loop(1, marks, more, 0)
@@ -139,22 +147,19 @@
         out_ref[...] = compose(own_ref[...], other_ref[...], width)
 
 
-def top_kernel(bit, vec_ref, own_ref, other_ref, out_ref):
-    width = own_ref.shape[1]
-    first = early(bit)
-
-    @pl.when(first)
-    def _():
-        out_ref[...] = apply(apply(vec_ref[...], other_ref[...], width), own_ref[...], width)
-
-    @pl.when(jnp.logical_not(first))
-    def _():
-        out_ref[...] = apply(apply(vec_ref[...], own_ref[...], width), other_ref[...], width)
-
-
-def later_kernel(bit, other_ref, later_ref, out_ref):
+def end_kernel(bit, own_ref, other_ref, vec_ref, out_ref, through_ref):
+    merge_kernel(bit, own_ref, other_ref, out_ref)
+    through_ref[...] = apply(vec_ref[...], out_ref[...], own_ref.shape[1])
+
+
+def apply_kernel(vec_ref, map_ref, out_ref):
+    out_ref[...] = apply(vec_ref[...], map_ref[...], map_ref.shape[1])
+
+
+def later_kernel(quarter, other_ref, later_ref, out_ref):
+    bit, only = quarter
     width = other_ref.shape[1]
-    first = early(bit)
+    first = lax.axis_index("tm") < only if only else early(bit)
 
     @pl.when(first)
     def _():
@@ -181,12 +186,16 @@
 
 
 def sweep_kernel(
-    bit, end_ref, got_ref, later_ref, zh_ref, zl_ref, zu_ref, rot_ref, d_ref, f_ref, flip_ref,
+    part, end_ref, got_ref, up_ref, down_ref, later_ref, zh_ref, zl_ref, zu_ref,
+    rot_ref, d_ref, f_ref, flip_ref,
     adj_hbm, keep_ref, give_ref, cur, low_ref, sems,
 ):
     count, width = zh_ref.shape[0], zh_ref.shape[1]
     cols = end_ref.shape[0]
-    v = jnp.where(early(bit), got_ref[...], end_ref[...])
+    place = lax.axis_index("tm") // part
+    v = jnp.where(place == 3, end_ref[...], got_ref[...])
+    v = jnp.where(place == 1, up_ref[...], v)
+    v = jnp.where(place == 0, down_ref[...], v)
     v = apply(v, later_ref[...], width)
     v_high, v_low = split(v)
 
@@ -248,14 +257,10 @@
 VM = pltpu.VMEM
 
 
-def near(x):
-    return pltpu.with_memory_space_constraint(x, VM)
-
-
 def call(kernel, name, out, *args, where=None, scratch=(), flops=0, data=0):
     where = where or {}
     ins = [pl.BlockSpec(memory_space=pl.ANY if i in where else VM) for i in range(len(args))]
-    args = [a if i in where else near(a) for i, a in enumerate(args)]
+    args = [pltpu.with_memory_space_constraint(a, pltpu.HBM if i in where else VM) for i, a in enumerate(args)]
     outs = tuple(
         pl.BlockSpec(memory_space=pl.ANY if isinstance(o, jax.ShapeDtypeStruct) and len(o.shape) > 2 else VM)
         for o in out
@@ -284,13 +289,14 @@
             VM((steps // SEG, rows, width), F32),
             VM((CHUNKS - 1, rows, width), F32),
             VM((2, width, width), BF16),
+            VM(derivs.shape, F32),
             VM(force.shape, BF16),
         ),
         gen,
         derivs,
         force,
-        where={2},
-        scratch=[pltpu.SemaphoreType.DMA],
+        where={0, 1, 2},
+        scratch=[VM(gen.shape, F32), pltpu.SemaphoreType.DMA((3,))],
         flops=6 * steps * rows * width * width,
     )
 
@@ -317,19 +323,19 @@
     )
 
 
-def sweep(bit, end, got, later, zh, zl, zu, rot, derivs, force, flipped):
+def sweep(entering, later, zh, zl, zu, rot, derivs, force, flipped):
     steps, cols, width = force.shape
     feats = flipped.shape[1]
     segs = steps // SEG
     adj, keep, give = call(
-        functools.partial(sweep_kernel, bit),
+        functools.partial(sweep_kernel, lax.axis_size("tm") // 4),
         "sweep",
         (
             shape((segs, SEG, cols, width), BF16),
             VM((width // 2, feats), F32),
             VM((width // 2, feats), F32),
         ),
-        end, got, later, zh, zl, zu, rot, derivs, force, flipped,
+        *entering, later, zh, zl, zu, rot, derivs, force, flipped,
         scratch=[
             VM((segs, cols, width), F32),
             VM((SEG, segs, cols, width), BF16),
@@ -349,25 +355,34 @@
     return lax.ppermute(x, "tm", [(i, i ^ bit) for i in range(n)])
 
 
-def incoming(own, terminal):
+def incoming(own, end):
     n = lax.axis_size("tm")
+    part = n // 4
     rows, width = own.shape
     flops = 6 * rows * width * width
-    bits = [1 << k for k in range(n.bit_length() - 1)]
-    total, later, top = own, None, None
-    vec = VM(terminal.shape, F32)
+    vec = VM(end.shape, F32)
     whole = VM(own.shape, F32)
-    for bit in bits[:-1]:
+    total, later, bit = own, None, 1
+    while bit < part:
         other = swap(total, bit)
         if later is None:
             (later,) = call(functools.partial(first_later_kernel, bit), "later", (whole,), other)
         else:
-            (later,) = call(functools.partial(later_kernel, bit), "later", (whole,), other, later, flops=flops)
-        if bit < bits[-2]:
+            (later,) = call(functools.partial(later_kernel, (bit, 0)), "later", (whole,), other, later, flops=flops)
+        if 2 * bit < part:
             (total,) = call(functools.partial(merge_kernel, bit), "merge", (whole,), total, other, flops=flops)
         else:
-            (top,) = call(functools.partial(top_kernel, bit), "top", (vec,), terminal, total, other, flops=flops // 5)
-    return bits[-1], swap(top, bits[-1]), later
+            total, last = call(
+                functools.partial(end_kernel, bit), "end", (whole, vec), total, other, end, flops=flops
+            )
+        bit *= 2
+    got = lax.ppermute(last, "tm", [(i + 3 * part, i + 2 * part) for i in range(part)])
+    second = lax.ppermute(total, "tm", [(i + part, i) for i in range(part)])
+    (top,) = call(apply_kernel, "top", (vec,), got, total, flops=flops // 5)
+    up = lax.ppermute(top, "tm", [(i + 2 * part, i + part) for i in range(part)])
+    down = lax.ppermute(top, "tm", [(i + 2 * part, i) for i in range(part)])
+    (later,) = call(functools.partial(later_kernel, (0, part)), "later", (whole,), second, later, flops=flops)
+    return (end, got, up, down), later
 
 
 def all_sum(keep, give):
@@ -390,10 +405,10 @@
     force = jnp.transpose(forcing, (0, 2, 1))
     ins = jnp.transpose(inputs, (0, 2, 1))
     end = terminal.T
-    own, raw, suffix, rot, force = build(generator, derivs, force)
+    own, raw, suffix, rot, derivs, force = build(generator, derivs, force)
     zh, zl, zu, flipped = mark_maps(raw, suffix, ins)
-    bit, got, later = incoming(own, end)
-    adj, keep, give = sweep(bit, end, got, later, zh, zl, zu, rot, derivs, force, flipped)
+    entering, later = incoming(own, end)
+    adj, keep, give = sweep(entering, later, zh, zl, zu, rot, derivs, force, flipped)
     return jnp.transpose(adj, (0, 2, 1)), all_sum(keep, give)
 
 

time: 84.2 us -> 76.9 us (0.913)
  waiting for transfers between devices: 32.4 us -> 27.1 us
  local copies, waits for them, and re-layouts: 4.05 us -> 0.01 us
  starting transfers between devices: 13.1 us -> 15.7 us
    ppermute x11 -> x9, waiting for transfers between devices: 32.4 us -> 22.2 us  [swap(): return lax.ppermute(x, 'tm', [(i, i ^ bit) for i in range(n)])]
    ppermute x0 -> x4, waiting for transfers between devices: none -> 4.94 us  [the longest x1 3.71 us: incoming(): second = lax.ppermute(total, 'tm', [(i + part, i) for i in range(part)])]
    ppermute x0 -> x4, starting transfers between devices: none -> 4.1 us  [the longest x1 1.3 us: incoming(): down = lax.ppermute(top, 'tm', [(i + 2 * part, i) for i in range(part)])]
    unnamed x12 -> x2, local copies, waits for them, and re-layouts: 4.05 us -> 0.01 us
    ppermute x11 -> x9, starting transfers between devices: 13.1 us -> 11.6 us  [swap(): return lax.ppermute(x, 'tm', [(i, i ^ bit) for i in range(n)])]
  transfers between devices with their start and end apart: 11 -> 13, of which waited for: 9 -> 10; matrix products, arithmetic and copies ran while one was open for 0% -> 0% of each run, Pallas kernels for 5% -> 6%
where the time goes in v2:
time: 76.9 us; the launch traced here: 76.7 us
  Pallas kernels  33 us (43%)
  waiting for transfers between devices  27.1 us (35%)
  starting transfers between devices  15.7 us (20%)
  between operations  0.78 us (1%)
    pallas_call x11, Pallas kernels, call(): pl.pallas_call(kernel, out_shape=tuple(out), in_specs=ins, out_specs=outs...  33 us
    ppermute x9, waiting for transfers between devices, swap(): return lax.ppermute(x, 'tm', [(i, i ^ bit) for i in range(n)])  22.2 us
    ppermute x9, starting transfers between devices, swap(): return lax.ppermute(x, 'tm', [(i, i ^ bit) for i in range(n)])  11.6 us
    ppermute x1, waiting for transfers between devices, incoming(): second = lax.ppermute(total, 'tm', [(i + part, i) for i in range(part)])  3.71 us
  transfers between devices with their start and end apart: 13, of which 10 were waited for; matrix products, arithmetic and copies ran while one was open for 0% of the time, Pallas kernels for 6%

profile of v2, /device:TPU:0, one launch (start us, length us, event | category | flops | bytes accessed | tf_op | source)
XLA Modules:
  0.0 76.7 jit_solution(9631727862545709189)
XLA Ops:
  0.6 20.7 %build.1 = (f32[320,256]{1,0:T(8,128)S(1)}, f32[16,320,256]{2,1,0:T(8,128)S(1)}, f32[3,320,256]{2,1,0:T(8,128)S(1)}, bf16[2,256,256]{2,1,0:T(8,128)(2,1)S(1)}, f...) custom-call(f32[256,256]{1,0:T(8,128)} %gen_hbm.1, f32[128,256]{1,0:T(8,128)} %d_hbm.1, bf16[128,64,256]{2,1,0:T(8,128)(2,1)} %bitcast.9), custom_call_target="tpu_custom_call" | custom-call | flops 16106127360 | tf_op jit(solution)/shard_map/build/pallas_call | solution.py:268
  21.4 0.5 collective-permute-start
  21.9 1.3 %collective-permute-done.other_ref = f32[320,256]{1,0:T(8,128)S(1)} collective-permute-done((f32[320,256]{1,0:T(8,128)S(1)}, f32[320,256]{1,0:T(8,128)S(1)}, u32[]{:S(2)}, u32[]{:S(2)}) %collective-permute-start) | collective-permute-done | bytes 327712 | tf_op jit(solution)/shard_map/ppermute | solution.py:355
  23.1 0.3 merge.1.own_ref
  23.4 3.0 %collective-permute-start.1 = (f32[320,256]{1,0:T(8,128)S(1)}, f32[320,256]{1,0:T(8,128)S(1)}, u32[]{:S(2)}, u32[]{:S(2)}) collective-permute-start(f32[320,256]{1,0:T(8,128)S(1)} %merge.1.own_ref), channel_id=1, source_target_pairs={{0,2},{1,3},{2,0},{3,1},{4,6},{5,7},{6,4},{7,5},{8,10},{9,11},{10,... | collective-permute-start | bytes 983048 | tf_op jit(solution)/shard_map/ppermute | solution.py:355
  26.4 8.0 %collective-permute-done.1.other_ref = f32[320,256]{1,0:T(8,128)S(1)} collective-permute-done((f32[320,256]{1,0:T(8,128)S(1)}, f32[320,256]{1,0:T(8,128)S(1)}, u32[]{:S(2)}, u32[]{:S(2)}) %collective-permute-start.1) | collective-permute-done | bytes 327712 | tf_op jit(solution)/shard_map/ppermute | solution.py:355
  34.4 0.5 end.1
  34.9 1.3 %collective-permute-start.5 = (f32[320,256]{1,0:T(8,128)S(1)}, f32[320,256]{1,0:T(8,128)S(1)}, u32[]{:S(2)}, u32[]{:S(2)}) collective-permute-start(f32[320,256]{1,0:T(8,128)S(1)} %get-tuple-element.21.map_ref), channel_id=1, source_target_pairs={{4,0},{5,1},{6,2},{7,3},{20,16},{21,17},{22,18},{23,19}} | collective-permute-start | bytes 983048 | tf_op jit(solution)/shard_map/ppermute | solution.py:380
  36.2 0.7 collective-permute-start.2
  36.9 0.0 collective-permute-done.2.vec_ref.got_ref
  36.9 0.2 top.1
  37.1 1.3 %collective-permute-start.4 = (f32[64,256]{1,0:T(8,128)S(1)}, f32[64,256]{1,0:T(8,128)S(1)}, u32[]{:S(2)}, u32[]{:S(2)}) collective-permute-start(f32[64,256]{1,0:T(8,128)S(1)} %top.1), channel_id=1, source_target_pairs={{8,0},{9,1},{10,2},{11,3},{24,16},{25,17},{26,18},{27,19}} | collective-permute-start | bytes 196616 | tf_op jit(solution)/shard_map/ppermute | solution.py:383
  38.4 0.8 %collective-permute-start.3 = (f32[64,256]{1,0:T(8,128)S(1)}, f32[64,256]{1,0:T(8,128)S(1)}, u32[]{:S(2)}, u32[]{:S(2)}) collective-permute-start(f32[64,256]{1,0:T(8,128)S(1)} %top.1), channel_id=1, source_target_pairs={{8,4},{9,5},{10,6},{11,7},{24,20},{25,21},{26,22},{27,23}} | collective-permute-start | bytes 196616 | tf_op jit(solution)/shard_map/ppermute | solution.py:382
  39.2 3.4 %marks.1 = (bf16[16,256,256]{2,1,0:T(8,128)(2,1)S(1)}, bf16[16,256,256]{2,1,0:T(8,128)(2,1)S(1)}, f32[16,64,256]{2,1,0:T(8,128)S(1)}, bf16[8,256,1024]{2,1,0:T(8,128)(2,1)S(1)}) custom-call(f32[16,320,256]{2,1,0:T(8,128)S(1)} %get-tuple-element.22.raw_ref, f32[3,320,256]{2,1,0:T(8,128)S(1)} %get-tuple-element.23.suffix_ref, bf16[128,64,256]{2,1,0:T(8,128)(2,1)} %bitcast.8), custom_call_target="tpu_custom_call" | custom-call | flops 2013265920 | bytes 15000000 | tf_op jit(solution)/shard_map/marks/pallas_call | solution.py:268
  42.7 0.3 later.4.later_ref
  43.0 3.7 %collective-permute-done.5.other_ref = f32[320,256]{1,0:T(8,128)S(1)} collective-permute-done((f32[320,256]{1,0:T(8,128)S(1)}, f32[320,256]{1,0:T(8,128)S(1)}, u32[]{:S(2)}, u32[]{:S(2)}) %collective-permute-start.5) | collective-permute-done | bytes 327712 | tf_op jit(solution)/shard_map/ppermute | solution.py:380
  46.7 0.3 later.5.later_ref
  47.0 1.2 %collective-permute-done.4.down_ref = f32[64,256]{1,0:T(8,128)S(1)} collective-permute-done((f32[64,256]{1,0:T(8,128)S(1)}, f32[64,256]{1,0:T(8,128)S(1)}, u32[]{:S(2)}, u32[]{:S(2)}) %collective-permute-start.4) | collective-permute-done | bytes 65568 | tf_op jit(solution)/shard_map/ppermute | solution.py:383
  48.3 0.0 collective-permute-done.3.up_ref
  48.3 6.5 %sweep.1 = (bf16[16,8,64,256]{3,2,1,0:T(8,128)(2,1)}, f32[128,256]{1,0:T(8,128)S(1)}, f32[128,256]{1,0:T(8,128)S(1)}) custom-call(f32[64,256]{1,0:T(8,128)S(1)} %bitcast.7, f32[64,256]{1,0:T(8,128)S(1)} %collective-permute-done.2.vec_ref.got_ref, f32[64,256]{1,0:T(8,128)S(1)} %collective-permute-done.3.up_ref, ...), custom_call_target="tpu_custom_call" | custom-call | flops 4294967296 | tf_op jit(solution)/shard_map/sweep/pallas_call | solution.py:268
  54.8 0.1 collective-permute-start.6
  54.8 1.3 %collective-permute-done.6.got_ref = f32[128,256]{1,0:T(8,128)S(1)} collective-permute-done((f32[128,256]{1,0:T(8,128)S(1)}, f32[128,256]{1,0:T(8,128)S(1)}, u32[]{:S(2)}, u32[]{:S(2)}) %collective-permute-start.6) | collective-permute-done | bytes 131104 | tf_op jit(solution)/shard_map/ppermute | solution.py:355
  56.2 1.6 %collective-permute-start.7 = (f32[64,256]{1,0:T(8,128)S(1)}, f32[64,256]{1,0:T(8,128)S(1)}, u32[]{:S(2)}, u32[]{:S(2)}) collective-permute-start(f32[64,256]{1,0:T(8,128)S(1)} %get-tuple-element.35), channel_id=1, source_target_pairs={{0,2},{1,3},{2,0},{3,1},{4,6},{5,7},{6,4},{7,5},{8,10},{9,11},{10,... | collective-permute-start | bytes 196616 | tf_op jit(solution)/shard_map/ppermute | solution.py:355
  57.8 2.7 %collective-permute-done.7 = f32[64,256]{1,0:T(8,128)S(1)} collective-permute-done((f32[64,256]{1,0:T(8,128)S(1)}, f32[64,256]{1,0:T(8,128)S(1)}, u32[]{:S(2)}, u32[]{:S(2)}) %collective-permute-start.7) | collective-permute-done | bytes 65568 | tf_op jit(solution)/shard_map/ppermute | solution.py:355
  60.5 1.9 %collective-permute-start.8 = (f32[64,256]{1,0:T(8,128)S(1)}, f32[64,256]{1,0:T(8,128)S(1)}, u32[]{:S(2)}, u32[]{:S(2)}) collective-permute-start(f32[64,256]{1,0:T(8,128)S(1)} %add.9), channel_id=1, source_target_pairs={{0,4},{1,5},{2,6},{3,7},{4,0},{5,1},{6,2},{7,3},{8,12},{9,13},{10,... | collective-permute-start | bytes 196616 | tf_op jit(solution)/shard_map/ppermute | solution.py:355
  62.5 2.4 %collective-permute-done.8 = f32[64,256]{1,0:T(8,128)S(1)} collective-permute-done((f32[64,256]{1,0:T(8,128)S(1)}, f32[64,256]{1,0:T(8,128)S(1)}, u32[]{:S(2)}, u32[]{:S(2)}) %collective-permute-start.8) | collective-permute-done | bytes 65568 | tf_op jit(solution)/shard_map/ppermute | solution.py:355
  64.9 3.2 %collective-permute-start.9 = (f32[64,256]{1,0:T(8,128)S(1)}, f32[64,256]{1,0:T(8,128)S(1)}, u32[]{:S(2)}, u32[]{:S(2)}) collective-permute-start(f32[64,256]{1,0:T(8,128)S(1)} %add.10), channel_id=1, source_target_pairs={{0,8},{1,9},{2,10},{3,11},{4,12},{5,13},{6,14},{7,15},{8,0},{9,1},... | collective-permute-start | bytes 196616 | tf_op jit(solution)/shard_map/ppermute | solution.py:355
  68.1 2.2 %collective-permute-done.9 = f32[64,256]{1,0:T(8,128)S(1)} collective-permute-done((f32[64,256]{1,0:T(8,128)S(1)}, f32[64,256]{1,0:T(8,128)S(1)}, u32[]{:S(2)}, u32[]{:S(2)}) %collective-permute-start.9) | collective-permute-done | bytes 65568 | tf_op jit(solution)/shard_map/ppermute | solution.py:355
  70.3 1.4 %collective-permute-start.10 = (f32[64,256]{1,0:T(8,128)S(1)}, f32[64,256]{1,0:T(8,128)S(1)}, u32[]{:S(2)}, u32[]{:S(2)}) collective-permute-start(f32[64,256]{1,0:T(8,128)S(1)} %add.11.own_ref), channel_id=1, source_target_pairs={{0,2},{1,3},{2,0},{3,1},{4,6},{5,7},{6,4},{7,5},{8,10},{9,11},{10,... | collective-permute-start | bytes 196616 | tf_op jit(solution)/shard_map/ppermute | solution.py:355
  71.7 3.0 %collective-permute-done.10.far_ref = f32[64,256]{1,0:T(8,128)S(1)} collective-permute-done((f32[64,256]{1,0:T(8,128)S(1)}, f32[64,256]{1,0:T(8,128)S(1)}, u32[]{:S(2)}, u32[]{:S(2)}) %collective-permute-start.10) | collective-permute-done | bytes 65568 | tf_op jit(solution)/shard_map/ppermute | solution.py:355
  74.7 1.2 %collective-permute-done.12.both_ref = f32[64,256]{1,0:T(8,128)S(1)} collective-permute-done((f32[64,256]{1,0:T(8,128)S(1)}, f32[64,256]{1,0:T(8,128)S(1)}, u32[]{:S(2)}, u32[]{:S(2)}) %collective-permute-start.12) | collective-permute-done | bytes 65568 | tf_op jit(solution)/shard_map/ppermute | solution.py:355
  75.9 0.7 join.1
  (10 shorter events, 0.1 us)
Async XLA Ops:
  0.6 33.8 %copy-start = (f32[256,64]{0,1:T(8,128)S(1)}, f32[256,64]{0,1:T(8,128)}, u32[]{:S(2)}) copy-start(f32[256,64]{0,1:T(8,128)} %param.9) | copy-start | bytes 196612
  21.4 1.8 %collective-permute-start = (f32[320,256]{1,0:T(8,128)S(1)}, f32[320,256]{1,0:T(8,128)S(1)}, u32[]{:S(2)}, u32[]{:S(2)}) collective-permute-start(f32[320,256]{1,0:T(8,128)S(1)} %get-tuple-element.19.own_ref), channel_id=1, source_target_pairs={{0,1},{1,0},{2,3},{3,2},{4,5},{5,4},{6,7},{7,6},{8,9},{9,8},{10,11... | collective-permute-start | bytes 983048 | tf_op jit(solution)/shard_map/ppermute | solution.py:355
  23.4 11.0 %collective-permute-start.1 = (f32[320,256]{1,0:T(8,128)S(1)}, f32[320,256]{1,0:T(8,128)S(1)}, u32[]{:S(2)}, u32[]{:S(2)}) collective-permute-start(f32[320,256]{1,0:T(8,128)S(1)} %merge.1.own_ref), channel_id=1, source_target_pairs={{0,2},{1,3},{2,0},{3,1},{4,6},{5,7},{6,4},{7,5},{8,10},{9,11},{10,... | collective-permute-start | bytes 983048 | tf_op jit(solution)/shard_map/ppermute | solution.py:355
  34.9 11.8 %collective-permute-start.5 = (f32[320,256]{1,0:T(8,128)S(1)}, f32[320,256]{1,0:T(8,128)S(1)}, u32[]{:S(2)}, u32[]{:S(2)}) collective-permute-start(f32[320,256]{1,0:T(8,128)S(1)} %get-tuple-element.21.map_ref), channel_id=1, source_target_pairs={{4,0},{5,1},{6,2},{7,3},{20,16},{21,17},{22,18},{23,19}} | collective-permute-start | bytes 983048 | tf_op jit(solution)/shard_map/ppermute | solution.py:380
  36.2 0.7 collective-permute-start.2
  37.1 11.2 %collective-permute-start.4 = (f32[64,256]{1,0:T(8,128)S(1)}, f32[64,256]{1,0:T(8,128)S(1)}, u32[]{:S(2)}, u32[]{:S(2)}) collective-permute-start(f32[64,256]{1,0:T(8,128)S(1)} %top.1), channel_id=1, source_target_pairs={{8,0},{9,1},{10,2},{11,3},{24,16},{25,17},{26,18},{27,19}} | collective-permute-start | bytes 196616 | tf_op jit(solution)/shard_map/ppermute | solution.py:383
  38.4 9.9 %collective-permute-start.3 = (f32[64,256]{1,0:T(8,128)S(1)}, f32[64,256]{1,0:T(8,128)S(1)}, u32[]{:S(2)}, u32[]{:S(2)}) collective-permute-start(f32[64,256]{1,0:T(8,128)S(1)} %top.1), channel_id=1, source_target_pairs={{8,4},{9,5},{10,6},{11,7},{24,20},{25,21},{26,22},{27,23}} | collective-permute-start | bytes 196616 | tf_op jit(solution)/shard_map/ppermute | solution.py:382
  54.8 1.4 %collective-permute-start.6 = (f32[128,256]{1,0:T(8,128)S(1)}, f32[128,256]{1,0:T(8,128)S(1)}, u32[]{:S(2)}, u32[]{:S(2)}) collective-permute-start(f32[128,256]{1,0:T(8,128)S(1)} %get-tuple-element.33), channel_id=1, source_target_pairs={{0,1},{1,0},{2,3},{3,2},{4,5},{5,4},{6,7},{7,6},{8,9},{9,8},{10,11... | collective-permute-start | bytes 393224 | tf_op jit(solution)/shard_map/ppermute | solution.py:355
  56.2 4.3 %collective-permute-start.7 = (f32[64,256]{1,0:T(8,128)S(1)}, f32[64,256]{1,0:T(8,128)S(1)}, u32[]{:S(2)}, u32[]{:S(2)}) collective-permute-start(f32[64,256]{1,0:T(8,128)S(1)} %get-tuple-element.35), channel_id=1, source_target_pairs={{0,2},{1,3},{2,0},{3,1},{4,6},{5,7},{6,4},{7,5},{8,10},{9,11},{10,... | collective-permute-start | bytes 196616 | tf_op jit(solution)/shard_map/ppermute | solution.py:355
  60.5 4.3 %collective-permute-start.8 = (f32[64,256]{1,0:T(8,128)S(1)}, f32[64,256]{1,0:T(8,128)S(1)}, u32[]{:S(2)}, u32[]{:S(2)}) collective-permute-start(f32[64,256]{1,0:T(8,128)S(1)} %add.9), channel_id=1, source_target_pairs={{0,4},{1,5},{2,6},{3,7},{4,0},{5,1},{6,2},{7,3},{8,12},{9,13},{10,... | collective-permute-start | bytes 196616 | tf_op jit(solution)/shard_map/ppermute | solution.py:355
  64.9 5.4 %collective-permute-start.9 = (f32[64,256]{1,0:T(8,128)S(1)}, f32[64,256]{1,0:T(8,128)S(1)}, u32[]{:S(2)}, u32[]{:S(2)}) collective-permute-start(f32[64,256]{1,0:T(8,128)S(1)} %add.10), channel_id=1, source_target_pairs={{0,8},{1,9},{2,10},{3,11},{4,12},{5,13},{6,14},{7,15},{8,0},{9,1},... | collective-permute-start | bytes 196616 | tf_op jit(solution)/shard_map/ppermute | solution.py:355
  70.3 4.3 %collective-permute-start.10 = (f32[64,256]{1,0:T(8,128)S(1)}, f32[64,256]{1,0:T(8,128)S(1)}, u32[]{:S(2)}, u32[]{:S(2)}) collective-permute-start(f32[64,256]{1,0:T(8,128)S(1)} %add.11.own_ref), channel_id=1, source_target_pairs={{0,2},{1,3},{2,0},{3,1},{4,6},{5,7},{6,4},{7,5},{8,10},{9,11},{10,... | collective-permute-start | bytes 196616 | tf_op jit(solution)/shard_map/ppermute | solution.py:355
  71.7 3.0 %collective-permute-start.11 = (f32[64,256]{1,0:T(8,128)S(1)}, f32[64,256]{1,0:T(8,128)S(1)}, u32[]{:S(2)}, u32[]{:S(2)}) collective-permute-start(f32[64,256]{1,0:T(8,128)S(1)} %add.11.own_ref), channel_id=1, source_target_pairs={{0,1},{1,0},{2,3},{3,2},{4,5},{5,4},{6,7},{7,6},{8,9},{9,8},{10,11... | collective-permute-start | bytes 196616 | tf_op jit(solution)/shard_map/ppermute | solution.py:355
  74.7 1.3 %collective-permute-start.12 = (f32[64,256]{1,0:T(8,128)S(1)}, f32[64,256]{1,0:T(8,128)S(1)}, u32[]{:S(2)}, u32[]{:S(2)}) collective-permute-start(f32[64,256]{1,0:T(8,128)S(1)} %collective-permute-done.10.far_ref), channel_id=1, source_target_pairs={{0,1},{1,0},{2,3},{3,2},{4,5},{5,4},{6,7},{7,6},{8,9},{9,8},{10,11... | collective-permute-start | bytes 196616 | tf_op jit(solution)/shard_map/ppermute | solution.py:355

commit v3 on v2

--- a/solution.py
+++ b/solution.py
@@ -109,7 +109,7 @@
     map_ref[...] = acc
 
 
-def marks_kernel(raw_ref, suffix_ref, in_hbm, zh_ref, zl_ref, zu_ref, flip_ref, in_ref, sem):
+def marks_kernel(raw_ref, suffix_ref, in_hbm, _, zh_ref, zl_ref, zu_ref, flip_ref, __, in_ref, sem):
     fetch = pltpu.make_async_copy(in_hbm, in_ref, sem)
     fetch.start()
     count, rows, width = raw_ref.shape
@@ -134,7 +134,19 @@
     return (lax.axis_index("tm") & bit) == 0
 
 
-def merge_kernel(bit, own_ref, other_ref, out_ref):
+def core_half(x):
+    half = x.shape[0] // 2
+    return jnp.where(early(1), x[:half], x[half:])
+
+
+def place_halves(mine, other, out_ref):
+    half = mine.shape[0]
+    start = pl.multiple_of((lax.axis_index("tm") & 1) * half, half)
+    out_ref[pl.ds(start, half), :] = mine
+    out_ref[pl.ds(pl.multiple_of(half - start, half), half), :] = other
+
+
+def ordered(bit, own_ref, other_ref, out_ref):
     width = own_ref.shape[1]
     first = early(bit)
 
@@ -147,27 +159,57 @@
         out_ref[...] = compose(own_ref[...], other_ref[...], width)
 
 
-def end_kernel(bit, own_ref, other_ref, vec_ref, out_ref, through_ref):
-    merge_kernel(bit, own_ref, other_ref, out_ref)
-    through_ref[...] = apply(vec_ref[...], out_ref[...], own_ref.shape[1])
-
-
-def apply_kernel(vec_ref, map_ref, out_ref):
-    out_ref[...] = apply(vec_ref[...], map_ref[...], map_ref.shape[1])
-
-
-def later_kernel(quarter, other_ref, later_ref, out_ref):
-    bit, only = quarter
-    width = other_ref.shape[1]
-    first = lax.axis_index("tm") < only if only else early(bit)
-
-    @pl.when(first)
-    def _():
-        out_ref[...] = compose(other_ref[...], later_ref[...], width)
-
-    @pl.when(jnp.logical_not(first))
-    def _():
-        out_ref[...] = later_ref[...]
+def pair_kernel(own_ref, other_ref, out_ref, half_ref):
+    ordered(1, own_ref, other_ref, out_ref)
+    half_ref[...] = core_half(out_ref[...])
+
+
+def position(low_bit, count):
+    return (lax.axis_index("tm") // low_bit) % count
+
+
+def group_maps(own_ref, halves, maps):
+    maps[0] = own_ref[...]
+    for mask in range(1, maps.shape[0]):
+        place_halves(halves[2 * mask - 2][...], halves[2 * mask - 1][...], maps.at[mask])
+
+
+def top_kernel(low_bit, own_ref, vec_ref, *rest):
+    halves, (out_ref, maps) = rest[:-2], rest[-2:]
+    group_maps(own_ref, halves, maps)
+    count, _, width = maps.shape
+    here = position(low_bit, count)
+    vec = vec_ref[...]
+    for at in range(count - 1, -1, -1):
+        vec = apply(vec, maps[at ^ here], width)
+    out_ref[...] = vec
+
+
+def total_kernel(low_bit, own_ref, *rest):
+    halves, (out_ref, half_ref, maps) = rest[:-3], rest[-3:]
+    group_maps(own_ref, halves, maps)
+    count, _, width = maps.shape
+    here = position(low_bit, count)
+    acc = maps[(count - 1) ^ here]
+    for at in range(count - 2, -1, -1):
+        acc = compose(acc, maps[at ^ here], width)
+    out_ref[...] = acc
+    half_ref[...] = core_half(acc)
+
+
+def later_kernel(low_bit, later_ref, *rest):
+    halves, (out_ref, maps) = rest[:-2], rest[-2:]
+    count, _, width = maps.shape
+    for mask in range(1, count):
+        place_halves(halves[2 * mask - 2][...], halves[2 * mask - 1][...], maps.at[mask])
+    here = position(low_bit, count)
+    maps[0] = later_ref[...]
+    out_ref[...] = maps[jnp.where(here == count - 1, 0, (count - 1) ^ here)]
+    for at in range(count - 2, -1, -1):
+
+        @pl.when(at >= here)
+        def _():
+            out_ref[...] = compose(out_ref[...], maps[at ^ here], width)
 
 
 def first_later_kernel(bit, other_ref, out_ref):
@@ -186,16 +228,13 @@
 
 
 def sweep_kernel(
-    part, end_ref, got_ref, up_ref, down_ref, later_ref, zh_ref, zl_ref, zu_ref,
+    bit, end_ref, got_ref, later_ref, zh_ref, zl_ref, zu_ref,
     rot_ref, d_ref, f_ref, flip_ref,
     adj_hbm, keep_ref, give_ref, cur, low_ref, sems,
 ):
     count, width = zh_ref.shape[0], zh_ref.shape[1]
     cols = end_ref.shape[0]
-    place = lax.axis_index("tm") // part
-    v = jnp.where(place == 3, end_ref[...], got_ref[...])
-    v = jnp.where(place == 1, up_ref[...], v)
-    v = jnp.where(place == 0, down_ref[...], v)
+    v = jnp.where(early(bit), got_ref[...], end_ref[...])
     v = apply(v, later_ref[...], width)
     v_high, v_low = split(v)
 
@@ -257,7 +296,7 @@
 VM = pltpu.VMEM
 
 
-def call(kernel, name, out, *args, where=None, scratch=(), flops=0, data=0):
+def call(kernel, name, out, *args, where=None, scratch=(), flops=0, data=0, alias=None):
     where = where or {}
     ins = [pl.BlockSpec(memory_space=pl.ANY if i in where else VM) for i in range(len(args))]
     args = [pltpu.with_memory_space_constraint(a, pltpu.HBM if i in where else VM) for i, a in enumerate(args)]
@@ -271,6 +310,7 @@
         in_specs=ins,
         out_specs=outs,
         scratch_shapes=list(scratch),
+        input_output_aliases=alias or {},
         compiler_params=pltpu.CompilerParams(vmem_limit_bytes=VMEM_LIMIT),
         cost_estimate=pl.CostEstimate(flops=flops, bytes_accessed=data, transcendentals=0),
         name=name,
@@ -301,7 +341,7 @@
     )
 
 
-def mark_maps(raw, suffix, ins):
+def mark_maps(raw, suffix, ins, through):
     count, rows, width = raw.shape
     steps, cols, feats = ins.shape
     return call(
@@ -312,10 +352,13 @@
             VM((count, width, width), BF16),
             VM((count, rows - width, width), F32),
             VM((SEG, feats, steps // SEG * cols), BF16),
+            VM(through.shape, F32),
         ),
         raw,
         suffix,
         ins,
+        through,
+        alias={3: 4},
         where={2},
         scratch=[VM(ins.shape, BF16), pltpu.SemaphoreType.DMA],
         flops=6 * count * rows * width * width,
@@ -328,7 +371,7 @@
     feats = flipped.shape[1]
     segs = steps // SEG
     adj, keep, give = call(
-        functools.partial(sweep_kernel, lax.axis_size("tm") // 4),
+        functools.partial(sweep_kernel, lax.axis_size("tm") // 2),
         "sweep",
         (
             shape((segs, SEG, cols, width), BF16),
@@ -355,34 +398,40 @@
     return lax.ppermute(x, "tm", [(i, i ^ bit) for i in range(n)])
 
 
-def incoming(own, end):
+def incoming(own, end, aside):
     n = lax.axis_size("tm")
-    part = n // 4
     rows, width = own.shape
     flops = 6 * rows * width * width
     vec = VM(end.shape, F32)
     whole = VM(own.shape, F32)
-    total, later, bit = own, None, 1
-    while bit < part:
-        other = swap(total, bit)
-        if later is None:
-            (later,) = call(functools.partial(first_later_kernel, bit), "later", (whole,), other)
+    half = VM((rows // 2, width), F32)
+    other = swap(own, 1)
+    total, piece = call(pair_kernel, "pair", (whole, half), own, other, flops=flops)
+    (later,) = call(functools.partial(first_later_kernel, 1), "later", (whole,), other)
+    bit = 2
+    while bit < n // 2:
+        count = 4 if 4 * bit <= n // 2 else 2
+        mine = [swap(piece, mask * bit) for mask in range(1, count)]
+        if bit == 2:
+            *marks, mine[0] = aside(mine[0])
+        halves = [x for got in mine for x in (got, swap(got, 1))]
+        maps = [VM((count, rows, width), F32)]
+        if count * bit < n // 2:
+            total, piece = call(
+                functools.partial(total_kernel, bit), "total", (whole, half), total, *halves,
+                scratch=maps, flops=count * flops,
+            )
         else:
-            (later,) = call(functools.partial(later_kernel, (bit, 0)), "later", (whole,), other, later, flops=flops)
-        if 2 * bit < part:
-            (total,) = call(functools.partial(merge_kernel, bit), "merge", (whole,), total, other, flops=flops)
-        else:
-            total, last = call(
-                functools.partial(end_kernel, bit), "end", (whole, vec), total, other, end, flops=flops
+            (top,) = call(
+                functools.partial(top_kernel, bit), "top", (vec,), total, end, *halves,
+                scratch=maps, flops=count * flops // 5,
             )
-        bit *= 2
-    got = lax.ppermute(last, "tm", [(i + 3 * part, i + 2 * part) for i in range(part)])
-    second = lax.ppermute(total, "tm", [(i + part, i) for i in range(part)])
-    (top,) = call(apply_kernel, "top", (vec,), got, total, flops=flops // 5)
-    up = lax.ppermute(top, "tm", [(i + 2 * part, i + part) for i in range(part)])
-    down = lax.ppermute(top, "tm", [(i + 2 * part, i) for i in range(part)])
-    (later,) = call(functools.partial(later_kernel, (0, part)), "later", (whole,), second, later, flops=flops)
-    return (end, got, up, down), later
+        (later,) = call(
+            functools.partial(later_kernel, bit), "later", (whole,), later, *halves,
+            scratch=maps, flops=count * flops,
+        )
+        bit *= count
+    return marks, (end, swap(top, n // 2)), later
 
 
 def all_sum(keep, give):
@@ -406,8 +455,7 @@
     ins = jnp.transpose(inputs, (0, 2, 1))
     end = terminal.T
     own, raw, suffix, rot, derivs, force = build(generator, derivs, force)
-    zh, zl, zu, flipped = mark_maps(raw, suffix, ins)
-    entering, later = incoming(own, end)
+    (zh, zl, zu, flipped), entering, later = incoming(own, end, functools.partial(mark_maps, raw, suffix, ins))
     adj, keep, give = sweep(entering, later, zh, zl, zu, rot, derivs, force, flipped)
     return jnp.transpose(adj, (0, 2, 1)), all_sum(keep, give)
 

time: 76.9 us -> 73.8 us (0.960)
  waiting for transfers between devices: 27.1 us -> 24.2 us
  starting transfers between devices: 15.7 us -> 14.8 us
  Pallas kernels: 33 us -> 33.8 us
    ppermute x4 -> x0, waiting for transfers between devices: 4.94 us -> none  [the longest x1 3.71 us: incoming(): second = lax.ppermute(total, 'tm', [(i + part, i) for i in range(part)])]
    ppermute x4 -> x0, starting transfers between devices: 4.1 us -> none  [the longest x1 1.3 us: incoming(): down = lax.ppermute(top, 'tm', [(i + 2 * part, i) for i in range(part)])]
    ppermute x9 -> x15, starting transfers between devices: 11.6 us -> 14.8 us  [swap(): return lax.ppermute(x, 'tm', [(i, i ^ bit) for i in range(n)])]
    ppermute x9 -> x15, waiting for transfers between devices: 22.2 us -> 24.2 us  [swap(): return lax.ppermute(x, 'tm', [(i, i ^ bit) for i in range(n)])]
    pallas_call x11 -> x9, Pallas kernels: 33 us -> 33.8 us  [call(): pl.pallas_call(kernel, out_shape=tuple(out), in_specs=ins, out_specs=outs...]
  transfers between devices with their start and end apart: 13 -> 15, of which waited for: 10 -> 13; matrix products, arithmetic and copies ran while one was open for 0% -> 0% of each run, Pallas kernels for 6% -> 6%
where the time goes in v3:
time: 73.8 us; the launch traced here: 73.6 us
  Pallas kernels  33.8 us (46%)
  waiting for transfers between devices  24.2 us (33%)
  starting transfers between devices  14.8 us (20%)
  between operations  0.74 us (1%)
    pallas_call x9, Pallas kernels, call(): pl.pallas_call(kernel, out_shape=tuple(out), in_specs=ins, out_specs=outs...  33.8 us
    ppermute x15, waiting for transfers between devices, swap(): return lax.ppermute(x, 'tm', [(i, i ^ bit) for i in range(n)])  24.2 us
    ppermute x15, starting transfers between devices, swap(): return lax.ppermute(x, 'tm', [(i, i ^ bit) for i in range(n)])  14.8 us
  transfers between devices with their start and end apart: 15, of which 13 were waited for; matrix products, arithmetic and copies ran while one was open for 0% of the time, Pallas kernels for 6%

profile of v3, /device:TPU:0, one launch (start us, length us, event | category | flops | bytes accessed | tf_op | source)
XLA Modules:
  0.0 73.6 jit_solution(3641280756789598529)
XLA Ops:
  0.6 20.7 %build.1 = (f32[320,256]{1,0:T(8,128)S(1)}, f32[16,320,256]{2,1,0:T(8,128)S(1)}, f32[3,320,256]{2,1,0:T(8,128)S(1)}, bf16[2,256,256]{2,1,0:T(8,128)(2,1)S(1)}, f...) custom-call(f32[256,256]{1,0:T(8,128)} %gen_hbm.1, f32[128,256]{1,0:T(8,128)} %d_hbm.1, bf16[128,64,256]{2,1,0:T(8,128)(2,1)} %bitcast.9), custom_call_target="tpu_custom_call" | custom-call | flops 16106127360 | tf_op jit(solution)/shard_map/build/pallas_call | solution.py:307
  21.3 0.5 collective-permute-start
  21.8 1.3 %collective-permute-done.other_ref = f32[320,256]{1,0:T(8,128)S(1)} collective-permute-done((f32[320,256]{1,0:T(8,128)S(1)}, f32[320,256]{1,0:T(8,128)S(1)}, u32[]{:S(2)}, u32[]{:S(2)}) %collective-permute-start) | collective-permute-done | bytes 327712 | tf_op jit(solution)/shard_map/ppermute | solution.py:398
  23.1 0.5 pair.1
  23.6 3.0 %collective-permute-start.1 = (f32[160,256]{1,0:T(8,128)S(1)}, f32[160,256]{1,0:T(8,128)S(1)}, u32[]{:S(2)}, u32[]{:S(2)}) collective-permute-start(f32[160,256]{1,0:T(8,128)S(1)} %get-tuple-element.24), channel_id=1, source_target_pairs={{0,2},{1,3},{2,0},{3,1},{4,6},{5,7},{6,4},{7,5},{8,10},{9,11},{10,... | collective-permute-start | bytes 491528 | tf_op jit(solution)/shard_map/ppermute | solution.py:398
  26.5 1.6 %collective-permute-start.3 = (f32[160,256]{1,0:T(8,128)S(1)}, f32[160,256]{1,0:T(8,128)S(1)}, u32[]{:S(2)}, u32[]{:S(2)}) collective-permute-start(f32[160,256]{1,0:T(8,128)S(1)} %get-tuple-element.24), channel_id=1, source_target_pairs={{0,4},{1,5},{2,6},{3,7},{4,0},{5,1},{6,2},{7,3},{8,12},{9,13},{10,... | collective-permute-start | bytes 491528 | tf_op jit(solution)/shard_map/ppermute | solution.py:398
  28.1 2.9 %collective-permute-done.1._ = f32[160,256]{1,0:T(8,128)S(1)} collective-permute-done((f32[160,256]{1,0:T(8,128)S(1)}, f32[160,256]{1,0:T(8,128)S(1)}, u32[]{:S(2)}, u32[]{:S(2)}) %collective-permute-start.1) | collective-permute-done | bytes 163872 | tf_op jit(solution)/shard_map/ppermute | solution.py:398
  31.0 3.4 %marks.1 = (bf16[16,256,256]{2,1,0:T(8,128)(2,1)S(1)}, bf16[16,256,256]{2,1,0:T(8,128)(2,1)S(1)}, f32[16,64,256]{2,1,0:T(8,128)S(1)}, bf16[8,256,1024]{2,1,0:T(8,128)(2,1)S(1)}, f32[160,256]{1,0:T(8,128)S(1)}) custom-call(f32[16,320,256]{2,1,0:T(8,128)S(1)} %get-tuple-element.22.raw_ref, ...), custom_call_target="tpu_custom_call", output_to_operand_aliasing={{4}: (3, {})} | custom-call | flops 2013265920 | bytes 15000000 | tf_op jit(solution)/shard_map/marks/pallas_call | solution.py:307
  34.5 0.1 collective-permute-start.2
  34.6 0.0 collective-permute-done.3.rest_2_
  34.6 0.5 collective-permute-start.4
  35.1 0.7 collective-permute-done.5.rest_4_
  35.8 0.1 collective-permute-done.2.rest_1_
  36.0 0.2 collective-permute-done.4.rest_3_
  36.2 1.0 %collective-permute-done.6.rest_5_ = f32[160,256]{1,0:T(8,128)S(1)} collective-permute-done((f32[160,256]{1,0:T(8,128)S(1)}, f32[160,256]{1,0:T(8,128)S(1)}, u32[]{:S(2)}, u32[]{:S(2)}) %collective-permute-start.6) | collective-permute-done | bytes 163872 | tf_op jit(solution)/shard_map/ppermute | solution.py:398
  37.2 0.9 %top.1 = f32[64,256]{1,0:T(8,128)S(1)} custom-call(f32[320,256]{1,0:T(8,128)S(1)} %get-tuple-element.21.own_ref, f32[64,256]{1,0:T(8,128)S(1)} %bitcast.6, f32[160,256]{1,0:T(8,128)S(1)} %get-tuple-element.25.rest_0_, f32[160,256]{1,0:T(8,128)S(1)} %collective-permute-done.2.rest_1_, f32[160,256]{1,0:T(8,128)S(1)} %collective-permute-done.3.rest_2_, ...), custom_call_target="tpu_custom_call" | custom-call | flops 100663296 | tf_op jit(solution)/shard_map/top/pallas_call | solution.py:307
  38.1 2.8 %collective-permute-start.7 = (f32[64,256]{1,0:T(8,128)S(1)}, f32[64,256]{1,0:T(8,128)S(1)}, u32[]{:S(2)}, u32[]{:S(2)}) collective-permute-start(f32[64,256]{1,0:T(8,128)S(1)} %top.1), channel_id=1, source_target_pairs={{0,8},{1,9},{2,10},{3,11},{4,12},{5,13},{6,14},{7,15},{8,0},{9,1},... | collective-permute-start | bytes 196616 | tf_op jit(solution)/shard_map/ppermute | solution.py:398
  40.9 1.0 %later.3.later_ref = f32[320,256]{1,0:T(8,128)S(1)} custom-call(f32[320,256]{1,0:T(8,128)S(1)} %later.2.later_ref, f32[160,256]{1,0:T(8,128)S(1)} %get-tuple-element.25.rest_0_, f32[160,256]{1,0:T(8,128)S(1)} %collective-permute-done.2.rest_1_, f32[160,256]{1,0:T(8,128)S(1)} %collective-permute-done.3.rest_2_, ...), custom_call_target="tpu_custom_call" | custom-call | flops 503316480 | tf_op jit(solution)/shard_map/later/pallas_call | solution.py:307
  42.0 2.8 %collective-permute-done.7.got_ref = f32[64,256]{1,0:T(8,128)S(1)} collective-permute-done((f32[64,256]{1,0:T(8,128)S(1)}, f32[64,256]{1,0:T(8,128)S(1)}, u32[]{:S(2)}, u32[]{:S(2)}) %collective-permute-start.7) | collective-permute-done | bytes 65568 | tf_op jit(solution)/shard_map/ppermute | solution.py:398
  44.8 6.5 %sweep.1 = (bf16[16,8,64,256]{3,2,1,0:T(8,128)(2,1)}, f32[128,256]{1,0:T(8,128)S(1)}, f32[128,256]{1,0:T(8,128)S(1)}) custom-call(f32[64,256]{1,0:T(8,128)S(1)} %bitcast.7, f32[64,256]{1,0:T(8,128)S(1)} %collective-permute-done.7.got_ref, f32[320,256]{1,0:T(8,128)S(1)} %later.3.later_ref, bf16[16,256,256]{2,1,0:T(8,128)(2,1)S(1)} %get-tuple-element.26.zh_ref, ...), custom_call_target="tpu_custom_call" | custom-call | flops 4294967296 | tf_op jit(solution)/shard_map/sweep/pallas_call | solution.py:307
  51.3 0.1 collective-permute-start.8
  51.3 1.3 %collective-permute-done.8.got_ref = f32[128,256]{1,0:T(8,128)S(1)} collective-permute-done((f32[128,256]{1,0:T(8,128)S(1)}, f32[128,256]{1,0:T(8,128)S(1)}, u32[]{:S(2)}, u32[]{:S(2)}) %collective-permute-start.8) | collective-permute-done | bytes 131104 | tf_op jit(solution)/shard_map/ppermute | solution.py:398
  52.7 1.7 %collective-permute-start.9 = (f32[64,256]{1,0:T(8,128)S(1)}, f32[64,256]{1,0:T(8,128)S(1)}, u32[]{:S(2)}, u32[]{:S(2)}) collective-permute-start(f32[64,256]{1,0:T(8,128)S(1)} %get-tuple-element.37), channel_id=1, source_target_pairs={{0,2},{1,3},{2,0},{3,1},{4,6},{5,7},{6,4},{7,5},{8,10},{9,11},{10,... | collective-permute-start | bytes 196616 | tf_op jit(solution)/shard_map/ppermute | solution.py:398
  54.4 2.6 %collective-permute-done.9 = f32[64,256]{1,0:T(8,128)S(1)} collective-permute-done((f32[64,256]{1,0:T(8,128)S(1)}, f32[64,256]{1,0:T(8,128)S(1)}, u32[]{:S(2)}, u32[]{:S(2)}) %collective-permute-start.9) | collective-permute-done | bytes 65568 | tf_op jit(solution)/shard_map/ppermute | solution.py:398
  57.0 0.8 %collective-permute-start.10 = (f32[64,256]{1,0:T(8,128)S(1)}, f32[64,256]{1,0:T(8,128)S(1)}, u32[]{:S(2)}, u32[]{:S(2)}) collective-permute-start(f32[64,256]{1,0:T(8,128)S(1)} %add.9), channel_id=1, source_target_pairs={{0,4},{1,5},{2,6},{3,7},{4,0},{5,1},{6,2},{7,3},{8,12},{9,13},{10,... | collective-permute-start | bytes 196616 | tf_op jit(solution)/shard_map/ppermute | solution.py:398
  57.8 3.6 %collective-permute-done.10 = f32[64,256]{1,0:T(8,128)S(1)} collective-permute-done((f32[64,256]{1,0:T(8,128)S(1)}, f32[64,256]{1,0:T(8,128)S(1)}, u32[]{:S(2)}, u32[]{:S(2)}) %collective-permute-start.10) | collective-permute-done | bytes 65568 | tf_op jit(solution)/shard_map/ppermute | solution.py:398
  61.4 2.1 %collective-permute-start.11 = (f32[64,256]{1,0:T(8,128)S(1)}, f32[64,256]{1,0:T(8,128)S(1)}, u32[]{:S(2)}, u32[]{:S(2)}) collective-permute-start(f32[64,256]{1,0:T(8,128)S(1)} %add.10), channel_id=1, source_target_pairs={{0,8},{1,9},{2,10},{3,11},{4,12},{5,13},{6,14},{7,15},{8,0},{9,1},... | collective-permute-start | bytes 196616 | tf_op jit(solution)/shard_map/ppermute | solution.py:398
  63.5 3.8 %collective-permute-done.11 = f32[64,256]{1,0:T(8,128)S(1)} collective-permute-done((f32[64,256]{1,0:T(8,128)S(1)}, f32[64,256]{1,0:T(8,128)S(1)}, u32[]{:S(2)}, u32[]{:S(2)}) %collective-permute-start.11) | collective-permute-done | bytes 65568 | tf_op jit(solution)/shard_map/ppermute | solution.py:398
  67.3 1.7 %collective-permute-start.12 = (f32[64,256]{1,0:T(8,128)S(1)}, f32[64,256]{1,0:T(8,128)S(1)}, u32[]{:S(2)}, u32[]{:S(2)}) collective-permute-start(f32[64,256]{1,0:T(8,128)S(1)} %add.11.own_ref), channel_id=1, source_target_pairs={{0,2},{1,3},{2,0},{3,1},{4,6},{5,7},{6,4},{7,5},{8,10},{9,11},{10,... | collective-permute-start | bytes 196616 | tf_op jit(solution)/shard_map/ppermute | solution.py:398
  69.1 2.6 %collective-permute-done.12.far_ref = f32[64,256]{1,0:T(8,128)S(1)} collective-permute-done((f32[64,256]{1,0:T(8,128)S(1)}, f32[64,256]{1,0:T(8,128)S(1)}, u32[]{:S(2)}, u32[]{:S(2)}) %collective-permute-start.12) | collective-permute-done | bytes 65568 | tf_op jit(solution)/shard_map/ppermute | solution.py:398
  71.7 1.2 %collective-permute-done.14.both_ref = f32[64,256]{1,0:T(8,128)S(1)} collective-permute-done((f32[64,256]{1,0:T(8,128)S(1)}, f32[64,256]{1,0:T(8,128)S(1)}, u32[]{:S(2)}, u32[]{:S(2)}) %collective-permute-start.14) | collective-permute-done | bytes 65568 | tf_op jit(solution)/shard_map/ppermute | solution.py:398
  72.9 0.7 join.1
  (12 shorter events, 0.1 us)
Async XLA Ops:
  21.3 1.8 %collective-permute-start = (f32[320,256]{1,0:T(8,128)S(1)}, f32[320,256]{1,0:T(8,128)S(1)}, u32[]{:S(2)}, u32[]{:S(2)}) collective-permute-start(f32[320,256]{1,0:T(8,128)S(1)} %get-tuple-element.20.own_ref), channel_id=1, source_target_pairs={{0,1},{1,0},{2,3},{3,2},{4,5},{5,4},{6,7},{7,6},{8,9},{9,8},{10,11... | collective-permute-start | bytes 983048 | tf_op jit(solution)/shard_map/ppermute | solution.py:398
  23.6 7.5 %collective-permute-start.1 = (f32[160,256]{1,0:T(8,128)S(1)}, f32[160,256]{1,0:T(8,128)S(1)}, u32[]{:S(2)}, u32[]{:S(2)}) collective-permute-start(f32[160,256]{1,0:T(8,128)S(1)} %get-tuple-element.24), channel_id=1, source_target_pairs={{0,2},{1,3},{2,0},{3,1},{4,6},{5,7},{6,4},{7,5},{8,10},{9,11},{10,... | collective-permute-start | bytes 491528 | tf_op jit(solution)/shard_map/ppermute | solution.py:398
  26.5 8.0 %collective-permute-start.3 = (f32[160,256]{1,0:T(8,128)S(1)}, f32[160,256]{1,0:T(8,128)S(1)}, u32[]{:S(2)}, u32[]{:S(2)}) collective-permute-start(f32[160,256]{1,0:T(8,128)S(1)} %get-tuple-element.24), channel_id=1, source_target_pairs={{0,4},{1,5},{2,6},{3,7},{4,0},{5,1},{6,2},{7,3},{8,12},{9,13},{10,... | collective-permute-start | bytes 491528 | tf_op jit(solution)/shard_map/ppermute | solution.py:398
  28.1 7.7 %collective-permute-start.5 = (f32[160,256]{1,0:T(8,128)S(1)}, f32[160,256]{1,0:T(8,128)S(1)}, u32[]{:S(2)}, u32[]{:S(2)}) collective-permute-start(f32[160,256]{1,0:T(8,128)S(1)} %get-tuple-element.24), channel_id=1, source_target_pairs={{0,6},{1,7},{2,4},{3,5},{4,2},{5,3},{6,0},{7,1},{8,14},{9,15},{10,... | collective-permute-start | bytes 491528 | tf_op jit(solution)/shard_map/ppermute | solution.py:398
  31.0 6.2 %copy-start = (f32[256,64]{0,1:T(8,128)S(1)}, f32[256,64]{0,1:T(8,128)}, u32[]{:S(2)}) copy-start(f32[256,64]{0,1:T(8,128)} %param.9) | copy-start | bytes 196612
  34.5 1.5 %collective-permute-start.2 = (f32[160,256]{1,0:T(8,128)S(1)}, f32[160,256]{1,0:T(8,128)S(1)}, u32[]{:S(2)}, u32[]{:S(2)}) collective-permute-start(f32[160,256]{1,0:T(8,128)S(1)} %get-tuple-element.25.rest_0_), channel_id=1, source_target_pairs={{0,1},{1,0},{2,3},{3,2},{4,5},{5,4},{6,7},{7,6},{8,9},{9,8},{10,11... | collective-permute-start | bytes 491528 | tf_op jit(solution)/shard_map/ppermute | solution.py:398
  34.6 1.6 %collective-permute-start.4 = (f32[160,256]{1,0:T(8,128)S(1)}, f32[160,256]{1,0:T(8,128)S(1)}, u32[]{:S(2)}, u32[]{:S(2)}) collective-permute-start(f32[160,256]{1,0:T(8,128)S(1)} %collective-permute-done.3.rest_2_), channel_id=1, source_target_pairs={{0,1},{1,0},{2,3},{3,2},{4,5},{5,4},{6,7},{7,6},{8,9},{9,8},{10,11... | collective-permute-start | bytes 491528 | tf_op jit(solution)/shard_map/ppermute | solution.py:398
  35.8 1.4 %collective-permute-start.6 = (f32[160,256]{1,0:T(8,128)S(1)}, f32[160,256]{1,0:T(8,128)S(1)}, u32[]{:S(2)}, u32[]{:S(2)}) collective-permute-start(f32[160,256]{1,0:T(8,128)S(1)} %collective-permute-done.5.rest_4_), channel_id=1, source_target_pairs={{0,1},{1,0},{2,3},{3,2},{4,5},{5,4},{6,7},{7,6},{8,9},{9,8},{10,11... | collective-permute-start | bytes 491528 | tf_op jit(solution)/shard_map/ppermute | solution.py:398
  38.1 6.6 %collective-permute-start.7 = (f32[64,256]{1,0:T(8,128)S(1)}, f32[64,256]{1,0:T(8,128)S(1)}, u32[]{:S(2)}, u32[]{:S(2)}) collective-permute-start(f32[64,256]{1,0:T(8,128)S(1)} %top.1), channel_id=1, source_target_pairs={{0,8},{1,9},{2,10},{3,11},{4,12},{5,13},{6,14},{7,15},{8,0},{9,1},... | collective-permute-start | bytes 196616 | tf_op jit(solution)/shard_map/ppermute | solution.py:398
  51.3 1.4 %collective-permute-start.8 = (f32[128,256]{1,0:T(8,128)S(1)}, f32[128,256]{1,0:T(8,128)S(1)}, u32[]{:S(2)}, u32[]{:S(2)}) collective-permute-start(f32[128,256]{1,0:T(8,128)S(1)} %get-tuple-element.35), channel_id=1, source_target_pairs={{0,1},{1,0},{2,3},{3,2},{4,5},{5,4},{6,7},{7,6},{8,9},{9,8},{10,11... | collective-permute-start | bytes 393224 | tf_op jit(solution)/shard_map/ppermute | solution.py:398
  52.7 4.3 %collective-permute-start.9 = (f32[64,256]{1,0:T(8,128)S(1)}, f32[64,256]{1,0:T(8,128)S(1)}, u32[]{:S(2)}, u32[]{:S(2)}) collective-permute-start(f32[64,256]{1,0:T(8,128)S(1)} %get-tuple-element.37), channel_id=1, source_target_pairs={{0,2},{1,3},{2,0},{3,1},{4,6},{5,7},{6,4},{7,5},{8,10},{9,11},{10,... | collective-permute-start | bytes 196616 | tf_op jit(solution)/shard_map/ppermute | solution.py:398
  57.0 4.3 %collective-permute-start.10 = (f32[64,256]{1,0:T(8,128)S(1)}, f32[64,256]{1,0:T(8,128)S(1)}, u32[]{:S(2)}, u32[]{:S(2)}) collective-permute-start(f32[64,256]{1,0:T(8,128)S(1)} %add.9), channel_id=1, source_target_pairs={{0,4},{1,5},{2,6},{3,7},{4,0},{5,1},{6,2},{7,3},{8,12},{9,13},{10,... | collective-permute-start | bytes 196616 | tf_op jit(solution)/shard_map/ppermute | solution.py:398
  61.4 5.9 %collective-permute-start.11 = (f32[64,256]{1,0:T(8,128)S(1)}, f32[64,256]{1,0:T(8,128)S(1)}, u32[]{:S(2)}, u32[]{:S(2)}) collective-permute-start(f32[64,256]{1,0:T(8,128)S(1)} %add.10), channel_id=1, source_target_pairs={{0,8},{1,9},{2,10},{3,11},{4,12},{5,13},{6,14},{7,15},{8,0},{9,1},... | collective-permute-start | bytes 196616 | tf_op jit(solution)/shard_map/ppermute | solution.py:398
  67.3 4.3 %collective-permute-start.12 = (f32[64,256]{1,0:T(8,128)S(1)}, f32[64,256]{1,0:T(8,128)S(1)}, u32[]{:S(2)}, u32[]{:S(2)}) collective-permute-start(f32[64,256]{1,0:T(8,128)S(1)} %add.11.own_ref), channel_id=1, source_target_pairs={{0,2},{1,3},{2,0},{3,1},{4,6},{5,7},{6,4},{7,5},{8,10},{9,11},{10,... | collective-permute-start | bytes 196616 | tf_op jit(solution)/shard_map/ppermute | solution.py:398
  69.1 2.6 %collective-permute-start.13 = (f32[64,256]{1,0:T(8,128)S(1)}, f32[64,256]{1,0:T(8,128)S(1)}, u32[]{:S(2)}, u32[]{:S(2)}) collective-permute-start(f32[64,256]{1,0:T(8,128)S(1)} %add.11.own_ref), channel_id=1, source_target_pairs={{0,1},{1,0},{2,3},{3,2},{4,5},{5,4},{6,7},{7,6},{8,9},{9,8},{10,11... | collective-permute-start | bytes 196616 | tf_op jit(solution)/shard_map/ppermute | solution.py:398
  71.7 1.3 %collective-permute-start.14 = (f32[64,256]{1,0:T(8,128)S(1)}, f32[64,256]{1,0:T(8,128)S(1)}, u32[]{:S(2)}, u32[]{:S(2)}) collective-permute-start(f32[64,256]{1,0:T(8,128)S(1)} %collective-permute-done.12.far_ref), channel_id=1, source_target_pairs={{0,1},{1,0},{2,3},{3,2},{4,5},{5,4},{6,7},{7,6},{8,9},{9,8},{10,11... | collective-permute-start | bytes 196616 | tf_op jit(solution)/shard_map/ppermute | solution.py:398

commit v4 on v3

--- a/solution.py
+++ b/solution.py
@@ -59,7 +59,7 @@
     return mm3(vec, high, low) + through[width:]
 
 
-def build_kernel(gen_hbm, d_hbm, f_hbm, map_ref, raw_ref, suffix_ref, rot_ref, d_ref, f_ref, gen_ref, sems):
+def build_kernel(gen_hbm, d_hbm, f_hbm, map_ref, raw_ref, rot_ref, d_ref, f_ref, gen_ref, sems):
     steps, width = d_ref.shape
     per = steps // CHUNKS
     marks = per // SEG
@@ -102,27 +102,28 @@
         return 0
 
     lax.fori_loop(1, marks, more, 0)
-    acc = raw_ref[(CHUNKS - 1) * marks]
-    for g in range(CHUNKS - 2, -1, -1):
-        suffix_ref[g] = acc
-        acc = compose(acc, raw_ref[g * marks], width)
-    map_ref[...] = acc
-
-
-def marks_kernel(raw_ref, suffix_ref, in_hbm, _, zh_ref, zl_ref, zu_ref, flip_ref, __, in_ref, sem):
+    maps = [raw_ref[g * marks] for g in range(CHUNKS)]
+    while len(maps) > 1:
+        maps = [compose(maps[i + 1], maps[i], width) for i in range(0, len(maps), 2)]
+    map_ref[...] = maps[0]
+
+
+def marks_kernel(raw_ref, in_hbm, _, zh_ref, zl_ref, zu_ref, flip_ref, __, in_ref, sem):
     fetch = pltpu.make_async_copy(in_hbm, in_ref, sem)
     fetch.start()
     count, rows, width = raw_ref.shape
     marks = count // CHUNKS
-    for j in range(count):
-        g = j // marks
-        full = raw_ref[j]
-        if g < CHUNKS - 1:
-            full = compose(suffix_ref[g], full, width)
-        high, low = split(full[:width])
-        zh_ref[j] = high
-        zl_ref[j] = low
-        zu_ref[j] = full[width:]
+    suffix = None
+    for g in range(CHUNKS - 1, -1, -1):
+        for j in range((g + 1) * marks - 1, g * marks - 1, -1):
+            full = raw_ref[j]
+            if suffix is not None:
+                full = compose(suffix, full, width)
+            high, low = split(full[:width])
+            zh_ref[j] = high
+            zl_ref[j] = low
+            zu_ref[j] = full[width:]
+        suffix = full
     fetch.wait()
     segs = in_ref.shape[0] // SEG
     for s in range(SEG):
@@ -134,9 +135,9 @@
     return (lax.axis_index("tm") & bit) == 0
 
 
-def core_half(x):
-    half = x.shape[0] // 2
-    return jnp.where(early(1), x[:half], x[half:])
+def core_half(ref):
+    half = ref.shape[0] // 2
+    return ref[pl.ds(pl.multiple_of((lax.axis_index("tm") & 1) * half, half), half), :]
 
 
 def place_halves(mine, other, out_ref):
@@ -161,7 +162,7 @@
 
 def pair_kernel(own_ref, other_ref, out_ref, half_ref):
     ordered(1, own_ref, other_ref, out_ref)
-    half_ref[...] = core_half(out_ref[...])
+    half_ref[...] = core_half(out_ref)
 
 
 def position(low_bit, count):
@@ -194,7 +195,7 @@
     for at in range(count - 2, -1, -1):
         acc = compose(acc, maps[at ^ here], width)
     out_ref[...] = acc
-    half_ref[...] = core_half(acc)
+    half_ref[...] = core_half(out_ref)
 
 
 def later_kernel(low_bit, later_ref, *rest):
@@ -237,12 +238,14 @@
     v = jnp.where(early(bit), got_ref[...], end_ref[...])
     v = apply(v, later_ref[...], width)
     v_high, v_low = split(v)
+    v_both = jnp.concatenate([v_high, v_low], axis=0)
 
     def send(at):
         return pltpu.make_async_copy(low_ref.at[at], adj_hbm.at[:, at], sems.at[at])
 
     for j in range(count):
-        z = mm(v_high, zh_ref[j]) + mm(v_low, zh_ref[j]) + mm(v_high, zl_ref[j]) + zu_ref[j]
+        both = mm(v_both, zh_ref[j])
+        z = both[:cols] + both[cols:] + mm(v_high, zl_ref[j]) + zu_ref[j]
         if j > 0:
             cur[j - 1] = z
         low_ref[0, j] = z.astype(BF16)
@@ -280,10 +283,10 @@
     give_ref[...] = jnp.where(first, total[half:], total[:half])
 
 
-def join_kernel(own_ref, far_ref, core_ref, both_ref, out_ref):
+def join_kernel(bit, own_ref, far_ref, core_ref, both_ref, out_ref):
     rows = own_ref.shape[0]
     place = lax.axis_index("tm")
-    low, high = place & 1, (place // 2) & 1
+    low, high = place & 1, (place // bit) & 1
     for ref, a, b in (
         (own_ref, low, high),
         (far_ref, low, 1 - high),
@@ -327,7 +330,6 @@
         (
             VM((rows, width), F32),
             VM((steps // SEG, rows, width), F32),
-            VM((CHUNKS - 1, rows, width), F32),
             VM((2, width, width), BF16),
             VM(derivs.shape, F32),
             VM(force.shape, BF16),
@@ -341,7 +343,7 @@
     )
 
 
-def mark_maps(raw, suffix, ins, through):
+def mark_maps(raw, ins, through):
     count, rows, width = raw.shape
     steps, cols, feats = ins.shape
     return call(
@@ -355,11 +357,10 @@
             VM(through.shape, F32),
         ),
         raw,
-        suffix,
         ins,
         through,
-        alias={3: 4},
-        where={2},
+        alias={2: 4},
+        where={1},
         scratch=[VM(ins.shape, BF16), pltpu.SemaphoreType.DMA],
         flops=6 * count * rows * width * width,
         data=15_000_000,
@@ -436,17 +437,22 @@
 
 def all_sum(keep, give):
     n = lax.axis_size("tm")
+    near = 2
     quarter = VM((keep.shape[0] // 2, keep.shape[1]), F32)
-    mine, give = call(functools.partial(halve_kernel, 2), "halve", (quarter, quarter), keep, swap(give, 1))
-    x = mine + swap(give, 2)
-    bit = 4
+    x, give = call(functools.partial(halve_kernel, near), "halve", (quarter, quarter), keep, swap(give, 1))
+    x = x + swap(give, near)
+    bit = 2 * near
     while bit < n:
-        x = x + swap(x, bit)
-        bit *= 2
-    far = swap(x, 2)
+        count = 4 if 4 * bit <= n else 2
+        others = [swap(x, mask * bit) for mask in range(1, count)]
+        x = sum(others, x)
+        bit *= count
+    far = swap(x, near)
     core = swap(x, 1)
     both = swap(far, 1)
-    (out,) = call(join_kernel, "join", (shape((4 * x.shape[0], x.shape[1])),), x, far, core, both)
+    (out,) = call(
+        functools.partial(join_kernel, near), "join", (shape((4 * x.shape[0], x.shape[1])),), x, far, core, both
+    )
     return out
 
 
@@ -454,8 +460,8 @@
     force = jnp.transpose(forcing, (0, 2, 1))
     ins = jnp.transpose(inputs, (0, 2, 1))
     end = terminal.T
-    own, raw, suffix, rot, derivs, force = build(generator, derivs, force)
-    (zh, zl, zu, flipped), entering, later = incoming(own, end, functools.partial(mark_maps, raw, suffix, ins))
+    own, raw, rot, derivs, force = build(generator, derivs, force)
+    (zh, zl, zu, flipped), entering, later = incoming(own, end, functools.partial(mark_maps, raw, ins))
     adj, keep, give = sweep(entering, later, zh, zl, zu, rot, derivs, force, flipped)
     return jnp.transpose(adj, (0, 2, 1)), all_sum(keep, give)
 

time: 73.8 us -> 72 us (0.976)
  waiting for transfers between devices: 24.2 us -> 21.5 us
  starting transfers between devices: 14.8 us -> 16.4 us
    ppermute x15 -> x16, waiting for transfers between devices: 24.2 us -> 21.5 us  [swap(): return lax.ppermute(x, 'tm', [(i, i ^ bit) for i in range(n)])]
    ppermute x15 -> x16, starting transfers between devices: 14.8 us -> 16.4 us  [swap(): return lax.ppermute(x, 'tm', [(i, i ^ bit) for i in range(n)])]
  transfers between devices with their start and end apart: 15 -> 16, of which waited for: 13 -> 14; matrix products, arithmetic and copies ran while one was open for 0% -> 0% of each run, Pallas kernels for 6% -> 6%
where the time goes in v4:
time: 72 us; the launch traced here: 71.9 us
  Pallas kernels  33.2 us (46%)
  waiting for transfers between devices  21.5 us (30%)
  starting transfers between devices  16.4 us (23%)
  between operations  0.73 us (1%)
    pallas_call x9, Pallas kernels, call(): pl.pallas_call(kernel, out_shape=tuple(out), in_specs=ins, out_specs=outs...  33.2 us
    ppermute x16, waiting for transfers between devices, swap(): return lax.ppermute(x, 'tm', [(i, i ^ bit) for i in range(n)])  21.5 us
    ppermute x16, starting transfers between devices, swap(): return lax.ppermute(x, 'tm', [(i, i ^ bit) for i in range(n)])  16.4 us
  transfers between devices with their start and end apart: 16, of which 14 were waited for; matrix products, arithmetic and copies ran while one was open for 0% of the time, Pallas kernels for 6%

profile of v4, /device:TPU:0, one launch (start us, length us, event | category | flops | bytes accessed | tf_op | source)
XLA Modules:
  0.0 71.9 jit_solution(2588184874568983295)
XLA Ops:
  0.6 20.6 %build.1 = (f32[320,256]{1,0:T(8,128)S(1)}, f32[16,320,256]{2,1,0:T(8,128)S(1)}, bf16[2,256,256]{2,1,0:T(8,128)(2,1)S(1)}, f32[128,256]{1,0:T(8,128)S(1)}, bf16[128,64,256]{2,1,0:T(8,128)(2,1)S(1)}) custom-call(f32[256,256]{1,0:T(8,128)} %gen_hbm.1, f32[128,256]{1,0:T(8,128)} %d_hbm.1, bf16[128,64,256]{2,1,0:T(8,128)(2,1)} %bitcast.9), custom_call_target="tpu_custom_call" | custom-call | flops 16106127360 | tf_op jit(solution)/shard_map/build/pallas_call | solution.py:310
  21.2 0.5 collective-permute-start
  21.8 1.3 %collective-permute-done.other_ref = f32[320,256]{1,0:T(8,128)S(1)} collective-permute-done((f32[320,256]{1,0:T(8,128)S(1)}, f32[320,256]{1,0:T(8,128)S(1)}, u32[]{:S(2)}, u32[]{:S(2)}) %collective-permute-start) | collective-permute-done | bytes 327712 | tf_op jit(solution)/shard_map/ppermute | solution.py:399
  23.0 0.5 pair.1
  23.5 3.0 %collective-permute-start.1 = (f32[160,256]{1,0:T(8,128)S(1)}, f32[160,256]{1,0:T(8,128)S(1)}, u32[]{:S(2)}, u32[]{:S(2)}) collective-permute-start(f32[160,256]{1,0:T(8,128)S(1)} %get-tuple-element.22), channel_id=1, source_target_pairs={{0,2},{1,3},{2,0},{3,1},{4,6},{5,7},{6,4},{7,5},{8,10},{9,11},{10,... | collective-permute-start | bytes 491528 | tf_op jit(solution)/shard_map/ppermute | solution.py:399
  26.5 1.6 %collective-permute-start.3 = (f32[160,256]{1,0:T(8,128)S(1)}, f32[160,256]{1,0:T(8,128)S(1)}, u32[]{:S(2)}, u32[]{:S(2)}) collective-permute-start(f32[160,256]{1,0:T(8,128)S(1)} %get-tuple-element.22), channel_id=1, source_target_pairs={{0,4},{1,5},{2,6},{3,7},{4,0},{5,1},{6,2},{7,3},{8,12},{9,13},{10,... | collective-permute-start | bytes 491528 | tf_op jit(solution)/shard_map/ppermute | solution.py:399
  28.1 2.9 %collective-permute-done.1._ = f32[160,256]{1,0:T(8,128)S(1)} collective-permute-done((f32[160,256]{1,0:T(8,128)S(1)}, f32[160,256]{1,0:T(8,128)S(1)}, u32[]{:S(2)}, u32[]{:S(2)}) %collective-permute-start.1) | collective-permute-done | bytes 163872 | tf_op jit(solution)/shard_map/ppermute | solution.py:399
  31.0 3.4 %marks.1 = (bf16[16,256,256]{2,1,0:T(8,128)(2,1)S(1)}, bf16[16,256,256]{2,1,0:T(8,128)(2,1)S(1)}, f32[16,64,256]{2,1,0:T(8,128)S(1)}, bf16[8,256,1024]{2,1,0:T(8,128)(2,1)S(1)}, f32[160,256]{1,0:T(8,128)S(1)}) custom-call(f32[16,320,256]{2,1,0:T(8,128)S(1)} %get-tuple-element.21.raw_ref, ...), custom_call_target="tpu_custom_call", output_to_operand_aliasing={{4}: (2, {})} | custom-call | flops 2013265920 | bytes 15000000 | tf_op jit(solution)/shard_map/marks/pallas_call | solution.py:310
  34.4 0.1 collective-permute-start.2
  34.5 0.5 collective-permute-start.4
  35.0 0.7 %collective-permute-done.5.rest_4_ = f32[160,256]{1,0:T(8,128)S(1)} collective-permute-done((f32[160,256]{1,0:T(8,128)S(1)}, f32[160,256]{1,0:T(8,128)S(1)}, u32[]{:S(2)}, u32[]{:S(2)}) %collective-permute-start.5) | collective-permute-done | bytes 163872 | tf_op jit(solution)/shard_map/ppermute | solution.py:399
  35.7 0.1 collective-permute-done.2.rest_1_
  35.9 0.2 collective-permute-done.4.rest_3_
  36.1 1.0 %collective-permute-done.6.rest_5_ = f32[160,256]{1,0:T(8,128)S(1)} collective-permute-done((f32[160,256]{1,0:T(8,128)S(1)}, f32[160,256]{1,0:T(8,128)S(1)}, u32[]{:S(2)}, u32[]{:S(2)}) %collective-permute-start.6) | collective-permute-done | bytes 163872 | tf_op jit(solution)/shard_map/ppermute | solution.py:399
  37.1 0.9 %top.1 = f32[64,256]{1,0:T(8,128)S(1)} custom-call(f32[320,256]{1,0:T(8,128)S(1)} %get-tuple-element.20.own_ref, f32[64,256]{1,0:T(8,128)S(1)} %bitcast.6, f32[160,256]{1,0:T(8,128)S(1)} %get-tuple-element.23.rest_0_, f32[160,256]{1,0:T(8,128)S(1)} %collective-permute-done.2.rest_1_, f32[160,256]{1,0:T(8,128)S(1)} %collective-permute-done.3.rest_2_, ...), custom_call_target="tpu_custom_call" | custom-call | flops 100663296 | tf_op jit(solution)/shard_map/top/pallas_call | solution.py:310
  38.1 2.8 %collective-permute-start.7 = (f32[64,256]{1,0:T(8,128)S(1)}, f32[64,256]{1,0:T(8,128)S(1)}, u32[]{:S(2)}, u32[]{:S(2)}) collective-permute-start(f32[64,256]{1,0:T(8,128)S(1)} %top.1), channel_id=1, source_target_pairs={{0,8},{1,9},{2,10},{3,11},{4,12},{5,13},{6,14},{7,15},{8,0},{9,1},... | collective-permute-start | bytes 196616 | tf_op jit(solution)/shard_map/ppermute | solution.py:399
  40.9 1.0 %later.3.later_ref = f32[320,256]{1,0:T(8,128)S(1)} custom-call(f32[320,256]{1,0:T(8,128)S(1)} %later.2.later_ref, f32[160,256]{1,0:T(8,128)S(1)} %get-tuple-element.23.rest_0_, f32[160,256]{1,0:T(8,128)S(1)} %collective-permute-done.2.rest_1_, f32[160,256]{1,0:T(8,128)S(1)} %collective-permute-done.3.rest_2_, ...), custom_call_target="tpu_custom_call" | custom-call | flops 503316480 | tf_op jit(solution)/shard_map/later/pallas_call | solution.py:310
  41.9 2.8 %collective-permute-done.7.got_ref = f32[64,256]{1,0:T(8,128)S(1)} collective-permute-done((f32[64,256]{1,0:T(8,128)S(1)}, f32[64,256]{1,0:T(8,128)S(1)}, u32[]{:S(2)}, u32[]{:S(2)}) %collective-permute-start.7) | collective-permute-done | bytes 65568 | tf_op jit(solution)/shard_map/ppermute | solution.py:399
  44.7 6.0 %sweep.1 = (bf16[16,8,64,256]{3,2,1,0:T(8,128)(2,1)}, f32[128,256]{1,0:T(8,128)S(1)}, f32[128,256]{1,0:T(8,128)S(1)}) custom-call(f32[64,256]{1,0:T(8,128)S(1)} %bitcast.7, f32[64,256]{1,0:T(8,128)S(1)} %collective-permute-done.7.got_ref, f32[320,256]{1,0:T(8,128)S(1)} %later.3.later_ref, bf16[16,256,256]{2,1,0:T(8,128)(2,1)S(1)} %get-tuple-element.24.zh_ref, ...), custom_call_target="tpu_custom_call" | custom-call | flops 4294967296 | tf_op jit(solution)/shard_map/sweep/pallas_call | solution.py:310
  50.7 0.1 collective-permute-start.8
  50.7 1.3 %collective-permute-done.8.got_ref = f32[128,256]{1,0:T(8,128)S(1)} collective-permute-done((f32[128,256]{1,0:T(8,128)S(1)}, f32[128,256]{1,0:T(8,128)S(1)}, u32[]{:S(2)}, u32[]{:S(2)}) %collective-permute-start.8) | collective-permute-done | bytes 131104 | tf_op jit(solution)/shard_map/ppermute | solution.py:399
  52.1 1.7 %collective-permute-start.9 = (f32[64,256]{1,0:T(8,128)S(1)}, f32[64,256]{1,0:T(8,128)S(1)}, u32[]{:S(2)}, u32[]{:S(2)}) collective-permute-start(f32[64,256]{1,0:T(8,128)S(1)} %get-tuple-element.35), channel_id=1, source_target_pairs={{0,2},{1,3},{2,0},{3,1},{4,6},{5,7},{6,4},{7,5},{8,10},{9,11},{10,... | collective-permute-start | bytes 196616 | tf_op jit(solution)/shard_map/ppermute | solution.py:399
  53.8 2.6 %collective-permute-done.9 = f32[64,256]{1,0:T(8,128)S(1)} collective-permute-done((f32[64,256]{1,0:T(8,128)S(1)}, f32[64,256]{1,0:T(8,128)S(1)}, u32[]{:S(2)}, u32[]{:S(2)}) %collective-permute-start.9) | collective-permute-done | bytes 65568 | tf_op jit(solution)/shard_map/ppermute | solution.py:399
  56.4 3.6 %collective-permute-start.12 = (f32[64,256]{1,0:T(8,128)S(1)}, f32[64,256]{1,0:T(8,128)S(1)}, u32[]{:S(2)}, u32[]{:S(2)}) collective-permute-start(f32[64,256]{1,0:T(8,128)S(1)} %add.12), channel_id=1, source_target_pairs={{0,12},{1,13},{2,14},{3,15},{4,8},{5,9},{6,10},{7,11},{8,4},{9,5},... | collective-permute-start | bytes 196616 | tf_op jit(solution)/shard_map/ppermute | solution.py:399
  60.0 0.9 %collective-permute-start.10 = (f32[64,256]{1,0:T(8,128)S(1)}, f32[64,256]{1,0:T(8,128)S(1)}, u32[]{:S(2)}, u32[]{:S(2)}) collective-permute-start(f32[64,256]{1,0:T(8,128)S(1)} %add.12), channel_id=1, source_target_pairs={{0,4},{1,5},{2,6},{3,7},{4,0},{5,1},{6,2},{7,3},{8,12},{9,13},{10,... | collective-permute-start | bytes 196616 | tf_op jit(solution)/shard_map/ppermute | solution.py:399
  60.9 1.8 %collective-permute-done.12 = f32[64,256]{1,0:T(8,128)S(1)} collective-permute-done((f32[64,256]{1,0:T(8,128)S(1)}, f32[64,256]{1,0:T(8,128)S(1)}, u32[]{:S(2)}, u32[]{:S(2)}) %collective-permute-start.12) | collective-permute-done | bytes 65568 | tf_op jit(solution)/shard_map/ppermute | solution.py:399
  62.7 2.5 %collective-permute-done.11 = f32[64,256]{1,0:T(8,128)S(1)} collective-permute-done((f32[64,256]{1,0:T(8,128)S(1)}, f32[64,256]{1,0:T(8,128)S(1)}, u32[]{:S(2)}, u32[]{:S(2)}) %collective-permute-start.11) | collective-permute-done | bytes 65568 | tf_op jit(solution)/shard_map/ppermute | solution.py:399
  65.2 0.3 collective-permute-done.10
  65.5 1.7 %collective-permute-start.13 = (f32[64,256]{1,0:T(8,128)S(1)}, f32[64,256]{1,0:T(8,128)S(1)}, u32[]{:S(2)}, u32[]{:S(2)}) collective-permute-start(f32[64,256]{1,0:T(8,128)S(1)} %add_add_fusion.own_ref), channel_id=1, source_target_pairs={{0,2},{1,3},{2,0},{3,1},{4,6},{5,7},{6,4},{7,5},{8,10},{9,11},{10,... | collective-permute-start | bytes 196616 | tf_op jit(solution)/shard_map/ppermute | solution.py:399
  67.3 2.6 %collective-permute-done.13.far_ref = f32[64,256]{1,0:T(8,128)S(1)} collective-permute-done((f32[64,256]{1,0:T(8,128)S(1)}, f32[64,256]{1,0:T(8,128)S(1)}, u32[]{:S(2)}, u32[]{:S(2)}) %collective-permute-start.13) | collective-permute-done | bytes 65568 | tf_op jit(solution)/shard_map/ppermute | solution.py:399
  69.9 1.2 %collective-permute-done.15.both_ref = f32[64,256]{1,0:T(8,128)S(1)} collective-permute-done((f32[64,256]{1,0:T(8,128)S(1)}, f32[64,256]{1,0:T(8,128)S(1)}, u32[]{:S(2)}, u32[]{:S(2)}) %collective-permute-start.15) | collective-permute-done | bytes 65568 | tf_op jit(solution)/shard_map/ppermute | solution.py:399
  71.1 0.7 %join.1 = f32[256,256]{1,0:T(8,128)} custom-call(f32[64,256]{1,0:T(8,128)S(1)} %add_add_fusion.own_ref, f32[64,256]{1,0:T(8,128)S(1)} %collective-permute-done.13.far_ref, f32[64,256]{1,0:T(8,128)S(1)} %collective-permute-done.14.core_ref, f32[64,256]{1,0:T(8,128)S(1)} %collective-permute-done.15.both_ref), custom_call_target="tpu_custom_call" | custom-call | tf_op jit(solution)/shard_map/join/pallas_call | solution.py:310
  (13 shorter events, 0.1 us)
Async XLA Ops:
  21.2 1.8 %collective-permute-start = (f32[320,256]{1,0:T(8,128)S(1)}, f32[320,256]{1,0:T(8,128)S(1)}, u32[]{:S(2)}, u32[]{:S(2)}) collective-permute-start(f32[320,256]{1,0:T(8,128)S(1)} %get-tuple-element.19.own_ref), channel_id=1, source_target_pairs={{0,1},{1,0},{2,3},{3,2},{4,5},{5,4},{6,7},{7,6},{8,9},{9,8},{10,11... | collective-permute-start | bytes 983048 | tf_op jit(solution)/shard_map/ppermute | solution.py:399
  23.5 7.5 %collective-permute-start.1 = (f32[160,256]{1,0:T(8,128)S(1)}, f32[160,256]{1,0:T(8,128)S(1)}, u32[]{:S(2)}, u32[]{:S(2)}) collective-permute-start(f32[160,256]{1,0:T(8,128)S(1)} %get-tuple-element.22), channel_id=1, source_target_pairs={{0,2},{1,3},{2,0},{3,1},{4,6},{5,7},{6,4},{7,5},{8,10},{9,11},{10,... | collective-permute-start | bytes 491528 | tf_op jit(solution)/shard_map/ppermute | solution.py:399
  26.5 8.0 %collective-permute-start.3 = (f32[160,256]{1,0:T(8,128)S(1)}, f32[160,256]{1,0:T(8,128)S(1)}, u32[]{:S(2)}, u32[]{:S(2)}) collective-permute-start(f32[160,256]{1,0:T(8,128)S(1)} %get-tuple-element.22), channel_id=1, source_target_pairs={{0,4},{1,5},{2,6},{3,7},{4,0},{5,1},{6,2},{7,3},{8,12},{9,13},{10,... | collective-permute-start | bytes 491528 | tf_op jit(solution)/shard_map/ppermute | solution.py:399
  28.1 7.7 %collective-permute-start.5 = (f32[160,256]{1,0:T(8,128)S(1)}, f32[160,256]{1,0:T(8,128)S(1)}, u32[]{:S(2)}, u32[]{:S(2)}) collective-permute-start(f32[160,256]{1,0:T(8,128)S(1)} %get-tuple-element.22), channel_id=1, source_target_pairs={{0,6},{1,7},{2,4},{3,5},{4,2},{5,3},{6,0},{7,1},{8,14},{9,15},{10,... | collective-permute-start | bytes 491528 | tf_op jit(solution)/shard_map/ppermute | solution.py:399
  31.0 6.2 %copy-start = (f32[256,64]{0,1:T(8,128)S(1)}, f32[256,64]{0,1:T(8,128)}, u32[]{:S(2)}) copy-start(f32[256,64]{0,1:T(8,128)} %param.9) | copy-start | bytes 196612
  34.4 1.5 %collective-permute-start.2 = (f32[160,256]{1,0:T(8,128)S(1)}, f32[160,256]{1,0:T(8,128)S(1)}, u32[]{:S(2)}, u32[]{:S(2)}) collective-permute-start(f32[160,256]{1,0:T(8,128)S(1)} %get-tuple-element.23.rest_0_), channel_id=1, source_target_pairs={{0,1},{1,0},{2,3},{3,2},{4,5},{5,4},{6,7},{7,6},{8,9},{9,8},{10,11... | collective-permute-start | bytes 491528 | tf_op jit(solution)/shard_map/ppermute | solution.py:399
  34.5 1.6 %collective-permute-start.4 = (f32[160,256]{1,0:T(8,128)S(1)}, f32[160,256]{1,0:T(8,128)S(1)}, u32[]{:S(2)}, u32[]{:S(2)}) collective-permute-start(f32[160,256]{1,0:T(8,128)S(1)} %collective-permute-done.3.rest_2_), channel_id=1, source_target_pairs={{0,1},{1,0},{2,3},{3,2},{4,5},{5,4},{6,7},{7,6},{8,9},{9,8},{10,11... | collective-permute-start | bytes 491528 | tf_op jit(solution)/shard_map/ppermute | solution.py:399
  35.7 1.4 %collective-permute-start.6 = (f32[160,256]{1,0:T(8,128)S(1)}, f32[160,256]{1,0:T(8,128)S(1)}, u32[]{:S(2)}, u32[]{:S(2)}) collective-permute-start(f32[160,256]{1,0:T(8,128)S(1)} %collective-permute-done.5.rest_4_), channel_id=1, source_target_pairs={{0,1},{1,0},{2,3},{3,2},{4,5},{5,4},{6,7},{7,6},{8,9},{9,8},{10,11... | collective-permute-start | bytes 491528 | tf_op jit(solution)/shard_map/ppermute | solution.py:399
  38.1 6.6 %collective-permute-start.7 = (f32[64,256]{1,0:T(8,128)S(1)}, f32[64,256]{1,0:T(8,128)S(1)}, u32[]{:S(2)}, u32[]{:S(2)}) collective-permute-start(f32[64,256]{1,0:T(8,128)S(1)} %top.1), channel_id=1, source_target_pairs={{0,8},{1,9},{2,10},{3,11},{4,12},{5,13},{6,14},{7,15},{8,0},{9,1},... | collective-permute-start | bytes 196616 | tf_op jit(solution)/shard_map/ppermute | solution.py:399
  50.7 1.4 %collective-permute-start.8 = (f32[128,256]{1,0:T(8,128)S(1)}, f32[128,256]{1,0:T(8,128)S(1)}, u32[]{:S(2)}, u32[]{:S(2)}) collective-permute-start(f32[128,256]{1,0:T(8,128)S(1)} %get-tuple-element.33), channel_id=1, source_target_pairs={{0,1},{1,0},{2,3},{3,2},{4,5},{5,4},{6,7},{7,6},{8,9},{9,8},{10,11... | collective-permute-start | bytes 393224 | tf_op jit(solution)/shard_map/ppermute | solution.py:399
  52.1 4.3 %collective-permute-start.9 = (f32[64,256]{1,0:T(8,128)S(1)}, f32[64,256]{1,0:T(8,128)S(1)}, u32[]{:S(2)}, u32[]{:S(2)}) collective-permute-start(f32[64,256]{1,0:T(8,128)S(1)} %get-tuple-element.35), channel_id=1, source_target_pairs={{0,2},{1,3},{2,0},{3,1},{4,6},{5,7},{6,4},{7,5},{8,10},{9,11},{10,... | collective-permute-start | bytes 196616 | tf_op jit(solution)/shard_map/ppermute | solution.py:399
  56.4 6.3 %collective-permute-start.12 = (f32[64,256]{1,0:T(8,128)S(1)}, f32[64,256]{1,0:T(8,128)S(1)}, u32[]{:S(2)}, u32[]{:S(2)}) collective-permute-start(f32[64,256]{1,0:T(8,128)S(1)} %add.12), channel_id=1, source_target_pairs={{0,12},{1,13},{2,14},{3,15},{4,8},{5,9},{6,10},{7,11},{8,4},{9,5},... | collective-permute-start | bytes 196616 | tf_op jit(solution)/shard_map/ppermute | solution.py:399
  60.0 5.2 %collective-permute-start.11 = (f32[64,256]{1,0:T(8,128)S(1)}, f32[64,256]{1,0:T(8,128)S(1)}, u32[]{:S(2)}, u32[]{:S(2)}) collective-permute-start(f32[64,256]{1,0:T(8,128)S(1)} %add.12), channel_id=1, source_target_pairs={{0,8},{1,9},{2,10},{3,11},{4,12},{5,13},{6,14},{7,15},{8,0},{9,1},... | collective-permute-start | bytes 196616 | tf_op jit(solution)/shard_map/ppermute | solution.py:399
  60.0 5.5 %collective-permute-start.10 = (f32[64,256]{1,0:T(8,128)S(1)}, f32[64,256]{1,0:T(8,128)S(1)}, u32[]{:S(2)}, u32[]{:S(2)}) collective-permute-start(f32[64,256]{1,0:T(8,128)S(1)} %add.12), channel_id=1, source_target_pairs={{0,4},{1,5},{2,6},{3,7},{4,0},{5,1},{6,2},{7,3},{8,12},{9,13},{10,... | collective-permute-start | bytes 196616 | tf_op jit(solution)/shard_map/ppermute | solution.py:399
  65.5 4.3 %collective-permute-start.13 = (f32[64,256]{1,0:T(8,128)S(1)}, f32[64,256]{1,0:T(8,128)S(1)}, u32[]{:S(2)}, u32[]{:S(2)}) collective-permute-start(f32[64,256]{1,0:T(8,128)S(1)} %add_add_fusion.own_ref), channel_id=1, source_target_pairs={{0,2},{1,3},{2,0},{3,1},{4,6},{5,7},{6,4},{7,5},{8,10},{9,11},{10,... | collective-permute-start | bytes 196616 | tf_op jit(solution)/shard_map/ppermute | solution.py:399
  67.3 2.6 %collective-permute-start.14 = (f32[64,256]{1,0:T(8,128)S(1)}, f32[64,256]{1,0:T(8,128)S(1)}, u32[]{:S(2)}, u32[]{:S(2)}) collective-permute-start(f32[64,256]{1,0:T(8,128)S(1)} %add_add_fusion.own_ref), channel_id=1, source_target_pairs={{0,1},{1,0},{2,3},{3,2},{4,5},{5,4},{6,7},{7,6},{8,9},{9,8},{10,11... | collective-permute-start | bytes 196616 | tf_op jit(solution)/shard_map/ppermute | solution.py:399
  69.9 1.3 %collective-permute-start.15 = (f32[64,256]{1,0:T(8,128)S(1)}, f32[64,256]{1,0:T(8,128)S(1)}, u32[]{:S(2)}, u32[]{:S(2)}) collective-permute-start(f32[64,256]{1,0:T(8,128)S(1)} %collective-permute-done.13.far_ref), channel_id=1, source_target_pairs={{0,1},{1,0},{2,3},{3,2},{4,5},{5,4},{6,7},{7,6},{8,9},{9,8},{10,11... | collective-permute-start | bytes 196616 | tf_op jit(solution)/shard_map/ppermute | solution.py:399

commit v5 on v4

--- a/solution.py
+++ b/solution.py
@@ -10,6 +10,8 @@
 
 F32 = jnp.float32
 BF16 = jnp.bfloat16
+F8 = jnp.float8_e4m3fn
+LIFT = 4096.0
 VMEM_LIMIT = 24 * 1024 * 1024
 CHUNKS = 4
 SEG = 8
@@ -48,6 +50,18 @@
     return bottom + mm3(s4, *split(inner))
 
 
+def step_rows(x, width, rot_ref, coarse_ref):
+    rows = x.shape[0]
+    high = x.astype(BF16)
+    low = x - high.astype(F32)
+    both = mm(jnp.concatenate([high, low[width:].astype(BF16)], axis=0), rot_ref[0])
+    fine = mm(high, rot_ref[1])
+    small = mm((low[:width] * LIFT).astype(F8), coarse_ref[...]) * (1.0 / LIFT)
+    return jnp.concatenate(
+        [both[:width] + fine[:width] + small, both[width:rows] + fine[width:] + both[rows:]], axis=0
+    )
+
+
 def compose(rows_in, through, width):
     high, low = split(through[:width])
     out = mm3(rows_in, high, low)
@@ -59,7 +73,7 @@
     return mm3(vec, high, low) + through[width:]
 
 
-def build_kernel(gen_hbm, d_hbm, f_hbm, map_ref, raw_ref, rot_ref, d_ref, f_ref, gen_ref, sems):
+def build_kernel(gen_hbm, d_hbm, f_hbm, map_ref, raw_ref, rot_ref, d_ref, f_ref, gen_ref, coarse_ref, sems):
     steps, width = d_ref.shape
     per = steps // CHUNKS
     marks = per // SEG
@@ -74,6 +88,7 @@
     rot_high, rot_low = split(rot)
     rot_ref[0] = rot_high
     rot_ref[1] = rot_low
+    coarse_ref[...] = rot.astype(F8)
     fetches[1].wait()
     fetches[2].wait()
 
@@ -82,7 +97,7 @@
             out = []
             for g in range(CHUNKS):
                 t = g * per + per - 1 - k * SEG - s
-                moved = mm3(states[g] * d_ref[pl.ds(t, 1), :], rot_ref[0], rot_ref[1])
+                moved = step_rows(states[g] * d_ref[pl.ds(t, 1), :], width, rot_ref, coarse_ref)
                 out.append(
                     jnp.concatenate([moved[:width], moved[width:] + f_ref[t].astype(F32)], axis=0)
                 )
@@ -338,7 +353,7 @@
         derivs,
         force,
         where={0, 1, 2},
-        scratch=[VM(gen.shape, F32), pltpu.SemaphoreType.DMA((3,))],
+        scratch=[VM(gen.shape, F32), VM(gen.shape, F8), pltpu.SemaphoreType.DMA((3,))],
         flops=6 * steps * rows * width * width,
     )
 

time: 72 us -> 70.4 us (0.978)
  Pallas kernels: 33.2 us -> 31.6 us
    pallas_call x9, Pallas kernels: 33.2 us -> 31.6 us  [call(): pl.pallas_call(kernel, out_shape=tuple(out), in_specs=ins, out_specs=outs...]
where the time goes in v5:
time: 70.4 us; the launch traced here: 70.2 us
  Pallas kernels  31.6 us (45%)
  waiting for transfers between devices  21.5 us (31%)
  starting transfers between devices  16.4 us (23%)
  between operations  0.73 us (1%)
    pallas_call x9, Pallas kernels, call(): pl.pallas_call(kernel, out_shape=tuple(out), in_specs=ins, out_specs=outs...  31.6 us
    ppermute x16, waiting for transfers between devices, swap(): return lax.ppermute(x, 'tm', [(i, i ^ bit) for i in range(n)])  21.5 us
    ppermute x16, starting transfers between devices, swap(): return lax.ppermute(x, 'tm', [(i, i ^ bit) for i in range(n)])  16.4 us
  transfers between devices with their start and end apart: 16, of which 14 were waited for; matrix products, arithmetic and copies ran while one was open for 0% of the time, Pallas kernels for 6%

profile of v5, /device:TPU:0, one launch (start us, length us, event | category | flops | bytes accessed | tf_op | source)
XLA Modules:
  0.0 70.2 jit_solution(12669996482389776266)
XLA Ops:
  0.6 19.0 %build.1 = (f32[320,256]{1,0:T(8,128)S(1)}, f32[16,320,256]{2,1,0:T(8,128)S(1)}, bf16[2,256,256]{2,1,0:T(8,128)(2,1)S(1)}, f32[128,256]{1,0:T(8,128)S(1)}, bf16[128,64,256]{2,1,0:T(8,128)(2,1)S(1)}) custom-call(f32[256,256]{1,0:T(8,128)} %gen_hbm.1, f32[128,256]{1,0:T(8,128)} %d_hbm.1, bf16[128,64,256]{2,1,0:T(8,128)(2,1)} %bitcast.9), custom_call_target="tpu_custom_call" | custom-call | flops 16106127360 | tf_op jit(solution)/shard_map/build/pallas_call | solution.py:325
  19.6 0.5 collective-permute-start
  20.2 1.3 %collective-permute-done.other_ref = f32[320,256]{1,0:T(8,128)S(1)} collective-permute-done((f32[320,256]{1,0:T(8,128)S(1)}, f32[320,256]{1,0:T(8,128)S(1)}, u32[]{:S(2)}, u32[]{:S(2)}) %collective-permute-start) | collective-permute-done | bytes 327712 | tf_op jit(solution)/shard_map/ppermute | solution.py:414
  21.4 0.5 pair.1
  21.9 2.9 %collective-permute-start.1 = (f32[160,256]{1,0:T(8,128)S(1)}, f32[160,256]{1,0:T(8,128)S(1)}, u32[]{:S(2)}, u32[]{:S(2)}) collective-permute-start(f32[160,256]{1,0:T(8,128)S(1)} %get-tuple-element.22), channel_id=1, source_target_pairs={{0,2},{1,3},{2,0},{3,1},{4,6},{5,7},{6,4},{7,5},{8,10},{9,11},{10,... | collective-permute-start | bytes 491528 | tf_op jit(solution)/shard_map/ppermute | solution.py:414
  24.9 1.6 %collective-permute-start.3 = (f32[160,256]{1,0:T(8,128)S(1)}, f32[160,256]{1,0:T(8,128)S(1)}, u32[]{:S(2)}, u32[]{:S(2)}) collective-permute-start(f32[160,256]{1,0:T(8,128)S(1)} %get-tuple-element.22), channel_id=1, source_target_pairs={{0,4},{1,5},{2,6},{3,7},{4,0},{5,1},{6,2},{7,3},{8,12},{9,13},{10,... | collective-permute-start | bytes 491528 | tf_op jit(solution)/shard_map/ppermute | solution.py:414
  26.4 2.9 %collective-permute-done.1._ = f32[160,256]{1,0:T(8,128)S(1)} collective-permute-done((f32[160,256]{1,0:T(8,128)S(1)}, f32[160,256]{1,0:T(8,128)S(1)}, u32[]{:S(2)}, u32[]{:S(2)}) %collective-permute-start.1) | collective-permute-done | bytes 163872 | tf_op jit(solution)/shard_map/ppermute | solution.py:414
  29.4 3.4 %marks.1 = (bf16[16,256,256]{2,1,0:T(8,128)(2,1)S(1)}, bf16[16,256,256]{2,1,0:T(8,128)(2,1)S(1)}, f32[16,64,256]{2,1,0:T(8,128)S(1)}, bf16[8,256,1024]{2,1,0:T(8,128)(2,1)S(1)}, f32[160,256]{1,0:T(8,128)S(1)}) custom-call(f32[16,320,256]{2,1,0:T(8,128)S(1)} %get-tuple-element.21.raw_ref, ...), custom_call_target="tpu_custom_call", output_to_operand_aliasing={{4}: (2, {})} | custom-call | flops 2013265920 | bytes 15000000 | tf_op jit(solution)/shard_map/marks/pallas_call | solution.py:325
  32.8 0.1 collective-permute-start.2
  32.9 0.5 collective-permute-start.4
  33.4 0.7 %collective-permute-done.5.rest_4_ = f32[160,256]{1,0:T(8,128)S(1)} collective-permute-done((f32[160,256]{1,0:T(8,128)S(1)}, f32[160,256]{1,0:T(8,128)S(1)}, u32[]{:S(2)}, u32[]{:S(2)}) %collective-permute-start.5) | collective-permute-done | bytes 163872 | tf_op jit(solution)/shard_map/ppermute | solution.py:414
  34.1 0.1 collective-permute-done.2.rest_1_
  34.3 0.2 collective-permute-done.4.rest_3_
  34.5 1.0 %collective-permute-done.6.rest_5_ = f32[160,256]{1,0:T(8,128)S(1)} collective-permute-done((f32[160,256]{1,0:T(8,128)S(1)}, f32[160,256]{1,0:T(8,128)S(1)}, u32[]{:S(2)}, u32[]{:S(2)}) %collective-permute-start.6) | collective-permute-done | bytes 163872 | tf_op jit(solution)/shard_map/ppermute | solution.py:414
  35.5 0.9 %top.1 = f32[64,256]{1,0:T(8,128)S(1)} custom-call(f32[320,256]{1,0:T(8,128)S(1)} %get-tuple-element.20.own_ref, f32[64,256]{1,0:T(8,128)S(1)} %bitcast.6, f32[160,256]{1,0:T(8,128)S(1)} %get-tuple-element.23.rest_0_, f32[160,256]{1,0:T(8,128)S(1)} %collective-permute-done.2.rest_1_, f32[160,256]{1,0:T(8,128)S(1)} %collective-permute-done.3.rest_2_, ...), custom_call_target="tpu_custom_call" | custom-call | flops 100663296 | tf_op jit(solution)/shard_map/top/pallas_call | solution.py:325
  36.4 2.8 %collective-permute-start.7 = (f32[64,256]{1,0:T(8,128)S(1)}, f32[64,256]{1,0:T(8,128)S(1)}, u32[]{:S(2)}, u32[]{:S(2)}) collective-permute-start(f32[64,256]{1,0:T(8,128)S(1)} %top.1), channel_id=1, source_target_pairs={{0,8},{1,9},{2,10},{3,11},{4,12},{5,13},{6,14},{7,15},{8,0},{9,1},... | collective-permute-start | bytes 196616 | tf_op jit(solution)/shard_map/ppermute | solution.py:414
  39.3 1.0 %later.3.later_ref = f32[320,256]{1,0:T(8,128)S(1)} custom-call(f32[320,256]{1,0:T(8,128)S(1)} %later.2.later_ref, f32[160,256]{1,0:T(8,128)S(1)} %get-tuple-element.23.rest_0_, f32[160,256]{1,0:T(8,128)S(1)} %collective-permute-done.2.rest_1_, f32[160,256]{1,0:T(8,128)S(1)} %collective-permute-done.3.rest_2_, ...), custom_call_target="tpu_custom_call" | custom-call | flops 503316480 | tf_op jit(solution)/shard_map/later/pallas_call | solution.py:325
  40.3 2.8 %collective-permute-done.7.got_ref = f32[64,256]{1,0:T(8,128)S(1)} collective-permute-done((f32[64,256]{1,0:T(8,128)S(1)}, f32[64,256]{1,0:T(8,128)S(1)}, u32[]{:S(2)}, u32[]{:S(2)}) %collective-permute-start.7) | collective-permute-done | bytes 65568 | tf_op jit(solution)/shard_map/ppermute | solution.py:414
  43.1 6.0 %sweep.1 = (bf16[16,8,64,256]{3,2,1,0:T(8,128)(2,1)}, f32[128,256]{1,0:T(8,128)S(1)}, f32[128,256]{1,0:T(8,128)S(1)}) custom-call(f32[64,256]{1,0:T(8,128)S(1)} %bitcast.7, f32[64,256]{1,0:T(8,128)S(1)} %collective-permute-done.7.got_ref, f32[320,256]{1,0:T(8,128)S(1)} %later.3.later_ref, bf16[16,256,256]{2,1,0:T(8,128)(2,1)S(1)} %get-tuple-element.24.zh_ref, ...), custom_call_target="tpu_custom_call" | custom-call | flops 4294967296 | tf_op jit(solution)/shard_map/sweep/pallas_call | solution.py:325
  49.1 0.1 collective-permute-start.8
  49.1 1.3 %collective-permute-done.8.got_ref = f32[128,256]{1,0:T(8,128)S(1)} collective-permute-done((f32[128,256]{1,0:T(8,128)S(1)}, f32[128,256]{1,0:T(8,128)S(1)}, u32[]{:S(2)}, u32[]{:S(2)}) %collective-permute-start.8) | collective-permute-done | bytes 131104 | tf_op jit(solution)/shard_map/ppermute | solution.py:414
  50.5 1.7 %collective-permute-start.9 = (f32[64,256]{1,0:T(8,128)S(1)}, f32[64,256]{1,0:T(8,128)S(1)}, u32[]{:S(2)}, u32[]{:S(2)}) collective-permute-start(f32[64,256]{1,0:T(8,128)S(1)} %get-tuple-element.35), channel_id=1, source_target_pairs={{0,2},{1,3},{2,0},{3,1},{4,6},{5,7},{6,4},{7,5},{8,10},{9,11},{10,... | collective-permute-start | bytes 196616 | tf_op jit(solution)/shard_map/ppermute | solution.py:414
  52.2 2.6 %collective-permute-done.9 = f32[64,256]{1,0:T(8,128)S(1)} collective-permute-done((f32[64,256]{1,0:T(8,128)S(1)}, f32[64,256]{1,0:T(8,128)S(1)}, u32[]{:S(2)}, u32[]{:S(2)}) %collective-permute-start.9) | collective-permute-done | bytes 65568 | tf_op jit(solution)/shard_map/ppermute | solution.py:414
  54.8 3.6 %collective-permute-start.12 = (f32[64,256]{1,0:T(8,128)S(1)}, f32[64,256]{1,0:T(8,128)S(1)}, u32[]{:S(2)}, u32[]{:S(2)}) collective-permute-start(f32[64,256]{1,0:T(8,128)S(1)} %add.12), channel_id=1, source_target_pairs={{0,12},{1,13},{2,14},{3,15},{4,8},{5,9},{6,10},{7,11},{8,4},{9,5},... | collective-permute-start | bytes 196616 | tf_op jit(solution)/shard_map/ppermute | solution.py:414
  58.4 0.9 %collective-permute-start.10 = (f32[64,256]{1,0:T(8,128)S(1)}, f32[64,256]{1,0:T(8,128)S(1)}, u32[]{:S(2)}, u32[]{:S(2)}) collective-permute-start(f32[64,256]{1,0:T(8,128)S(1)} %add.12), channel_id=1, source_target_pairs={{0,4},{1,5},{2,6},{3,7},{4,0},{5,1},{6,2},{7,3},{8,12},{9,13},{10,... | collective-permute-start | bytes 196616 | tf_op jit(solution)/shard_map/ppermute | solution.py:414
  59.3 1.8 %collective-permute-done.12 = f32[64,256]{1,0:T(8,128)S(1)} collective-permute-done((f32[64,256]{1,0:T(8,128)S(1)}, f32[64,256]{1,0:T(8,128)S(1)}, u32[]{:S(2)}, u32[]{:S(2)}) %collective-permute-start.12) | collective-permute-done | bytes 65568 | tf_op jit(solution)/shard_map/ppermute | solution.py:414
  61.1 2.5 %collective-permute-done.11 = f32[64,256]{1,0:T(8,128)S(1)} collective-permute-done((f32[64,256]{1,0:T(8,128)S(1)}, f32[64,256]{1,0:T(8,128)S(1)}, u32[]{:S(2)}, u32[]{:S(2)}) %collective-permute-start.11) | collective-permute-done | bytes 65568 | tf_op jit(solution)/shard_map/ppermute | solution.py:414
  63.6 0.3 collective-permute-done.10
  63.9 1.7 %collective-permute-start.13 = (f32[64,256]{1,0:T(8,128)S(1)}, f32[64,256]{1,0:T(8,128)S(1)}, u32[]{:S(2)}, u32[]{:S(2)}) collective-permute-start(f32[64,256]{1,0:T(8,128)S(1)} %add_add_fusion.own_ref), channel_id=1, source_target_pairs={{0,2},{1,3},{2,0},{3,1},{4,6},{5,7},{6,4},{7,5},{8,10},{9,11},{10,... | collective-permute-start | bytes 196616 | tf_op jit(solution)/shard_map/ppermute | solution.py:414
  65.7 2.6 %collective-permute-done.13.far_ref = f32[64,256]{1,0:T(8,128)S(1)} collective-permute-done((f32[64,256]{1,0:T(8,128)S(1)}, f32[64,256]{1,0:T(8,128)S(1)}, u32[]{:S(2)}, u32[]{:S(2)}) %collective-permute-start.13) | collective-permute-done | bytes 65568 | tf_op jit(solution)/shard_map/ppermute | solution.py:414
  68.3 1.2 %collective-permute-done.15.both_ref = f32[64,256]{1,0:T(8,128)S(1)} collective-permute-done((f32[64,256]{1,0:T(8,128)S(1)}, f32[64,256]{1,0:T(8,128)S(1)}, u32[]{:S(2)}, u32[]{:S(2)}) %collective-permute-start.15) | collective-permute-done | bytes 65568 | tf_op jit(solution)/shard_map/ppermute | solution.py:414
  69.5 0.7 %join.1 = f32[256,256]{1,0:T(8,128)} custom-call(f32[64,256]{1,0:T(8,128)S(1)} %add_add_fusion.own_ref, f32[64,256]{1,0:T(8,128)S(1)} %collective-permute-done.13.far_ref, f32[64,256]{1,0:T(8,128)S(1)} %collective-permute-done.14.core_ref, f32[64,256]{1,0:T(8,128)S(1)} %collective-permute-done.15.both_ref), custom_call_target="tpu_custom_call" | custom-call | tf_op jit(solution)/shard_map/join/pallas_call | solution.py:325
  (13 shorter events, 0.1 us)
Async XLA Ops:
  19.6 1.8 %collective-permute-start = (f32[320,256]{1,0:T(8,128)S(1)}, f32[320,256]{1,0:T(8,128)S(1)}, u32[]{:S(2)}, u32[]{:S(2)}) collective-permute-start(f32[320,256]{1,0:T(8,128)S(1)} %get-tuple-element.19.own_ref), channel_id=1, source_target_pairs={{0,1},{1,0},{2,3},{3,2},{4,5},{5,4},{6,7},{7,6},{8,9},{9,8},{10,11... | collective-permute-start | bytes 983048 | tf_op jit(solution)/shard_map/ppermute | solution.py:414
  21.9 7.4 %collective-permute-start.1 = (f32[160,256]{1,0:T(8,128)S(1)}, f32[160,256]{1,0:T(8,128)S(1)}, u32[]{:S(2)}, u32[]{:S(2)}) collective-permute-start(f32[160,256]{1,0:T(8,128)S(1)} %get-tuple-element.22), channel_id=1, source_target_pairs={{0,2},{1,3},{2,0},{3,1},{4,6},{5,7},{6,4},{7,5},{8,10},{9,11},{10,... | collective-permute-start | bytes 491528 | tf_op jit(solution)/shard_map/ppermute | solution.py:414
  24.9 8.0 %collective-permute-start.3 = (f32[160,256]{1,0:T(8,128)S(1)}, f32[160,256]{1,0:T(8,128)S(1)}, u32[]{:S(2)}, u32[]{:S(2)}) collective-permute-start(f32[160,256]{1,0:T(8,128)S(1)} %get-tuple-element.22), channel_id=1, source_target_pairs={{0,4},{1,5},{2,6},{3,7},{4,0},{5,1},{6,2},{7,3},{8,12},{9,13},{10,... | collective-permute-start | bytes 491528 | tf_op jit(solution)/shard_map/ppermute | solution.py:414
  26.4 7.7 %collective-permute-start.5 = (f32[160,256]{1,0:T(8,128)S(1)}, f32[160,256]{1,0:T(8,128)S(1)}, u32[]{:S(2)}, u32[]{:S(2)}) collective-permute-start(f32[160,256]{1,0:T(8,128)S(1)} %get-tuple-element.22), channel_id=1, source_target_pairs={{0,6},{1,7},{2,4},{3,5},{4,2},{5,3},{6,0},{7,1},{8,14},{9,15},{10,... | collective-permute-start | bytes 491528 | tf_op jit(solution)/shard_map/ppermute | solution.py:414
  29.4 6.2 %copy-start = (f32[256,64]{0,1:T(8,128)S(1)}, f32[256,64]{0,1:T(8,128)}, u32[]{:S(2)}) copy-start(f32[256,64]{0,1:T(8,128)} %param.9) | copy-start | bytes 196612
  32.8 1.5 %collective-permute-start.2 = (f32[160,256]{1,0:T(8,128)S(1)}, f32[160,256]{1,0:T(8,128)S(1)}, u32[]{:S(2)}, u32[]{:S(2)}) collective-permute-start(f32[160,256]{1,0:T(8,128)S(1)} %get-tuple-element.23.rest_0_), channel_id=1, source_target_pairs={{0,1},{1,0},{2,3},{3,2},{4,5},{5,4},{6,7},{7,6},{8,9},{9,8},{10,11... | collective-permute-start | bytes 491528 | tf_op jit(solution)/shard_map/ppermute | solution.py:414
  32.9 1.6 %collective-permute-start.4 = (f32[160,256]{1,0:T(8,128)S(1)}, f32[160,256]{1,0:T(8,128)S(1)}, u32[]{:S(2)}, u32[]{:S(2)}) collective-permute-start(f32[160,256]{1,0:T(8,128)S(1)} %collective-permute-done.3.rest_2_), channel_id=1, source_target_pairs={{0,1},{1,0},{2,3},{3,2},{4,5},{5,4},{6,7},{7,6},{8,9},{9,8},{10,11... | collective-permute-start | bytes 491528 | tf_op jit(solution)/shard_map/ppermute | solution.py:414
  34.1 1.4 %collective-permute-start.6 = (f32[160,256]{1,0:T(8,128)S(1)}, f32[160,256]{1,0:T(8,128)S(1)}, u32[]{:S(2)}, u32[]{:S(2)}) collective-permute-start(f32[160,256]{1,0:T(8,128)S(1)} %collective-permute-done.5.rest_4_), channel_id=1, source_target_pairs={{0,1},{1,0},{2,3},{3,2},{4,5},{5,4},{6,7},{7,6},{8,9},{9,8},{10,11... | collective-permute-start | bytes 491528 | tf_op jit(solution)/shard_map/ppermute | solution.py:414
  36.4 6.6 %collective-permute-start.7 = (f32[64,256]{1,0:T(8,128)S(1)}, f32[64,256]{1,0:T(8,128)S(1)}, u32[]{:S(2)}, u32[]{:S(2)}) collective-permute-start(f32[64,256]{1,0:T(8,128)S(1)} %top.1), channel_id=1, source_target_pairs={{0,8},{1,9},{2,10},{3,11},{4,12},{5,13},{6,14},{7,15},{8,0},{9,1},... | collective-permute-start | bytes 196616 | tf_op jit(solution)/shard_map/ppermute | solution.py:414
  49.1 1.4 %collective-permute-start.8 = (f32[128,256]{1,0:T(8,128)S(1)}, f32[128,256]{1,0:T(8,128)S(1)}, u32[]{:S(2)}, u32[]{:S(2)}) collective-permute-start(f32[128,256]{1,0:T(8,128)S(1)} %get-tuple-element.33), channel_id=1, source_target_pairs={{0,1},{1,0},{2,3},{3,2},{4,5},{5,4},{6,7},{7,6},{8,9},{9,8},{10,11... | collective-permute-start | bytes 393224 | tf_op jit(solution)/shard_map/ppermute | solution.py:414
  50.5 4.3 %collective-permute-start.9 = (f32[64,256]{1,0:T(8,128)S(1)}, f32[64,256]{1,0:T(8,128)S(1)}, u32[]{:S(2)}, u32[]{:S(2)}) collective-permute-start(f32[64,256]{1,0:T(8,128)S(1)} %get-tuple-element.35), channel_id=1, source_target_pairs={{0,2},{1,3},{2,0},{3,1},{4,6},{5,7},{6,4},{7,5},{8,10},{9,11},{10,... | collective-permute-start | bytes 196616 | tf_op jit(solution)/shard_map/ppermute | solution.py:414
  54.8 6.3 %collective-permute-start.12 = (f32[64,256]{1,0:T(8,128)S(1)}, f32[64,256]{1,0:T(8,128)S(1)}, u32[]{:S(2)}, u32[]{:S(2)}) collective-permute-start(f32[64,256]{1,0:T(8,128)S(1)} %add.12), channel_id=1, source_target_pairs={{0,12},{1,13},{2,14},{3,15},{4,8},{5,9},{6,10},{7,11},{8,4},{9,5},... | collective-permute-start | bytes 196616 | tf_op jit(solution)/shard_map/ppermute | solution.py:414
  58.4 5.2 %collective-permute-start.11 = (f32[64,256]{1,0:T(8,128)S(1)}, f32[64,256]{1,0:T(8,128)S(1)}, u32[]{:S(2)}, u32[]{:S(2)}) collective-permute-start(f32[64,256]{1,0:T(8,128)S(1)} %add.12), channel_id=1, source_target_pairs={{0,8},{1,9},{2,10},{3,11},{4,12},{5,13},{6,14},{7,15},{8,0},{9,1},... | collective-permute-start | bytes 196616 | tf_op jit(solution)/shard_map/ppermute | solution.py:414
  58.4 5.5 %collective-permute-start.10 = (f32[64,256]{1,0:T(8,128)S(1)}, f32[64,256]{1,0:T(8,128)S(1)}, u32[]{:S(2)}, u32[]{:S(2)}) collective-permute-start(f32[64,256]{1,0:T(8,128)S(1)} %add.12), channel_id=1, source_target_pairs={{0,4},{1,5},{2,6},{3,7},{4,0},{5,1},{6,2},{7,3},{8,12},{9,13},{10,... | collective-permute-start | bytes 196616 | tf_op jit(solution)/shard_map/ppermute | solution.py:414
  63.9 4.3 %collective-permute-start.13 = (f32[64,256]{1,0:T(8,128)S(1)}, f32[64,256]{1,0:T(8,128)S(1)}, u32[]{:S(2)}, u32[]{:S(2)}) collective-permute-start(f32[64,256]{1,0:T(8,128)S(1)} %add_add_fusion.own_ref), channel_id=1, source_target_pairs={{0,2},{1,3},{2,0},{3,1},{4,6},{5,7},{6,4},{7,5},{8,10},{9,11},{10,... | collective-permute-start | bytes 196616 | tf_op jit(solution)/shard_map/ppermute | solution.py:414
  65.7 2.6 %collective-permute-start.14 = (f32[64,256]{1,0:T(8,128)S(1)}, f32[64,256]{1,0:T(8,128)S(1)}, u32[]{:S(2)}, u32[]{:S(2)}) collective-permute-start(f32[64,256]{1,0:T(8,128)S(1)} %add_add_fusion.own_ref), channel_id=1, source_target_pairs={{0,1},{1,0},{2,3},{3,2},{4,5},{5,4},{6,7},{7,6},{8,9},{9,8},{10,11... | collective-permute-start | bytes 196616 | tf_op jit(solution)/shard_map/ppermute | solution.py:414
  68.3 1.3 %collective-permute-start.15 = (f32[64,256]{1,0:T(8,128)S(1)}, f32[64,256]{1,0:T(8,128)S(1)}, u32[]{:S(2)}, u32[]{:S(2)}) collective-permute-start(f32[64,256]{1,0:T(8,128)S(1)} %collective-permute-done.13.far_ref), channel_id=1, source_target_pairs={{0,1},{1,0},{2,3},{3,2},{4,5},{5,4},{6,7},{7,6},{8,9},{9,8},{10,11... | collective-permute-start | bytes 196616 | tf_op jit(solution)/shard_map/ppermute | solution.py:414

commit v6 on v5

--- a/solution.py
+++ b/solution.py
@@ -11,7 +11,8 @@
 F32 = jnp.float32
 BF16 = jnp.bfloat16
 F8 = jnp.float8_e4m3fn
-LIFT = 4096.0
+LIFT = 1024.0
+F8_MAX = 448.0
 VMEM_LIMIT = 24 * 1024 * 1024
 CHUNKS = 4
 SEG = 8
@@ -56,7 +57,8 @@
     low = x - high.astype(F32)
     both = mm(jnp.concatenate([high, low[width:].astype(BF16)], axis=0), rot_ref[0])
     fine = mm(high, rot_ref[1])
-    small = mm((low[:width] * LIFT).astype(F8), coarse_ref[...]) * (1.0 / LIFT)
+    lifted = jnp.clip(low[:width] * LIFT, -F8_MAX, F8_MAX).astype(F8)
+    small = mm(lifted, coarse_ref[...]) * (1.0 / LIFT)
     return jnp.concatenate(
         [both[:width] + fine[:width] + small, both[width:rows] + fine[width:] + both[rows:]], axis=0
     )
@@ -88,7 +90,7 @@
     rot_high, rot_low = split(rot)
     rot_ref[0] = rot_high
     rot_ref[1] = rot_low
-    coarse_ref[...] = rot.astype(F8)
+    coarse_ref[...] = jnp.clip(rot, -F8_MAX, F8_MAX).astype(F8)
     fetches[1].wait()
     fetches[2].wait()
 
@@ -196,9 +198,12 @@
     count, _, width = maps.shape
     here = position(low_bit, count)
     vec = vec_ref[...]
-    for at in range(count - 1, -1, -1):
+    final = maps[(count // 2 - 1) ^ here]
+    for at in range(count // 2 - 2, -1, -1):
+        final = compose(final, maps[at ^ here], width)
+    for at in range(count - 1, count // 2 - 1, -1):
         vec = apply(vec, maps[at ^ here], width)
-    out_ref[...] = vec
+    out_ref[...] = apply(vec, final, width)
 
 
 def total_kernel(low_bit, own_ref, *rest):
@@ -298,17 +303,25 @@
     give_ref[...] = jnp.where(first, total[half:], total[:half])
 
 
-def join_kernel(bit, own_ref, far_ref, core_ref, both_ref, out_ref):
+def join_kernel(bit, own_ref, far_ref, core_ref, both_ref, out_hbm, sems):
     rows = own_ref.shape[0]
     place = lax.axis_index("tm")
     low, high = place & 1, (place // bit) & 1
-    for ref, a, b in (
-        (own_ref, low, high),
-        (far_ref, low, 1 - high),
-        (core_ref, 1 - low, high),
-        (both_ref, 1 - low, 1 - high),
+    sends = []
+    for i, (ref, a, b) in enumerate(
+        (
+            (own_ref, low, high),
+            (far_ref, low, 1 - high),
+            (core_ref, 1 - low, high),
+            (both_ref, 1 - low, 1 - high),
+        )
     ):
-        out_ref[pl.ds(pl.multiple_of((2 * a + b) * rows, rows), rows), :] = ref[...]
+        start = pl.multiple_of((2 * a + b) * rows, rows)
+        sends.append(pltpu.make_async_copy(ref, out_hbm.at[pl.ds(start, rows), :], sems.at[i]))
+    for send in sends:
+        send.start()
+    for send in sends:
+        send.wait()
 
 
 VM = pltpu.VMEM
@@ -319,8 +332,7 @@
     ins = [pl.BlockSpec(memory_space=pl.ANY if i in where else VM) for i in range(len(args))]
     args = [pltpu.with_memory_space_constraint(a, pltpu.HBM if i in where else VM) for i, a in enumerate(args)]
     outs = tuple(
-        pl.BlockSpec(memory_space=pl.ANY if isinstance(o, jax.ShapeDtypeStruct) and len(o.shape) > 2 else VM)
-        for o in out
+        pl.BlockSpec(memory_space=pl.ANY if isinstance(o, jax.ShapeDtypeStruct) else VM) for o in out
     )
     return pl.pallas_call(
         kernel,
@@ -466,7 +478,8 @@
     core = swap(x, 1)
     both = swap(far, 1)
     (out,) = call(
-        functools.partial(join_kernel, near), "join", (shape((4 * x.shape[0], x.shape[1])),), x, far, core, both
+        functools.partial(join_kernel, near), "join", (shape((4 * x.shape[0], x.shape[1])),), x, far, core, both,
+        scratch=[pltpu.SemaphoreType.DMA((4,))],
     )
     return out
 

time: 70.4 us -> 70.5 us (level)
  no operation moved by 1% of the time
where the time goes in v6:
time: 70.5 us; the launch traced here: 70.3 us
  Pallas kernels  31.5 us (45%)
  waiting for transfers between devices  21.5 us (30%)
  starting transfers between devices  16.4 us (23%)
  between operations  0.89 us (1%)
    pallas_call x9, Pallas kernels, call(): pl.pallas_call(kernel, out_shape=tuple(out), in_specs=ins, out_specs=outs...  31.5 us
    ppermute x16, waiting for transfers between devices, swap(): return lax.ppermute(x, 'tm', [(i, i ^ bit) for i in range(n)])  21.5 us
    ppermute x16, starting transfers between devices, swap(): return lax.ppermute(x, 'tm', [(i, i ^ bit) for i in range(n)])  16.4 us
  transfers between devices with their start and end apart: 16, of which 14 were waited for; matrix products, arithmetic and copies ran while one was open for 0% of the time, Pallas kernels for 6%

profile of v6, /device:TPU:0, one launch (start us, length us, event | category | flops | bytes accessed | tf_op | source)
XLA Modules:
  0.0 70.3 jit_solution(427526221994731008)
XLA Ops:
  0.6 19.0 %build.1 = (f32[320,256]{1,0:T(8,128)S(1)}, f32[16,320,256]{2,1,0:T(8,128)S(1)}, bf16[2,256,256]{2,1,0:T(8,128)(2,1)S(1)}, f32[128,256]{1,0:T(8,128)S(1)}, bf16[128,64,256]{2,1,0:T(8,128)(2,1)S(1)}) custom-call(f32[256,256]{1,0:T(8,128)} %gen_hbm.1, f32[128,256]{1,0:T(8,128)} %d_hbm.1, bf16[128,64,256]{2,1,0:T(8,128)(2,1)} %bitcast.9), custom_call_target="tpu_custom_call" | custom-call | flops 16106127360 | tf_op jit(solution)/shard_map/build/pallas_call | solution.py:337
  19.6 0.5 collective-permute-start
  20.2 1.3 %collective-permute-done.other_ref = f32[320,256]{1,0:T(8,128)S(1)} collective-permute-done((f32[320,256]{1,0:T(8,128)S(1)}, f32[320,256]{1,0:T(8,128)S(1)}, u32[]{:S(2)}, u32[]{:S(2)}) %collective-permute-start) | collective-permute-done | bytes 327712 | tf_op jit(solution)/shard_map/ppermute | solution.py:426
  21.4 0.5 pair.1
  21.9 2.9 %collective-permute-start.1 = (f32[160,256]{1,0:T(8,128)S(1)}, f32[160,256]{1,0:T(8,128)S(1)}, u32[]{:S(2)}, u32[]{:S(2)}) collective-permute-start(f32[160,256]{1,0:T(8,128)S(1)} %get-tuple-element.22), channel_id=1, source_target_pairs={{0,2},{1,3},{2,0},{3,1},{4,6},{5,7},{6,4},{7,5},{8,10},{9,11},{10,... | collective-permute-start | bytes 491528 | tf_op jit(solution)/shard_map/ppermute | solution.py:426
  24.9 1.6 %collective-permute-start.3 = (f32[160,256]{1,0:T(8,128)S(1)}, f32[160,256]{1,0:T(8,128)S(1)}, u32[]{:S(2)}, u32[]{:S(2)}) collective-permute-start(f32[160,256]{1,0:T(8,128)S(1)} %get-tuple-element.22), channel_id=1, source_target_pairs={{0,4},{1,5},{2,6},{3,7},{4,0},{5,1},{6,2},{7,3},{8,12},{9,13},{10,... | collective-permute-start | bytes 491528 | tf_op jit(solution)/shard_map/ppermute | solution.py:426
  26.4 2.9 %collective-permute-done.1._ = f32[160,256]{1,0:T(8,128)S(1)} collective-permute-done((f32[160,256]{1,0:T(8,128)S(1)}, f32[160,256]{1,0:T(8,128)S(1)}, u32[]{:S(2)}, u32[]{:S(2)}) %collective-permute-start.1) | collective-permute-done | bytes 163872 | tf_op jit(solution)/shard_map/ppermute | solution.py:426
  29.4 3.4 %marks.1 = (bf16[16,256,256]{2,1,0:T(8,128)(2,1)S(1)}, bf16[16,256,256]{2,1,0:T(8,128)(2,1)S(1)}, f32[16,64,256]{2,1,0:T(8,128)S(1)}, bf16[8,256,1024]{2,1,0:T(8,128)(2,1)S(1)}, f32[160,256]{1,0:T(8,128)S(1)}) custom-call(f32[16,320,256]{2,1,0:T(8,128)S(1)} %get-tuple-element.21.raw_ref, ...), custom_call_target="tpu_custom_call", output_to_operand_aliasing={{4}: (2, {})} | custom-call | flops 2013265920 | bytes 15000000 | tf_op jit(solution)/shard_map/marks/pallas_call | solution.py:337
  32.8 0.1 collective-permute-start.2
  32.9 0.5 collective-permute-start.4
  33.4 0.7 %collective-permute-done.5.rest_4_ = f32[160,256]{1,0:T(8,128)S(1)} collective-permute-done((f32[160,256]{1,0:T(8,128)S(1)}, f32[160,256]{1,0:T(8,128)S(1)}, u32[]{:S(2)}, u32[]{:S(2)}) %collective-permute-start.5) | collective-permute-done | bytes 163872 | tf_op jit(solution)/shard_map/ppermute | solution.py:426
  34.1 0.1 collective-permute-done.2.rest_1_
  34.3 0.2 collective-permute-done.4.rest_3_
  34.5 1.0 %collective-permute-done.6.rest_5_ = f32[160,256]{1,0:T(8,128)S(1)} collective-permute-done((f32[160,256]{1,0:T(8,128)S(1)}, f32[160,256]{1,0:T(8,128)S(1)}, u32[]{:S(2)}, u32[]{:S(2)}) %collective-permute-start.6) | collective-permute-done | bytes 163872 | tf_op jit(solution)/shard_map/ppermute | solution.py:426
  35.5 0.8 %top.1 = f32[64,256]{1,0:T(8,128)S(1)} custom-call(f32[320,256]{1,0:T(8,128)S(1)} %get-tuple-element.20.own_ref, f32[64,256]{1,0:T(8,128)S(1)} %bitcast.6, f32[160,256]{1,0:T(8,128)S(1)} %get-tuple-element.23.rest_0_, f32[160,256]{1,0:T(8,128)S(1)} %collective-permute-done.2.rest_1_, f32[160,256]{1,0:T(8,128)S(1)} %collective-permute-done.3.rest_2_, ...), custom_call_target="tpu_custom_call" | custom-call | flops 100663296 | tf_op jit(solution)/shard_map/top/pallas_call | solution.py:337
  36.4 2.8 %collective-permute-start.7 = (f32[64,256]{1,0:T(8,128)S(1)}, f32[64,256]{1,0:T(8,128)S(1)}, u32[]{:S(2)}, u32[]{:S(2)}) collective-permute-start(f32[64,256]{1,0:T(8,128)S(1)} %top.1), channel_id=1, source_target_pairs={{0,8},{1,9},{2,10},{3,11},{4,12},{5,13},{6,14},{7,15},{8,0},{9,1},... | collective-permute-start | bytes 196616 | tf_op jit(solution)/shard_map/ppermute | solution.py:426
  39.2 1.0 %later.3.later_ref = f32[320,256]{1,0:T(8,128)S(1)} custom-call(f32[320,256]{1,0:T(8,128)S(1)} %later.2.later_ref, f32[160,256]{1,0:T(8,128)S(1)} %get-tuple-element.23.rest_0_, f32[160,256]{1,0:T(8,128)S(1)} %collective-permute-done.2.rest_1_, f32[160,256]{1,0:T(8,128)S(1)} %collective-permute-done.3.rest_2_, ...), custom_call_target="tpu_custom_call" | custom-call | flops 503316480 | tf_op jit(solution)/shard_map/later/pallas_call | solution.py:337
  40.2 2.8 %collective-permute-done.7.got_ref = f32[64,256]{1,0:T(8,128)S(1)} collective-permute-done((f32[64,256]{1,0:T(8,128)S(1)}, f32[64,256]{1,0:T(8,128)S(1)}, u32[]{:S(2)}, u32[]{:S(2)}) %collective-permute-start.7) | collective-permute-done | bytes 65568 | tf_op jit(solution)/shard_map/ppermute | solution.py:426
  43.0 6.0 %sweep.1 = (bf16[16,8,64,256]{3,2,1,0:T(8,128)(2,1)}, f32[128,256]{1,0:T(8,128)S(1)}, f32[128,256]{1,0:T(8,128)S(1)}) custom-call(f32[64,256]{1,0:T(8,128)S(1)} %bitcast.7, f32[64,256]{1,0:T(8,128)S(1)} %collective-permute-done.7.got_ref, f32[320,256]{1,0:T(8,128)S(1)} %later.3.later_ref, bf16[16,256,256]{2,1,0:T(8,128)(2,1)S(1)} %get-tuple-element.24.zh_ref, ...), custom_call_target="tpu_custom_call" | custom-call | flops 4294967296 | tf_op jit(solution)/shard_map/sweep/pallas_call | solution.py:337
  49.0 0.1 collective-permute-start.8
  49.1 1.3 %collective-permute-done.8.got_ref = f32[128,256]{1,0:T(8,128)S(1)} collective-permute-done((f32[128,256]{1,0:T(8,128)S(1)}, f32[128,256]{1,0:T(8,128)S(1)}, u32[]{:S(2)}, u32[]{:S(2)}) %collective-permute-start.8) | collective-permute-done | bytes 131104 | tf_op jit(solution)/shard_map/ppermute | solution.py:426
  50.4 1.7 %collective-permute-start.9 = (f32[64,256]{1,0:T(8,128)S(1)}, f32[64,256]{1,0:T(8,128)S(1)}, u32[]{:S(2)}, u32[]{:S(2)}) collective-permute-start(f32[64,256]{1,0:T(8,128)S(1)} %get-tuple-element.35), channel_id=1, source_target_pairs={{0,2},{1,3},{2,0},{3,1},{4,6},{5,7},{6,4},{7,5},{8,10},{9,11},{10,... | collective-permute-start | bytes 196616 | tf_op jit(solution)/shard_map/ppermute | solution.py:426
  52.1 2.6 %collective-permute-done.9 = f32[64,256]{1,0:T(8,128)S(1)} collective-permute-done((f32[64,256]{1,0:T(8,128)S(1)}, f32[64,256]{1,0:T(8,128)S(1)}, u32[]{:S(2)}, u32[]{:S(2)}) %collective-permute-start.9) | collective-permute-done | bytes 65568 | tf_op jit(solution)/shard_map/ppermute | solution.py:426
  54.8 3.6 %collective-permute-start.12 = (f32[64,256]{1,0:T(8,128)S(1)}, f32[64,256]{1,0:T(8,128)S(1)}, u32[]{:S(2)}, u32[]{:S(2)}) collective-permute-start(f32[64,256]{1,0:T(8,128)S(1)} %add.12), channel_id=1, source_target_pairs={{0,12},{1,13},{2,14},{3,15},{4,8},{5,9},{6,10},{7,11},{8,4},{9,5},... | collective-permute-start | bytes 196616 | tf_op jit(solution)/shard_map/ppermute | solution.py:426
  58.3 0.9 %collective-permute-start.10 = (f32[64,256]{1,0:T(8,128)S(1)}, f32[64,256]{1,0:T(8,128)S(1)}, u32[]{:S(2)}, u32[]{:S(2)}) collective-permute-start(f32[64,256]{1,0:T(8,128)S(1)} %add.12), channel_id=1, source_target_pairs={{0,4},{1,5},{2,6},{3,7},{4,0},{5,1},{6,2},{7,3},{8,12},{9,13},{10,... | collective-permute-start | bytes 196616 | tf_op jit(solution)/shard_map/ppermute | solution.py:426
  59.2 1.8 %collective-permute-done.12 = f32[64,256]{1,0:T(8,128)S(1)} collective-permute-done((f32[64,256]{1,0:T(8,128)S(1)}, f32[64,256]{1,0:T(8,128)S(1)}, u32[]{:S(2)}, u32[]{:S(2)}) %collective-permute-start.12) | collective-permute-done | bytes 65568 | tf_op jit(solution)/shard_map/ppermute | solution.py:426
  61.0 2.5 %collective-permute-done.11 = f32[64,256]{1,0:T(8,128)S(1)} collective-permute-done((f32[64,256]{1,0:T(8,128)S(1)}, f32[64,256]{1,0:T(8,128)S(1)}, u32[]{:S(2)}, u32[]{:S(2)}) %collective-permute-start.11) | collective-permute-done | bytes 65568 | tf_op jit(solution)/shard_map/ppermute | solution.py:426
  63.5 0.3 collective-permute-done.10
  63.8 1.7 %collective-permute-start.13 = (f32[64,256]{1,0:T(8,128)S(1)}, f32[64,256]{1,0:T(8,128)S(1)}, u32[]{:S(2)}, u32[]{:S(2)}) collective-permute-start(f32[64,256]{1,0:T(8,128)S(1)} %add_add_fusion.own_ref), channel_id=1, source_target_pairs={{0,2},{1,3},{2,0},{3,1},{4,6},{5,7},{6,4},{7,5},{8,10},{9,11},{10,... | collective-permute-start | bytes 196616 | tf_op jit(solution)/shard_map/ppermute | solution.py:426
  65.6 2.6 %collective-permute-done.13.far_ref = f32[64,256]{1,0:T(8,128)S(1)} collective-permute-done((f32[64,256]{1,0:T(8,128)S(1)}, f32[64,256]{1,0:T(8,128)S(1)}, u32[]{:S(2)}, u32[]{:S(2)}) %collective-permute-start.13) | collective-permute-done | bytes 65568 | tf_op jit(solution)/shard_map/ppermute | solution.py:426
  68.2 1.2 %collective-permute-done.15.both_ref = f32[64,256]{1,0:T(8,128)S(1)} collective-permute-done((f32[64,256]{1,0:T(8,128)S(1)}, f32[64,256]{1,0:T(8,128)S(1)}, u32[]{:S(2)}, u32[]{:S(2)}) %collective-permute-start.15) | collective-permute-done | bytes 65568 | tf_op jit(solution)/shard_map/ppermute | solution.py:426
  69.4 0.7 %join.1 = f32[256,256]{1,0:T(8,128)} custom-call(f32[64,256]{1,0:T(8,128)S(1)} %add_add_fusion.own_ref, f32[64,256]{1,0:T(8,128)S(1)} %collective-permute-done.13.far_ref, f32[64,256]{1,0:T(8,128)S(1)} %collective-permute-done.14.core_ref, f32[64,256]{1,0:T(8,128)S(1)} %collective-permute-done.15.both_ref), custom_call_target="tpu_custom_call" | custom-call | tf_op jit(solution)/shard_map/join/pallas_call | solution.py:337
  (13 shorter events, 0.1 us)
Async XLA Ops:
  19.6 1.8 %collective-permute-start = (f32[320,256]{1,0:T(8,128)S(1)}, f32[320,256]{1,0:T(8,128)S(1)}, u32[]{:S(2)}, u32[]{:S(2)}) collective-permute-start(f32[320,256]{1,0:T(8,128)S(1)} %get-tuple-element.19.own_ref), channel_id=1, source_target_pairs={{0,1},{1,0},{2,3},{3,2},{4,5},{5,4},{6,7},{7,6},{8,9},{9,8},{10,11... | collective-permute-start | bytes 983048 | tf_op jit(solution)/shard_map/ppermute | solution.py:426
  21.9 7.4 %collective-permute-start.1 = (f32[160,256]{1,0:T(8,128)S(1)}, f32[160,256]{1,0:T(8,128)S(1)}, u32[]{:S(2)}, u32[]{:S(2)}) collective-permute-start(f32[160,256]{1,0:T(8,128)S(1)} %get-tuple-element.22), channel_id=1, source_target_pairs={{0,2},{1,3},{2,0},{3,1},{4,6},{5,7},{6,4},{7,5},{8,10},{9,11},{10,... | collective-permute-start | bytes 491528 | tf_op jit(solution)/shard_map/ppermute | solution.py:426
  24.9 8.0 %collective-permute-start.3 = (f32[160,256]{1,0:T(8,128)S(1)}, f32[160,256]{1,0:T(8,128)S(1)}, u32[]{:S(2)}, u32[]{:S(2)}) collective-permute-start(f32[160,256]{1,0:T(8,128)S(1)} %get-tuple-element.22), channel_id=1, source_target_pairs={{0,4},{1,5},{2,6},{3,7},{4,0},{5,1},{6,2},{7,3},{8,12},{9,13},{10,... | collective-permute-start | bytes 491528 | tf_op jit(solution)/shard_map/ppermute | solution.py:426
  26.4 7.7 %collective-permute-start.5 = (f32[160,256]{1,0:T(8,128)S(1)}, f32[160,256]{1,0:T(8,128)S(1)}, u32[]{:S(2)}, u32[]{:S(2)}) collective-permute-start(f32[160,256]{1,0:T(8,128)S(1)} %get-tuple-element.22), channel_id=1, source_target_pairs={{0,6},{1,7},{2,4},{3,5},{4,2},{5,3},{6,0},{7,1},{8,14},{9,15},{10,... | collective-permute-start | bytes 491528 | tf_op jit(solution)/shard_map/ppermute | solution.py:426
  29.4 6.2 %copy-start = (f32[256,64]{0,1:T(8,128)S(1)}, f32[256,64]{0,1:T(8,128)}, u32[]{:S(2)}) copy-start(f32[256,64]{0,1:T(8,128)} %param.9) | copy-start | bytes 196612
  32.8 1.5 %collective-permute-start.2 = (f32[160,256]{1,0:T(8,128)S(1)}, f32[160,256]{1,0:T(8,128)S(1)}, u32[]{:S(2)}, u32[]{:S(2)}) collective-permute-start(f32[160,256]{1,0:T(8,128)S(1)} %get-tuple-element.23.rest_0_), channel_id=1, source_target_pairs={{0,1},{1,0},{2,3},{3,2},{4,5},{5,4},{6,7},{7,6},{8,9},{9,8},{10,11... | collective-permute-start | bytes 491528 | tf_op jit(solution)/shard_map/ppermute | solution.py:426
  32.9 1.6 %collective-permute-start.4 = (f32[160,256]{1,0:T(8,128)S(1)}, f32[160,256]{1,0:T(8,128)S(1)}, u32[]{:S(2)}, u32[]{:S(2)}) collective-permute-start(f32[160,256]{1,0:T(8,128)S(1)} %collective-permute-done.3.rest_2_), channel_id=1, source_target_pairs={{0,1},{1,0},{2,3},{3,2},{4,5},{5,4},{6,7},{7,6},{8,9},{9,8},{10,11... | collective-permute-start | bytes 491528 | tf_op jit(solution)/shard_map/ppermute | solution.py:426
  34.1 1.4 %collective-permute-start.6 = (f32[160,256]{1,0:T(8,128)S(1)}, f32[160,256]{1,0:T(8,128)S(1)}, u32[]{:S(2)}, u32[]{:S(2)}) collective-permute-start(f32[160,256]{1,0:T(8,128)S(1)} %collective-permute-done.5.rest_4_), channel_id=1, source_target_pairs={{0,1},{1,0},{2,3},{3,2},{4,5},{5,4},{6,7},{7,6},{8,9},{9,8},{10,11... | collective-permute-start | bytes 491528 | tf_op jit(solution)/shard_map/ppermute | solution.py:426
  36.4 6.6 %collective-permute-start.7 = (f32[64,256]{1,0:T(8,128)S(1)}, f32[64,256]{1,0:T(8,128)S(1)}, u32[]{:S(2)}, u32[]{:S(2)}) collective-permute-start(f32[64,256]{1,0:T(8,128)S(1)} %top.1), channel_id=1, source_target_pairs={{0,8},{1,9},{2,10},{3,11},{4,12},{5,13},{6,14},{7,15},{8,0},{9,1},... | collective-permute-start | bytes 196616 | tf_op jit(solution)/shard_map/ppermute | solution.py:426
  49.0 1.4 %collective-permute-start.8 = (f32[128,256]{1,0:T(8,128)S(1)}, f32[128,256]{1,0:T(8,128)S(1)}, u32[]{:S(2)}, u32[]{:S(2)}) collective-permute-start(f32[128,256]{1,0:T(8,128)S(1)} %get-tuple-element.33), channel_id=1, source_target_pairs={{0,1},{1,0},{2,3},{3,2},{4,5},{5,4},{6,7},{7,6},{8,9},{9,8},{10,11... | collective-permute-start | bytes 393224 | tf_op jit(solution)/shard_map/ppermute | solution.py:426
  50.4 4.3 %collective-permute-start.9 = (f32[64,256]{1,0:T(8,128)S(1)}, f32[64,256]{1,0:T(8,128)S(1)}, u32[]{:S(2)}, u32[]{:S(2)}) collective-permute-start(f32[64,256]{1,0:T(8,128)S(1)} %get-tuple-element.35), channel_id=1, source_target_pairs={{0,2},{1,3},{2,0},{3,1},{4,6},{5,7},{6,4},{7,5},{8,10},{9,11},{10,... | collective-permute-start | bytes 196616 | tf_op jit(solution)/shard_map/ppermute | solution.py:426
  54.8 6.3 %collective-permute-start.12 = (f32[64,256]{1,0:T(8,128)S(1)}, f32[64,256]{1,0:T(8,128)S(1)}, u32[]{:S(2)}, u32[]{:S(2)}) collective-permute-start(f32[64,256]{1,0:T(8,128)S(1)} %add.12), channel_id=1, source_target_pairs={{0,12},{1,13},{2,14},{3,15},{4,8},{5,9},{6,10},{7,11},{8,4},{9,5},... | collective-permute-start | bytes 196616 | tf_op jit(solution)/shard_map/ppermute | solution.py:426
  58.3 5.2 %collective-permute-start.11 = (f32[64,256]{1,0:T(8,128)S(1)}, f32[64,256]{1,0:T(8,128)S(1)}, u32[]{:S(2)}, u32[]{:S(2)}) collective-permute-start(f32[64,256]{1,0:T(8,128)S(1)} %add.12), channel_id=1, source_target_pairs={{0,8},{1,9},{2,10},{3,11},{4,12},{5,13},{6,14},{7,15},{8,0},{9,1},... | collective-permute-start | bytes 196616 | tf_op jit(solution)/shard_map/ppermute | solution.py:426
  58.3 5.5 %collective-permute-start.10 = (f32[64,256]{1,0:T(8,128)S(1)}, f32[64,256]{1,0:T(8,128)S(1)}, u32[]{:S(2)}, u32[]{:S(2)}) collective-permute-start(f32[64,256]{1,0:T(8,128)S(1)} %add.12), channel_id=1, source_target_pairs={{0,4},{1,5},{2,6},{3,7},{4,0},{5,1},{6,2},{7,3},{8,12},{9,13},{10,... | collective-permute-start | bytes 196616 | tf_op jit(solution)/shard_map/ppermute | solution.py:426
  63.8 4.3 %collective-permute-start.13 = (f32[64,256]{1,0:T(8,128)S(1)}, f32[64,256]{1,0:T(8,128)S(1)}, u32[]{:S(2)}, u32[]{:S(2)}) collective-permute-start(f32[64,256]{1,0:T(8,128)S(1)} %add_add_fusion.own_ref), channel_id=1, source_target_pairs={{0,2},{1,3},{2,0},{3,1},{4,6},{5,7},{6,4},{7,5},{8,10},{9,11},{10,... | collective-permute-start | bytes 196616 | tf_op jit(solution)/shard_map/ppermute | solution.py:426
  65.6 2.6 %collective-permute-start.14 = (f32[64,256]{1,0:T(8,128)S(1)}, f32[64,256]{1,0:T(8,128)S(1)}, u32[]{:S(2)}, u32[]{:S(2)}) collective-permute-start(f32[64,256]{1,0:T(8,128)S(1)} %add_add_fusion.own_ref), channel_id=1, source_target_pairs={{0,1},{1,0},{2,3},{3,2},{4,5},{5,4},{6,7},{7,6},{8,9},{9,8},{10,11... | collective-permute-start | bytes 196616 | tf_op jit(solution)/shard_map/ppermute | solution.py:426
  68.2 1.3 %collective-permute-start.15 = (f32[64,256]{1,0:T(8,128)S(1)}, f32[64,256]{1,0:T(8,128)S(1)}, u32[]{:S(2)}, u32[]{:S(2)}) collective-permute-start(f32[64,256]{1,0:T(8,128)S(1)} %collective-permute-done.13.far_ref), channel_id=1, source_target_pairs={{0,1},{1,0},{2,3},{3,2},{4,5},{5,4},{6,7},{7,6},{8,9},{9,8},{10,11... | collective-permute-start | bytes 196616 | tf_op jit(solution)/shard_map/ppermute | solution.py:426

commit v7 on v6

--- a/solution.py
+++ b/solution.py
@@ -125,9 +125,10 @@
     map_ref[...] = maps[0]
 
 
-def marks_kernel(raw_ref, in_hbm, _, zh_ref, zl_ref, zu_ref, flip_ref, __, in_ref, sem):
+def marks_kernel(raw_ref, in_hbm, own_ref, other_ref, _, zh_ref, zl_ref, zu_ref, flip_ref, pair_ref, __, in_ref, sem):
     fetch = pltpu.make_async_copy(in_hbm, in_ref, sem)
     fetch.start()
+    ordered(1, own_ref, other_ref, pair_ref)
     count, rows, width = raw_ref.shape
     marks = count // CHUNKS
     suffix = None
@@ -177,9 +178,19 @@
         out_ref[...] = compose(own_ref[...], other_ref[...], width)
 
 
-def pair_kernel(own_ref, other_ref, out_ref, half_ref):
-    ordered(1, own_ref, other_ref, out_ref)
-    half_ref[...] = core_half(out_ref)
+def pair_kernel(own_ref, other_ref, half_ref):
+    half, width = half_ref.shape
+    first = early(1)
+
+    @pl.when(first)
+    def _():
+        half_ref[...] = mm3(other_ref[:half], *split(own_ref[:width]))
+
+    @pl.when(jnp.logical_not(first))
+    def _():
+        out = mm3(own_ref[half:], *split(other_ref[:width]))
+        edge = width - half
+        half_ref[...] = jnp.concatenate([out[:edge], out[edge:] + other_ref[width:]], axis=0)
 
 
 def position(low_bit, count):
@@ -263,6 +274,12 @@
     def send(at):
         return pltpu.make_async_copy(low_ref.at[at], adj_hbm.at[:, at], sems.at[at])
 
+    pack = 4
+
+    def tail(p):
+        part = pl.ds(p, pack)
+        return pltpu.make_async_copy(low_ref.at[1, part], adj_hbm.at[part, 1], sems.at[SEG + p // pack])
+
     for j in range(count):
         both = mm(v_both, zh_ref[j])
         z = both[:cols] + both[cols:] + mm(v_high, zl_ref[j]) + zu_ref[j]
@@ -272,7 +289,6 @@
     cur[count - 1] = v
     send(0).start()
     grad = mm(flip_ref[0], low_ref[0].reshape(count * cols, width))
-    pack = 4
     for s in range(SEG - 1):
         at = SEG - 1 - s
         for p in range(0, count, pack):
@@ -284,7 +300,10 @@
                 value = out[(m - p) * cols : (m - p + 1) * cols] + f_ref[m * SEG + at].astype(F32)
                 cur[m] = value
                 low_ref[at, m] = value.astype(BF16)
-        send(at).start()
+            if at == 1:
+                tail(p).start()
+        if at > 1:
+            send(at).start()
         grad = grad + mm(flip_ref[at], low_ref[at].reshape(count * cols, width))
     grad = grad.T
     half = width // 2
@@ -292,7 +311,10 @@
     keep_ref[...] = jnp.where(first, grad[:half], grad[half:])
     give_ref[...] = jnp.where(first, grad[half:], grad[:half])
     for at in range(SEG):
-        send(at).wait()
+        if at != 1:
+            send(at).wait()
+    for p in range(0, count, pack):
+        tail(p).wait()
 
 
 def halve_kernel(bit, keep_ref, got_ref, mine_ref, give_ref):
@@ -370,7 +392,7 @@
     )
 
 
-def mark_maps(raw, ins, through):
+def mark_maps(raw, ins, own, other, through):
     count, rows, width = raw.shape
     steps, cols, feats = ins.shape
     return call(
@@ -381,12 +403,15 @@
             VM((count, width, width), BF16),
             VM((count, rows - width, width), F32),
             VM((SEG, feats, steps // SEG * cols), BF16),
+            VM((rows, width), F32),
             VM(through.shape, F32),
         ),
         raw,
         ins,
+        own,
+        other,
         through,
-        alias={2: 4},
+        alias={4: 5},
         where={1},
         scratch=[VM(ins.shape, BF16), pltpu.SemaphoreType.DMA],
         flops=6 * count * rows * width * width,
@@ -410,7 +435,7 @@
         scratch=[
             VM((segs, cols, width), F32),
             VM((SEG, segs, cols, width), BF16),
-            pltpu.SemaphoreType.DMA((SEG,)),
+            pltpu.SemaphoreType.DMA((SEG + segs // 4,)),
         ],
         flops=8 * steps * cols * width * width,
     )
@@ -434,14 +459,14 @@
     whole = VM(own.shape, F32)
     half = VM((rows // 2, width), F32)
     other = swap(own, 1)
-    total, piece = call(pair_kernel, "pair", (whole, half), own, other, flops=flops)
+    (piece,) = call(pair_kernel, "pair", (half,), own, other, flops=flops // 2)
     (later,) = call(functools.partial(first_later_kernel, 1), "later", (whole,), other)
     bit = 2
     while bit < n // 2:
         count = 4 if 4 * bit <= n // 2 else 2
         mine = [swap(piece, mask * bit) for mask in range(1, count)]
         if bit == 2:
-            *marks, mine[0] = aside(mine[0])
+            *marks, total, mine[0] = aside(own, other, mine[0])
         halves = [x for got in mine for x in (got, swap(got, 1))]
         maps = [VM((count, rows, width), F32)]
         if count * bit < n // 2:
@@ -471,7 +496,7 @@
     bit = 2 * near
     while bit < n:
         count = 4 if 4 * bit <= n else 2
-        others = [swap(x, mask * bit) for mask in range(1, count)]
+        others = [swap(x, mask * bit) for mask in range(count - 1, 0, -1)]
         x = sum(others, x)
         bit *= count
     far = swap(x, near)

time: 70.5 us -> 70.1 us (level)
  transfers between devices with their start and end apart: 16 -> 16, of which waited for: 14 -> 14; matrix products, arithmetic and copies ran while one was open for 0% -> 0% of each run, Pallas kernels for 6% -> 7%
where the time goes in v7:
time: 70.1 us; the launch traced here: 69.9 us
  Pallas kernels  31.5 us (45%)
  waiting for transfers between devices  21.2 us (30%)
  starting transfers between devices  16.4 us (23%)
  between operations  0.89 us (1%)
    pallas_call x9, Pallas kernels, call(): pl.pallas_call(kernel, out_shape=tuple(out), in_specs=ins, out_specs=outs...  31.5 us
    ppermute x16, waiting for transfers between devices, swap(): return lax.ppermute(x, 'tm', [(i, i ^ bit) for i in range(n)])  21.2 us
    ppermute x16, starting transfers between devices, swap(): return lax.ppermute(x, 'tm', [(i, i ^ bit) for i in range(n)])  16.4 us
  transfers between devices with their start and end apart: 16, of which 14 were waited for; matrix products, arithmetic and copies ran while one was open for 0% of the time, Pallas kernels for 7%

profile of v7, /device:TPU:0, one launch (start us, length us, event | category | flops | bytes accessed | tf_op | source)
XLA Modules:
  0.0 69.9 jit_solution(10393638456959517602)
XLA Ops:
  0.6 19.0 %build.1 = (f32[320,256]{1,0:T(8,128)S(1)}, f32[16,320,256]{2,1,0:T(8,128)S(1)}, bf16[2,256,256]{2,1,0:T(8,128)(2,1)S(1)}, f32[128,256]{1,0:T(8,128)S(1)}, bf16[128,64,256]{2,1,0:T(8,128)(2,1)S(1)}) custom-call(f32[256,256]{1,0:T(8,128)} %gen_hbm.1, f32[128,256]{1,0:T(8,128)} %d_hbm.1, bf16[128,64,256]{2,1,0:T(8,128)(2,1)} %bitcast.9), custom_call_target="tpu_custom_call" | custom-call | flops 16106127360 | tf_op jit(solution)/shard_map/build/pallas_call | solution.py:359
  19.6 0.5 collective-permute-start
  20.2 1.3 %collective-permute-done.other_ref = f32[320,256]{1,0:T(8,128)S(1)} collective-permute-done((f32[320,256]{1,0:T(8,128)S(1)}, f32[320,256]{1,0:T(8,128)S(1)}, u32[]{:S(2)}, u32[]{:S(2)}) %collective-permute-start) | collective-permute-done | bytes 327712 | tf_op jit(solution)/shard_map/ppermute | solution.py:451
  21.4 0.2 pair.1
  21.7 2.9 %collective-permute-start.1 = (f32[160,256]{1,0:T(8,128)S(1)}, f32[160,256]{1,0:T(8,128)S(1)}, u32[]{:S(2)}, u32[]{:S(2)}) collective-permute-start(f32[160,256]{1,0:T(8,128)S(1)} %pair.1), channel_id=1, source_target_pairs={{0,2},{1,3},{2,0},{3,1},{4,6},{5,7},{6,4},{7,5},{8,10},{9,11},{10,... | collective-permute-start | bytes 491528 | tf_op jit(solution)/shard_map/ppermute | solution.py:451
  24.6 1.6 %collective-permute-start.3 = (f32[160,256]{1,0:T(8,128)S(1)}, f32[160,256]{1,0:T(8,128)S(1)}, u32[]{:S(2)}, u32[]{:S(2)}) collective-permute-start(f32[160,256]{1,0:T(8,128)S(1)} %pair.1), channel_id=1, source_target_pairs={{0,4},{1,5},{2,6},{3,7},{4,0},{5,1},{6,2},{7,3},{8,12},{9,13},{10,... | collective-permute-start | bytes 491528 | tf_op jit(solution)/shard_map/ppermute | solution.py:451
  26.2 2.9 %collective-permute-done.1._ = f32[160,256]{1,0:T(8,128)S(1)} collective-permute-done((f32[160,256]{1,0:T(8,128)S(1)}, f32[160,256]{1,0:T(8,128)S(1)}, u32[]{:S(2)}, u32[]{:S(2)}) %collective-permute-start.1) | collective-permute-done | bytes 163872 | tf_op jit(solution)/shard_map/ppermute | solution.py:451
  29.1 3.8 %marks.1 = (bf16[16,256,256]{2,1,0:T(8,128)(2,1)S(1)}, bf16[16,256,256]{2,1,0:T(8,128)(2,1)S(1)}, f32[16,64,256]{2,1,0:T(8,128)S(1)}, bf16[8,256,1024]{2,1,0:T(8...) custom-call(f32[16,320,256]{2,1,0:T(8,128)S(1)} %get-tuple-element.18.raw_ref, ...), custom_call_target="tpu_custom_call", output_to_operand_aliasing={{5}: (4, {})} | custom-call | flops 2013265920 | bytes 15000000 | tf_op jit(solution)/shard_map/marks/pallas_call | solution.py:359
  32.9 0.1 collective-permute-start.2
  33.0 0.5 collective-permute-start.4
  33.5 0.4 collective-permute-done.5.rest_4_
  33.9 0.5 collective-permute-done.2.rest_1_
  34.3 0.2 collective-permute-done.4.rest_3_
  34.6 0.7 collective-permute-done.6.rest_5_
  35.3 0.8 %top.1 = f32[64,256]{1,0:T(8,128)S(1)} custom-call(f32[320,256]{1,0:T(8,128)S(1)} %get-tuple-element.20.own_ref, f32[64,256]{1,0:T(8,128)S(1)} %bitcast.6, f32[160,256]{1,0:T(8,128)S(1)} %get-tuple-element.21.rest_0_, f32[160,256]{1,0:T(8,128)S(1)} %collective-permute-done.2.rest_1_, f32[160,256]{1,0:T(8,128)S(1)} %collective-permute-done.3.rest_2_, ...), custom_call_target="tpu_custom_call" | custom-call | flops 100663296 | tf_op jit(solution)/shard_map/top/pallas_call | solution.py:359
  36.1 2.8 %collective-permute-start.7 = (f32[64,256]{1,0:T(8,128)S(1)}, f32[64,256]{1,0:T(8,128)S(1)}, u32[]{:S(2)}, u32[]{:S(2)}) collective-permute-start(f32[64,256]{1,0:T(8,128)S(1)} %top.1), channel_id=1, source_target_pairs={{0,8},{1,9},{2,10},{3,11},{4,12},{5,13},{6,14},{7,15},{8,0},{9,1},... | collective-permute-start | bytes 196616 | tf_op jit(solution)/shard_map/ppermute | solution.py:451
  38.9 1.0 %later.3.later_ref = f32[320,256]{1,0:T(8,128)S(1)} custom-call(f32[320,256]{1,0:T(8,128)S(1)} %later.2.later_ref, f32[160,256]{1,0:T(8,128)S(1)} %get-tuple-element.21.rest_0_, f32[160,256]{1,0:T(8,128)S(1)} %collective-permute-done.2.rest_1_, f32[160,256]{1,0:T(8,128)S(1)} %collective-permute-done.3.rest_2_, ...), custom_call_target="tpu_custom_call" | custom-call | flops 503316480 | tf_op jit(solution)/shard_map/later/pallas_call | solution.py:359
  40.0 2.8 %collective-permute-done.7.got_ref = f32[64,256]{1,0:T(8,128)S(1)} collective-permute-done((f32[64,256]{1,0:T(8,128)S(1)}, f32[64,256]{1,0:T(8,128)S(1)}, u32[]{:S(2)}, u32[]{:S(2)}) %collective-permute-start.7) | collective-permute-done | bytes 65568 | tf_op jit(solution)/shard_map/ppermute | solution.py:451
  42.7 5.9 %sweep.1 = (bf16[16,8,64,256]{3,2,1,0:T(8,128)(2,1)}, f32[128,256]{1,0:T(8,128)S(1)}, f32[128,256]{1,0:T(8,128)S(1)}) custom-call(f32[64,256]{1,0:T(8,128)S(1)} %bitcast.7, f32[64,256]{1,0:T(8,128)S(1)} %collective-permute-done.7.got_ref, f32[320,256]{1,0:T(8,128)S(1)} %later.3.later_ref, bf16[16,256,256]{2,1,0:T(8,128)(2,1)S(1)} %get-tuple-element.22.zh_ref, ...), custom_call_target="tpu_custom_call" | custom-call | flops 4294967296 | tf_op jit(solution)/shard_map/sweep/pallas_call | solution.py:359
  48.6 0.1 collective-permute-start.8
  48.7 1.3 %collective-permute-done.8.got_ref = f32[128,256]{1,0:T(8,128)S(1)} collective-permute-done((f32[128,256]{1,0:T(8,128)S(1)}, f32[128,256]{1,0:T(8,128)S(1)}, u32[]{:S(2)}, u32[]{:S(2)}) %collective-permute-start.8) | collective-permute-done | bytes 131104 | tf_op jit(solution)/shard_map/ppermute | solution.py:451
  50.0 1.7 %collective-permute-start.9 = (f32[64,256]{1,0:T(8,128)S(1)}, f32[64,256]{1,0:T(8,128)S(1)}, u32[]{:S(2)}, u32[]{:S(2)}) collective-permute-start(f32[64,256]{1,0:T(8,128)S(1)} %get-tuple-element.33), channel_id=1, source_target_pairs={{0,2},{1,3},{2,0},{3,1},{4,6},{5,7},{6,4},{7,5},{8,10},{9,11},{10,... | collective-permute-start | bytes 196616 | tf_op jit(solution)/shard_map/ppermute | solution.py:451
  51.8 2.6 %collective-permute-done.9 = f32[64,256]{1,0:T(8,128)S(1)} collective-permute-done((f32[64,256]{1,0:T(8,128)S(1)}, f32[64,256]{1,0:T(8,128)S(1)}, u32[]{:S(2)}, u32[]{:S(2)}) %collective-permute-start.9) | collective-permute-done | bytes 65568 | tf_op jit(solution)/shard_map/ppermute | solution.py:451
  54.4 3.6 %collective-permute-start.10 = (f32[64,256]{1,0:T(8,128)S(1)}, f32[64,256]{1,0:T(8,128)S(1)}, u32[]{:S(2)}, u32[]{:S(2)}) collective-permute-start(f32[64,256]{1,0:T(8,128)S(1)} %add.12), channel_id=1, source_target_pairs={{0,12},{1,13},{2,14},{3,15},{4,8},{5,9},{6,10},{7,11},{8,4},{9,5},... | collective-permute-start | bytes 196616 | tf_op jit(solution)/shard_map/ppermute | solution.py:451
  58.0 0.9 %collective-permute-start.12 = (f32[64,256]{1,0:T(8,128)S(1)}, f32[64,256]{1,0:T(8,128)S(1)}, u32[]{:S(2)}, u32[]{:S(2)}) collective-permute-start(f32[64,256]{1,0:T(8,128)S(1)} %add.12), channel_id=1, source_target_pairs={{0,4},{1,5},{2,6},{3,7},{4,0},{5,1},{6,2},{7,3},{8,12},{9,13},{10,... | collective-permute-start | bytes 196616 | tf_op jit(solution)/shard_map/ppermute | solution.py:451
  58.8 1.8 %collective-permute-done.10 = f32[64,256]{1,0:T(8,128)S(1)} collective-permute-done((f32[64,256]{1,0:T(8,128)S(1)}, f32[64,256]{1,0:T(8,128)S(1)}, u32[]{:S(2)}, u32[]{:S(2)}) %collective-permute-start.10) | collective-permute-done | bytes 65568 | tf_op jit(solution)/shard_map/ppermute | solution.py:451
  60.7 2.5 %collective-permute-done.11 = f32[64,256]{1,0:T(8,128)S(1)} collective-permute-done((f32[64,256]{1,0:T(8,128)S(1)}, f32[64,256]{1,0:T(8,128)S(1)}, u32[]{:S(2)}, u32[]{:S(2)}) %collective-permute-start.11) | collective-permute-done | bytes 65568 | tf_op jit(solution)/shard_map/ppermute | solution.py:451
  63.2 0.3 collective-permute-done.12
  63.5 1.7 %collective-permute-start.13 = (f32[64,256]{1,0:T(8,128)S(1)}, f32[64,256]{1,0:T(8,128)S(1)}, u32[]{:S(2)}, u32[]{:S(2)}) collective-permute-start(f32[64,256]{1,0:T(8,128)S(1)} %add_add_fusion.own_ref), channel_id=1, source_target_pairs={{0,2},{1,3},{2,0},{3,1},{4,6},{5,7},{6,4},{7,5},{8,10},{9,11},{10,... | collective-permute-start | bytes 196616 | tf_op jit(solution)/shard_map/ppermute | solution.py:451
  65.2 2.6 %collective-permute-done.13.far_ref = f32[64,256]{1,0:T(8,128)S(1)} collective-permute-done((f32[64,256]{1,0:T(8,128)S(1)}, f32[64,256]{1,0:T(8,128)S(1)}, u32[]{:S(2)}, u32[]{:S(2)}) %collective-permute-start.13) | collective-permute-done | bytes 65568 | tf_op jit(solution)/shard_map/ppermute | solution.py:451
  67.8 1.2 %collective-permute-done.15.both_ref = f32[64,256]{1,0:T(8,128)S(1)} collective-permute-done((f32[64,256]{1,0:T(8,128)S(1)}, f32[64,256]{1,0:T(8,128)S(1)}, u32[]{:S(2)}, u32[]{:S(2)}) %collective-permute-start.15) | collective-permute-done | bytes 65568 | tf_op jit(solution)/shard_map/ppermute | solution.py:451
  69.1 0.7 %join.1 = f32[256,256]{1,0:T(8,128)} custom-call(f32[64,256]{1,0:T(8,128)S(1)} %add_add_fusion.own_ref, f32[64,256]{1,0:T(8,128)S(1)} %collective-permute-done.13.far_ref, f32[64,256]{1,0:T(8,128)S(1)} %collective-permute-done.14.core_ref, f32[64,256]{1,0:T(8,128)S(1)} %collective-permute-done.15.both_ref), custom_call_target="tpu_custom_call" | custom-call | tf_op jit(solution)/shard_map/join/pallas_call | solution.py:359
  (13 shorter events, 0.1 us)
Async XLA Ops:
  19.6 1.8 %collective-permute-start = (f32[320,256]{1,0:T(8,128)S(1)}, f32[320,256]{1,0:T(8,128)S(1)}, u32[]{:S(2)}, u32[]{:S(2)}) collective-permute-start(f32[320,256]{1,0:T(8,128)S(1)} %get-tuple-element.19.own_ref), channel_id=1, source_target_pairs={{0,1},{1,0},{2,3},{3,2},{4,5},{5,4},{6,7},{7,6},{8,9},{9,8},{10,11... | collective-permute-start | bytes 983048 | tf_op jit(solution)/shard_map/ppermute | solution.py:451
  21.7 7.4 %collective-permute-start.1 = (f32[160,256]{1,0:T(8,128)S(1)}, f32[160,256]{1,0:T(8,128)S(1)}, u32[]{:S(2)}, u32[]{:S(2)}) collective-permute-start(f32[160,256]{1,0:T(8,128)S(1)} %pair.1), channel_id=1, source_target_pairs={{0,2},{1,3},{2,0},{3,1},{4,6},{5,7},{6,4},{7,5},{8,10},{9,11},{10,... | collective-permute-start | bytes 491528 | tf_op jit(solution)/shard_map/ppermute | solution.py:451
  24.6 8.4 %collective-permute-start.3 = (f32[160,256]{1,0:T(8,128)S(1)}, f32[160,256]{1,0:T(8,128)S(1)}, u32[]{:S(2)}, u32[]{:S(2)}) collective-permute-start(f32[160,256]{1,0:T(8,128)S(1)} %pair.1), channel_id=1, source_target_pairs={{0,4},{1,5},{2,6},{3,7},{4,0},{5,1},{6,2},{7,3},{8,12},{9,13},{10,... | collective-permute-start | bytes 491528 | tf_op jit(solution)/shard_map/ppermute | solution.py:451
  26.2 7.7 %collective-permute-start.5 = (f32[160,256]{1,0:T(8,128)S(1)}, f32[160,256]{1,0:T(8,128)S(1)}, u32[]{:S(2)}, u32[]{:S(2)}) collective-permute-start(f32[160,256]{1,0:T(8,128)S(1)} %pair.1), channel_id=1, source_target_pairs={{0,6},{1,7},{2,4},{3,5},{4,2},{5,3},{6,0},{7,1},{8,14},{9,15},{10,... | collective-permute-start | bytes 491528 | tf_op jit(solution)/shard_map/ppermute | solution.py:451
  29.1 6.2 %copy-start = (f32[256,64]{0,1:T(8,128)S(1)}, f32[256,64]{0,1:T(8,128)}, u32[]{:S(2)}) copy-start(f32[256,64]{0,1:T(8,128)} %param.9) | copy-start | bytes 196612
  32.9 1.5 %collective-permute-start.2 = (f32[160,256]{1,0:T(8,128)S(1)}, f32[160,256]{1,0:T(8,128)S(1)}, u32[]{:S(2)}, u32[]{:S(2)}) collective-permute-start(f32[160,256]{1,0:T(8,128)S(1)} %get-tuple-element.21.rest_0_), channel_id=1, source_target_pairs={{0,1},{1,0},{2,3},{3,2},{4,5},{5,4},{6,7},{7,6},{8,9},{9,8},{10,11... | collective-permute-start | bytes 491528 | tf_op jit(solution)/shard_map/ppermute | solution.py:451
  33.0 1.6 %collective-permute-start.4 = (f32[160,256]{1,0:T(8,128)S(1)}, f32[160,256]{1,0:T(8,128)S(1)}, u32[]{:S(2)}, u32[]{:S(2)}) collective-permute-start(f32[160,256]{1,0:T(8,128)S(1)} %collective-permute-done.3.rest_2_), channel_id=1, source_target_pairs={{0,1},{1,0},{2,3},{3,2},{4,5},{5,4},{6,7},{7,6},{8,9},{9,8},{10,11... | collective-permute-start | bytes 491528 | tf_op jit(solution)/shard_map/ppermute | solution.py:451
  33.9 1.4 %collective-permute-start.6 = (f32[160,256]{1,0:T(8,128)S(1)}, f32[160,256]{1,0:T(8,128)S(1)}, u32[]{:S(2)}, u32[]{:S(2)}) collective-permute-start(f32[160,256]{1,0:T(8,128)S(1)} %collective-permute-done.5.rest_4_), channel_id=1, source_target_pairs={{0,1},{1,0},{2,3},{3,2},{4,5},{5,4},{6,7},{7,6},{8,9},{9,8},{10,11... | collective-permute-start | bytes 491528 | tf_op jit(solution)/shard_map/ppermute | solution.py:451
  36.1 6.6 %collective-permute-start.7 = (f32[64,256]{1,0:T(8,128)S(1)}, f32[64,256]{1,0:T(8,128)S(1)}, u32[]{:S(2)}, u32[]{:S(2)}) collective-permute-start(f32[64,256]{1,0:T(8,128)S(1)} %top.1), channel_id=1, source_target_pairs={{0,8},{1,9},{2,10},{3,11},{4,12},{5,13},{6,14},{7,15},{8,0},{9,1},... | collective-permute-start | bytes 196616 | tf_op jit(solution)/shard_map/ppermute | solution.py:451
  48.6 1.4 %collective-permute-start.8 = (f32[128,256]{1,0:T(8,128)S(1)}, f32[128,256]{1,0:T(8,128)S(1)}, u32[]{:S(2)}, u32[]{:S(2)}) collective-permute-start(f32[128,256]{1,0:T(8,128)S(1)} %get-tuple-element.31), channel_id=1, source_target_pairs={{0,1},{1,0},{2,3},{3,2},{4,5},{5,4},{6,7},{7,6},{8,9},{9,8},{10,11... | collective-permute-start | bytes 393224 | tf_op jit(solution)/shard_map/ppermute | solution.py:451
  50.0 4.3 %collective-permute-start.9 = (f32[64,256]{1,0:T(8,128)S(1)}, f32[64,256]{1,0:T(8,128)S(1)}, u32[]{:S(2)}, u32[]{:S(2)}) collective-permute-start(f32[64,256]{1,0:T(8,128)S(1)} %get-tuple-element.33), channel_id=1, source_target_pairs={{0,2},{1,3},{2,0},{3,1},{4,6},{5,7},{6,4},{7,5},{8,10},{9,11},{10,... | collective-permute-start | bytes 196616 | tf_op jit(solution)/shard_map/ppermute | solution.py:451
  54.4 6.3 %collective-permute-start.10 = (f32[64,256]{1,0:T(8,128)S(1)}, f32[64,256]{1,0:T(8,128)S(1)}, u32[]{:S(2)}, u32[]{:S(2)}) collective-permute-start(f32[64,256]{1,0:T(8,128)S(1)} %add.12), channel_id=1, source_target_pairs={{0,12},{1,13},{2,14},{3,15},{4,8},{5,9},{6,10},{7,11},{8,4},{9,5},... | collective-permute-start | bytes 196616 | tf_op jit(solution)/shard_map/ppermute | solution.py:451
  57.9 5.2 %collective-permute-start.11 = (f32[64,256]{1,0:T(8,128)S(1)}, f32[64,256]{1,0:T(8,128)S(1)}, u32[]{:S(2)}, u32[]{:S(2)}) collective-permute-start(f32[64,256]{1,0:T(8,128)S(1)} %add.12), channel_id=1, source_target_pairs={{0,8},{1,9},{2,10},{3,11},{4,12},{5,13},{6,14},{7,15},{8,0},{9,1},... | collective-permute-start | bytes 196616 | tf_op jit(solution)/shard_map/ppermute | solution.py:451
  58.0 5.5 %collective-permute-start.12 = (f32[64,256]{1,0:T(8,128)S(1)}, f32[64,256]{1,0:T(8,128)S(1)}, u32[]{:S(2)}, u32[]{:S(2)}) collective-permute-start(f32[64,256]{1,0:T(8,128)S(1)} %add.12), channel_id=1, source_target_pairs={{0,4},{1,5},{2,6},{3,7},{4,0},{5,1},{6,2},{7,3},{8,12},{9,13},{10,... | collective-permute-start | bytes 196616 | tf_op jit(solution)/shard_map/ppermute | solution.py:451
  63.5 4.3 %collective-permute-start.13 = (f32[64,256]{1,0:T(8,128)S(1)}, f32[64,256]{1,0:T(8,128)S(1)}, u32[]{:S(2)}, u32[]{:S(2)}) collective-permute-start(f32[64,256]{1,0:T(8,128)S(1)} %add_add_fusion.own_ref), channel_id=1, source_target_pairs={{0,2},{1,3},{2,0},{3,1},{4,6},{5,7},{6,4},{7,5},{8,10},{9,11},{10,... | collective-permute-start | bytes 196616 | tf_op jit(solution)/shard_map/ppermute | solution.py:451
  65.2 2.6 %collective-permute-start.14 = (f32[64,256]{1,0:T(8,128)S(1)}, f32[64,256]{1,0:T(8,128)S(1)}, u32[]{:S(2)}, u32[]{:S(2)}) collective-permute-start(f32[64,256]{1,0:T(8,128)S(1)} %add_add_fusion.own_ref), channel_id=1, source_target_pairs={{0,1},{1,0},{2,3},{3,2},{4,5},{5,4},{6,7},{7,6},{8,9},{9,8},{10,11... | collective-permute-start | bytes 196616 | tf_op jit(solution)/shard_map/ppermute | solution.py:451
  67.8 1.3 %collective-permute-start.15 = (f32[64,256]{1,0:T(8,128)S(1)}, f32[64,256]{1,0:T(8,128)S(1)}, u32[]{:S(2)}, u32[]{:S(2)}) collective-permute-start(f32[64,256]{1,0:T(8,128)S(1)} %collective-permute-done.13.far_ref), channel_id=1, source_target_pairs={{0,1},{1,0},{2,3},{3,2},{4,5},{5,4},{6,7},{7,6},{8,9},{9,8},{10,11... | collective-permute-start | bytes 196616 | tf_op jit(solution)/shard_map/ppermute | solution.py:451

commit v8 on v7

--- a/solution.py
+++ b/solution.py
@@ -259,6 +259,16 @@
         ).astype(F32)
 
 
+def shift_kernel(later_ref, zh_ref, zl_ref, zu_ref, outh_ref, outl_ref, outu_ref):
+    width = later_ref.shape[1]
+    for j in range(zh_ref.shape[0]):
+        out = mm3(later_ref[...], zh_ref[j], zl_ref[j])
+        outu_ref[j] = out[width:] + zu_ref[j]
+        high, low = split(out[:width])
+        outh_ref[j] = high
+        outl_ref[j] = low
+
+
 def sweep_kernel(
     bit, end_ref, got_ref, later_ref, zh_ref, zl_ref, zu_ref,
     rot_ref, d_ref, f_ref, flip_ref,
@@ -267,7 +277,7 @@
     count, width = zh_ref.shape[0], zh_ref.shape[1]
     cols = end_ref.shape[0]
     v = jnp.where(early(bit), got_ref[...], end_ref[...])
-    v = apply(v, later_ref[...], width)
+    start = apply(v, later_ref[...], width)
     v_high, v_low = split(v)
     v_both = jnp.concatenate([v_high, v_low], axis=0)
 
@@ -286,7 +296,7 @@
         if j > 0:
             cur[j - 1] = z
         low_ref[0, j] = z.astype(BF16)
-    cur[count - 1] = v
+    cur[count - 1] = start
     send(0).start()
     grad = mm(flip_ref[0], low_ref[0].reshape(count * cols, width))
     for s in range(SEG - 1):
@@ -416,6 +426,17 @@
         scratch=[VM(ins.shape, BF16), pltpu.SemaphoreType.DMA],
         flops=6 * count * rows * width * width,
         data=15_000_000,
+    )
+
+
+def shift(later, zh, zl, zu):
+    count, width, _ = zh.shape
+    return call(
+        shift_kernel,
+        "shift",
+        (VM(zh.shape, BF16), VM(zl.shape, BF16), VM(zu.shape, F32)),
+        later, zh, zl, zu,
+        flops=6 * count * later.shape[0] * width * width,
     )
 
 
@@ -496,7 +517,7 @@
     bit = 2 * near
     while bit < n:
         count = 4 if 4 * bit <= n else 2
-        others = [swap(x, mask * bit) for mask in range(count - 1, 0, -1)]
+        others = [swap(x, mask * bit) for mask in range(1, count)]
         x = sum(others, x)
         bit *= count
     far = swap(x, near)
@@ -515,6 +536,7 @@
     end = terminal.T
     own, raw, rot, derivs, force = build(generator, derivs, force)
     (zh, zl, zu, flipped), entering, later = incoming(own, end, functools.partial(mark_maps, raw, ins))
+    zh, zl, zu = shift(later, zh, zl, zu)
     adj, keep, give = sweep(entering, later, zh, zl, zu, rot, derivs, force, flipped)
     return jnp.transpose(adj, (0, 2, 1)), all_sum(keep, give)
 

time: 70.1 us -> 69.9 us (level)
  waiting for transfers between devices: 21.2 us -> 18.9 us
  Pallas kernels: 31.5 us -> 33.5 us
    ppermute x16, waiting for transfers between devices: 21.2 us -> 18.9 us  [swap(): return lax.ppermute(x, 'tm', [(i, i ^ bit) for i in range(n)])]
    pallas_call x9 -> x10, Pallas kernels: 31.5 us -> 33.5 us  [call(): pl.pallas_call(kernel, out_shape=tuple(out), in_specs=ins, out_specs=outs...]
  transfers between devices with their start and end apart: 16 -> 16, of which waited for: 14 -> 14; matrix products, arithmetic and copies ran while one was open for 0% -> 0% of each run, Pallas kernels for 7% -> 10%
where the time goes in v8:
time: 69.9 us; the launch traced here: 69.7 us
  Pallas kernels  33.5 us (48%)
  waiting for transfers between devices  18.9 us (27%)
  starting transfers between devices  16.4 us (23%)
  between operations  0.9 us (1%)
    pallas_call x10, Pallas kernels, call(): pl.pallas_call(kernel, out_shape=tuple(out), in_specs=ins, out_specs=outs...  33.5 us
    ppermute x16, waiting for transfers between devices, swap(): return lax.ppermute(x, 'tm', [(i, i ^ bit) for i in range(n)])  18.9 us
    ppermute x16, starting transfers between devices, swap(): return lax.ppermute(x, 'tm', [(i, i ^ bit) for i in range(n)])  16.4 us
  transfers between devices with their start and end apart: 16, of which 14 were waited for; matrix products, arithmetic and copies ran while one was open for 0% of the time, Pallas kernels for 10%

profile of v8, /device:TPU:0, one launch (start us, length us, event | category | flops | bytes accessed | tf_op | source)
XLA Modules:
  0.0 69.7 jit_solution(4348286453370586959)
XLA Ops:
  0.6 19.0 %build.1 = (f32[320,256]{1,0:T(8,128)S(1)}, f32[16,320,256]{2,1,0:T(8,128)S(1)}, bf16[2,256,256]{2,1,0:T(8,128)(2,1)S(1)}, f32[128,256]{1,0:T(8,128)S(1)}, bf16[128,64,256]{2,1,0:T(8,128)(2,1)S(1)}) custom-call(f32[256,256]{1,0:T(8,128)} %gen_hbm.1, f32[128,256]{1,0:T(8,128)} %d_hbm.1, bf16[128,64,256]{2,1,0:T(8,128)(2,1)} %bitcast.9), custom_call_target="tpu_custom_call" | custom-call | flops 16106127360 | tf_op jit(solution)/shard_map/build/pallas_call | solution.py:369
  19.6 0.5 collective-permute-start
  20.2 1.3 %collective-permute-done.other_ref = f32[320,256]{1,0:T(8,128)S(1)} collective-permute-done((f32[320,256]{1,0:T(8,128)S(1)}, f32[320,256]{1,0:T(8,128)S(1)}, u32[]{:S(2)}, u32[]{:S(2)}) %collective-permute-start) | collective-permute-done | bytes 327712 | tf_op jit(solution)/shard_map/ppermute | solution.py:472
  21.4 0.2 pair.1
  21.7 2.9 %collective-permute-start.1 = (f32[160,256]{1,0:T(8,128)S(1)}, f32[160,256]{1,0:T(8,128)S(1)}, u32[]{:S(2)}, u32[]{:S(2)}) collective-permute-start(f32[160,256]{1,0:T(8,128)S(1)} %pair.1), channel_id=1, source_target_pairs={{0,2},{1,3},{2,0},{3,1},{4,6},{5,7},{6,4},{7,5},{8,10},{9,11},{10,... | collective-permute-start | bytes 491528 | tf_op jit(solution)/shard_map/ppermute | solution.py:472
  24.6 1.6 %collective-permute-start.3 = (f32[160,256]{1,0:T(8,128)S(1)}, f32[160,256]{1,0:T(8,128)S(1)}, u32[]{:S(2)}, u32[]{:S(2)}) collective-permute-start(f32[160,256]{1,0:T(8,128)S(1)} %pair.1), channel_id=1, source_target_pairs={{0,4},{1,5},{2,6},{3,7},{4,0},{5,1},{6,2},{7,3},{8,12},{9,13},{10,... | collective-permute-start | bytes 491528 | tf_op jit(solution)/shard_map/ppermute | solution.py:472
  26.2 2.9 %collective-permute-done.1._ = f32[160,256]{1,0:T(8,128)S(1)} collective-permute-done((f32[160,256]{1,0:T(8,128)S(1)}, f32[160,256]{1,0:T(8,128)S(1)}, u32[]{:S(2)}, u32[]{:S(2)}) %collective-permute-start.1) | collective-permute-done | bytes 163872 | tf_op jit(solution)/shard_map/ppermute | solution.py:472
  29.1 3.8 %marks.1 = (bf16[16,256,256]{2,1,0:T(8,128)(2,1)S(1)}, bf16[16,256,256]{2,1,0:T(8,128)(2,1)S(1)}, f32[16,64,256]{2,1,0:T(8,128)S(1)}, bf16[8,256,1024]{2,1,0:T(8...) custom-call(f32[16,320,256]{2,1,0:T(8,128)S(1)} %get-tuple-element.21.raw_ref, ...), custom_call_target="tpu_custom_call", output_to_operand_aliasing={{5}: (4, {})} | custom-call | flops 2013265920 | bytes 15000000 | tf_op jit(solution)/shard_map/marks/pallas_call | solution.py:369
  32.9 0.1 collective-permute-start.2
  33.0 0.5 collective-permute-start.4
  33.5 0.4 collective-permute-done.5.rest_4_
  33.9 0.4 collective-permute-done.2.rest_1_
  34.3 0.2 collective-permute-done.4.rest_3_
  34.6 0.7 collective-permute-done.6.rest_5_
  35.3 0.8 %top.1 = f32[64,256]{1,0:T(8,128)S(1)} custom-call(f32[320,256]{1,0:T(8,128)S(1)} %get-tuple-element.23.own_ref, f32[64,256]{1,0:T(8,128)S(1)} %bitcast.6, f32[160,256]{1,0:T(8,128)S(1)} %get-tuple-element.24.rest_0_, f32[160,256]{1,0:T(8,128)S(1)} %collective-permute-done.2.rest_1_, f32[160,256]{1,0:T(8,128)S(1)} %collective-permute-done.3.rest_2_, ...), custom_call_target="tpu_custom_call" | custom-call | flops 100663296 | tf_op jit(solution)/shard_map/top/pallas_call | solution.py:369
  36.1 2.8 %collective-permute-start.7 = (f32[64,256]{1,0:T(8,128)S(1)}, f32[64,256]{1,0:T(8,128)S(1)}, u32[]{:S(2)}, u32[]{:S(2)}) collective-permute-start(f32[64,256]{1,0:T(8,128)S(1)} %top.1), channel_id=1, source_target_pairs={{0,8},{1,9},{2,10},{3,11},{4,12},{5,13},{6,14},{7,15},{8,0},{9,1},... | collective-permute-start | bytes 196616 | tf_op jit(solution)/shard_map/ppermute | solution.py:472
  38.9 1.0 %later.3.later_ref = f32[320,256]{1,0:T(8,128)S(1)} custom-call(f32[320,256]{1,0:T(8,128)S(1)} %later.2.later_ref, f32[160,256]{1,0:T(8,128)S(1)} %get-tuple-element.24.rest_0_, f32[160,256]{1,0:T(8,128)S(1)} %collective-permute-done.2.rest_1_, f32[160,256]{1,0:T(8,128)S(1)} %collective-permute-done.3.rest_2_, ...), custom_call_target="tpu_custom_call" | custom-call | flops 503316480 | tf_op jit(solution)/shard_map/later/pallas_call | solution.py:369
  39.9 2.2 %shift.1 = (bf16[16,256,256]{2,1,0:T(8,128)(2,1)S(1)}, bf16[16,256,256]{2,1,0:T(8,128)(2,1)S(1)}, f32[16,64,256]{2,1,0:T(8,128)S(1)}) custom-call(f32[320,256]{1,0:T(8,128)S(1)} %later.3.later_ref, bf16[16,256,256]{2,1,0:T(8,128)(2,1)S(1)} %get-tuple-element.25.zh_ref, bf16[16,256,256]{2,1,0:T(8,128)(2,1)S(1)} %get-tuple-element.26.zl_ref, ...), custom_call_target="tpu_custom_call" | custom-call | flops 2013265920 | tf_op jit(solution)/shard_map/shift/pallas_call | solution.py:369
  42.2 0.6 collective-permute-done.7.got_ref
  42.7 5.6 %sweep.1 = (bf16[16,8,64,256]{3,2,1,0:T(8,128)(2,1)}, f32[128,256]{1,0:T(8,128)S(1)}, f32[128,256]{1,0:T(8,128)S(1)}) custom-call(f32[64,256]{1,0:T(8,128)S(1)} %bitcast.7, f32[64,256]{1,0:T(8,128)S(1)} %collective-permute-done.7.got_ref, f32[320,256]{1,0:T(8,128)S(1)} %later.3.later_ref, bf16[16,256,256]{2,1,0:T(8,128)(2,1)S(1)} %get-tuple-element.28.zh_ref, ...), custom_call_target="tpu_custom_call" | custom-call | flops 4294967296 | tf_op jit(solution)/shard_map/sweep/pallas_call | solution.py:369
  48.4 1.3 %collective-permute-done.8.got_ref = f32[128,256]{1,0:T(8,128)S(1)} collective-permute-done((f32[128,256]{1,0:T(8,128)S(1)}, f32[128,256]{1,0:T(8,128)S(1)}, u32[]{:S(2)}, u32[]{:S(2)}) %collective-permute-start.8) | collective-permute-done | bytes 131104 | tf_op jit(solution)/shard_map/ppermute | solution.py:472
  49.8 1.7 %collective-permute-start.9 = (f32[64,256]{1,0:T(8,128)S(1)}, f32[64,256]{1,0:T(8,128)S(1)}, u32[]{:S(2)}, u32[]{:S(2)}) collective-permute-start(f32[64,256]{1,0:T(8,128)S(1)} %get-tuple-element.39), channel_id=1, source_target_pairs={{0,2},{1,3},{2,0},{3,1},{4,6},{5,7},{6,4},{7,5},{8,10},{9,11},{10,... | collective-permute-start | bytes 196616 | tf_op jit(solution)/shard_map/ppermute | solution.py:472
  51.5 2.6 %collective-permute-done.9 = f32[64,256]{1,0:T(8,128)S(1)} collective-permute-done((f32[64,256]{1,0:T(8,128)S(1)}, f32[64,256]{1,0:T(8,128)S(1)}, u32[]{:S(2)}, u32[]{:S(2)}) %collective-permute-start.9) | collective-permute-done | bytes 65568 | tf_op jit(solution)/shard_map/ppermute | solution.py:472
  54.2 3.6 %collective-permute-start.12 = (f32[64,256]{1,0:T(8,128)S(1)}, f32[64,256]{1,0:T(8,128)S(1)}, u32[]{:S(2)}, u32[]{:S(2)}) collective-permute-start(f32[64,256]{1,0:T(8,128)S(1)} %add.12), channel_id=1, source_target_pairs={{0,12},{1,13},{2,14},{3,15},{4,8},{5,9},{6,10},{7,11},{8,4},{9,5},... | collective-permute-start | bytes 196616 | tf_op jit(solution)/shard_map/ppermute | solution.py:472
  57.7 0.9 %collective-permute-start.10 = (f32[64,256]{1,0:T(8,128)S(1)}, f32[64,256]{1,0:T(8,128)S(1)}, u32[]{:S(2)}, u32[]{:S(2)}) collective-permute-start(f32[64,256]{1,0:T(8,128)S(1)} %add.12), channel_id=1, source_target_pairs={{0,4},{1,5},{2,6},{3,7},{4,0},{5,1},{6,2},{7,3},{8,12},{9,13},{10,... | collective-permute-start | bytes 196616 | tf_op jit(solution)/shard_map/ppermute | solution.py:472
  58.6 1.8 %collective-permute-done.12 = f32[64,256]{1,0:T(8,128)S(1)} collective-permute-done((f32[64,256]{1,0:T(8,128)S(1)}, f32[64,256]{1,0:T(8,128)S(1)}, u32[]{:S(2)}, u32[]{:S(2)}) %collective-permute-start.12) | collective-permute-done | bytes 65568 | tf_op jit(solution)/shard_map/ppermute | solution.py:472
  60.4 2.5 %collective-permute-done.11 = f32[64,256]{1,0:T(8,128)S(1)} collective-permute-done((f32[64,256]{1,0:T(8,128)S(1)}, f32[64,256]{1,0:T(8,128)S(1)}, u32[]{:S(2)}, u32[]{:S(2)}) %collective-permute-start.11) | collective-permute-done | bytes 65568 | tf_op jit(solution)/shard_map/ppermute | solution.py:472
  63.0 0.3 collective-permute-done.10
  63.2 1.7 %collective-permute-start.13 = (f32[64,256]{1,0:T(8,128)S(1)}, f32[64,256]{1,0:T(8,128)S(1)}, u32[]{:S(2)}, u32[]{:S(2)}) collective-permute-start(f32[64,256]{1,0:T(8,128)S(1)} %add_add_fusion.own_ref), channel_id=1, source_target_pairs={{0,2},{1,3},{2,0},{3,1},{4,6},{5,7},{6,4},{7,5},{8,10},{9,11},{10,... | collective-permute-start | bytes 196616 | tf_op jit(solution)/shard_map/ppermute | solution.py:472
  65.0 2.6 %collective-permute-done.13.far_ref = f32[64,256]{1,0:T(8,128)S(1)} collective-permute-done((f32[64,256]{1,0:T(8,128)S(1)}, f32[64,256]{1,0:T(8,128)S(1)}, u32[]{:S(2)}, u32[]{:S(2)}) %collective-permute-start.13) | collective-permute-done | bytes 65568 | tf_op jit(solution)/shard_map/ppermute | solution.py:472
  67.6 1.2 %collective-permute-done.15.both_ref = f32[64,256]{1,0:T(8,128)S(1)} collective-permute-done((f32[64,256]{1,0:T(8,128)S(1)}, f32[64,256]{1,0:T(8,128)S(1)}, u32[]{:S(2)}, u32[]{:S(2)}) %collective-permute-start.15) | collective-permute-done | bytes 65568 | tf_op jit(solution)/shard_map/ppermute | solution.py:472
  68.8 0.7 %join.1 = f32[256,256]{1,0:T(8,128)} custom-call(f32[64,256]{1,0:T(8,128)S(1)} %add_add_fusion.own_ref, f32[64,256]{1,0:T(8,128)S(1)} %collective-permute-done.13.far_ref, f32[64,256]{1,0:T(8,128)S(1)} %collective-permute-done.14.core_ref, f32[64,256]{1,0:T(8,128)S(1)} %collective-permute-done.15.both_ref), custom_call_target="tpu_custom_call" | custom-call | tf_op jit(solution)/shard_map/join/pallas_call | solution.py:369
  (14 shorter events, 0.2 us)
Async XLA Ops:
  19.6 1.8 %collective-permute-start = (f32[320,256]{1,0:T(8,128)S(1)}, f32[320,256]{1,0:T(8,128)S(1)}, u32[]{:S(2)}, u32[]{:S(2)}) collective-permute-start(f32[320,256]{1,0:T(8,128)S(1)} %get-tuple-element.22.own_ref), channel_id=1, source_target_pairs={{0,1},{1,0},{2,3},{3,2},{4,5},{5,4},{6,7},{7,6},{8,9},{9,8},{10,11... | collective-permute-start | bytes 983048 | tf_op jit(solution)/shard_map/ppermute | solution.py:472
  21.7 7.4 %collective-permute-start.1 = (f32[160,256]{1,0:T(8,128)S(1)}, f32[160,256]{1,0:T(8,128)S(1)}, u32[]{:S(2)}, u32[]{:S(2)}) collective-permute-start(f32[160,256]{1,0:T(8,128)S(1)} %pair.1), channel_id=1, source_target_pairs={{0,2},{1,3},{2,0},{3,1},{4,6},{5,7},{6,4},{7,5},{8,10},{9,11},{10,... | collective-permute-start | bytes 491528 | tf_op jit(solution)/shard_map/ppermute | solution.py:472
  24.6 8.4 %collective-permute-start.3 = (f32[160,256]{1,0:T(8,128)S(1)}, f32[160,256]{1,0:T(8,128)S(1)}, u32[]{:S(2)}, u32[]{:S(2)}) collective-permute-start(f32[160,256]{1,0:T(8,128)S(1)} %pair.1), channel_id=1, source_target_pairs={{0,4},{1,5},{2,6},{3,7},{4,0},{5,1},{6,2},{7,3},{8,12},{9,13},{10,... | collective-permute-start | bytes 491528 | tf_op jit(solution)/shard_map/ppermute | solution.py:472
  26.2 7.7 %collective-permute-start.5 = (f32[160,256]{1,0:T(8,128)S(1)}, f32[160,256]{1,0:T(8,128)S(1)}, u32[]{:S(2)}, u32[]{:S(2)}) collective-permute-start(f32[160,256]{1,0:T(8,128)S(1)} %pair.1), channel_id=1, source_target_pairs={{0,6},{1,7},{2,4},{3,5},{4,2},{5,3},{6,0},{7,1},{8,14},{9,15},{10,... | collective-permute-start | bytes 491528 | tf_op jit(solution)/shard_map/ppermute | solution.py:472
  29.1 6.2 %copy-start = (f32[256,64]{0,1:T(8,128)S(1)}, f32[256,64]{0,1:T(8,128)}, u32[]{:S(2)}) copy-start(f32[256,64]{0,1:T(8,128)} %param.9) | copy-start | bytes 196612
  32.9 1.5 %collective-permute-start.2 = (f32[160,256]{1,0:T(8,128)S(1)}, f32[160,256]{1,0:T(8,128)S(1)}, u32[]{:S(2)}, u32[]{:S(2)}) collective-permute-start(f32[160,256]{1,0:T(8,128)S(1)} %get-tuple-element.24.rest_0_), channel_id=1, source_target_pairs={{0,1},{1,0},{2,3},{3,2},{4,5},{5,4},{6,7},{7,6},{8,9},{9,8},{10,11... | collective-permute-start | bytes 491528 | tf_op jit(solution)/shard_map/ppermute | solution.py:472
  33.0 1.6 %collective-permute-start.4 = (f32[160,256]{1,0:T(8,128)S(1)}, f32[160,256]{1,0:T(8,128)S(1)}, u32[]{:S(2)}, u32[]{:S(2)}) collective-permute-start(f32[160,256]{1,0:T(8,128)S(1)} %collective-permute-done.3.rest_2_), channel_id=1, source_target_pairs={{0,1},{1,0},{2,3},{3,2},{4,5},{5,4},{6,7},{7,6},{8,9},{9,8},{10,11... | collective-permute-start | bytes 491528 | tf_op jit(solution)/shard_map/ppermute | solution.py:472
  33.9 1.4 %collective-permute-start.6 = (f32[160,256]{1,0:T(8,128)S(1)}, f32[160,256]{1,0:T(8,128)S(1)}, u32[]{:S(2)}, u32[]{:S(2)}) collective-permute-start(f32[160,256]{1,0:T(8,128)S(1)} %collective-permute-done.5.rest_4_), channel_id=1, source_target_pairs={{0,1},{1,0},{2,3},{3,2},{4,5},{5,4},{6,7},{7,6},{8,9},{9,8},{10,11... | collective-permute-start | bytes 491528 | tf_op jit(solution)/shard_map/ppermute | solution.py:472
  36.1 6.6 %collective-permute-start.7 = (f32[64,256]{1,0:T(8,128)S(1)}, f32[64,256]{1,0:T(8,128)S(1)}, u32[]{:S(2)}, u32[]{:S(2)}) collective-permute-start(f32[64,256]{1,0:T(8,128)S(1)} %top.1), channel_id=1, source_target_pairs={{0,8},{1,9},{2,10},{3,11},{4,12},{5,13},{6,14},{7,15},{8,0},{9,1},... | collective-permute-start | bytes 196616 | tf_op jit(solution)/shard_map/ppermute | solution.py:472
  48.4 1.4 %collective-permute-start.8 = (f32[128,256]{1,0:T(8,128)S(1)}, f32[128,256]{1,0:T(8,128)S(1)}, u32[]{:S(2)}, u32[]{:S(2)}) collective-permute-start(f32[128,256]{1,0:T(8,128)S(1)} %get-tuple-element.37), channel_id=1, source_target_pairs={{0,1},{1,0},{2,3},{3,2},{4,5},{5,4},{6,7},{7,6},{8,9},{9,8},{10,11... | collective-permute-start | bytes 393224 | tf_op jit(solution)/shard_map/ppermute | solution.py:472
  49.8 4.3 %collective-permute-start.9 = (f32[64,256]{1,0:T(8,128)S(1)}, f32[64,256]{1,0:T(8,128)S(1)}, u32[]{:S(2)}, u32[]{:S(2)}) collective-permute-start(f32[64,256]{1,0:T(8,128)S(1)} %get-tuple-element.39), channel_id=1, source_target_pairs={{0,2},{1,3},{2,0},{3,1},{4,6},{5,7},{6,4},{7,5},{8,10},{9,11},{10,... | collective-permute-start | bytes 196616 | tf_op jit(solution)/shard_map/ppermute | solution.py:472
  54.2 6.3 %collective-permute-start.12 = (f32[64,256]{1,0:T(8,128)S(1)}, f32[64,256]{1,0:T(8,128)S(1)}, u32[]{:S(2)}, u32[]{:S(2)}) collective-permute-start(f32[64,256]{1,0:T(8,128)S(1)} %add.12), channel_id=1, source_target_pairs={{0,12},{1,13},{2,14},{3,15},{4,8},{5,9},{6,10},{7,11},{8,4},{9,5},... | collective-permute-start | bytes 196616 | tf_op jit(solution)/shard_map/ppermute | solution.py:472
  57.7 5.2 %collective-permute-start.11 = (f32[64,256]{1,0:T(8,128)S(1)}, f32[64,256]{1,0:T(8,128)S(1)}, u32[]{:S(2)}, u32[]{:S(2)}) collective-permute-start(f32[64,256]{1,0:T(8,128)S(1)} %add.12), channel_id=1, source_target_pairs={{0,8},{1,9},{2,10},{3,11},{4,12},{5,13},{6,14},{7,15},{8,0},{9,1},... | collective-permute-start | bytes 196616 | tf_op jit(solution)/shard_map/ppermute | solution.py:472
  57.7 5.5 %collective-permute-start.10 = (f32[64,256]{1,0:T(8,128)S(1)}, f32[64,256]{1,0:T(8,128)S(1)}, u32[]{:S(2)}, u32[]{:S(2)}) collective-permute-start(f32[64,256]{1,0:T(8,128)S(1)} %add.12), channel_id=1, source_target_pairs={{0,4},{1,5},{2,6},{3,7},{4,0},{5,1},{6,2},{7,3},{8,12},{9,13},{10,... | collective-permute-start | bytes 196616 | tf_op jit(solution)/shard_map/ppermute | solution.py:472
  63.2 4.3 %collective-permute-start.13 = (f32[64,256]{1,0:T(8,128)S(1)}, f32[64,256]{1,0:T(8,128)S(1)}, u32[]{:S(2)}, u32[]{:S(2)}) collective-permute-start(f32[64,256]{1,0:T(8,128)S(1)} %add_add_fusion.own_ref), channel_id=1, source_target_pairs={{0,2},{1,3},{2,0},{3,1},{4,6},{5,7},{6,4},{7,5},{8,10},{9,11},{10,... | collective-permute-start | bytes 196616 | tf_op jit(solution)/shard_map/ppermute | solution.py:472
  65.0 2.6 %collective-permute-start.14 = (f32[64,256]{1,0:T(8,128)S(1)}, f32[64,256]{1,0:T(8,128)S(1)}, u32[]{:S(2)}, u32[]{:S(2)}) collective-permute-start(f32[64,256]{1,0:T(8,128)S(1)} %add_add_fusion.own_ref), channel_id=1, source_target_pairs={{0,1},{1,0},{2,3},{3,2},{4,5},{5,4},{6,7},{7,6},{8,9},{9,8},{10,11... | collective-permute-start | bytes 196616 | tf_op jit(solution)/shard_map/ppermute | solution.py:472
  67.6 1.3 %collective-permute-start.15 = (f32[64,256]{1,0:T(8,128)S(1)}, f32[64,256]{1,0:T(8,128)S(1)}, u32[]{:S(2)}, u32[]{:S(2)}) collective-permute-start(f32[64,256]{1,0:T(8,128)S(1)} %collective-permute-done.13.far_ref), channel_id=1, source_target_pairs={{0,1},{1,0},{2,3},{3,2},{4,5},{5,4},{6,7},{7,6},{8,9},{9,8},{10,11... | collective-permute-start | bytes 196616 | tf_op jit(solution)/shard_map/ppermute | solution.py:472
